TPU v7x, 32 devices: a whole 2x2x4 slice. The times are simulated.
32 devices in a mesh: seg: 2 (over core), clip: 16 (over z, y, x).
Axes of the slice: x: 2, y: 2, z: 4, core: 2. Of those that a mesh axis runs over, the one named last changes fastest.
Arguments:
- inputs: bfloat16 [64, 16, 49, 2048], P('clip', 'seg'), may hold values from -6 to 6
- clip_counts: int32 [64], P('clip'), may hold values from 8 to 16, as said below
- labels: int32 [64], P('clip'), may hold values from 0 to 173
- master: float32 [9543872], P(('seg', 'clip'))
- first_moment: float32 [9543872], P(('seg', 'clip')), may hold values from -4.7683716e-07 to 4.7683716e-07
- second_moment: float32 [9543872], P(('seg', 'clip')), may hold values from 1.0488405e-16 to 4.195362e-16
Outputs:
- new_master: float32 [9543872], P(('seg', 'clip'))
- new_first: float32 [9543872], P(('seg', 'clip'))
- new_second: float32 [9543872], P(('seg', 'clip'))
- master_low: bfloat16 [9543872], P(('seg', 'clip'))
- input_grad: float32 [64, 16, 49, 2048], P('clip', 'seg')
- grad_norm: float32 [1], replicated
- bias_grad: float32 [174], replicated
Inputs may be any that keep to these rules, and one draw needn't show every extreme that they name: `clip_counts`: each clip has 8 or 16 true segments, which fill its first slots; both counts occur.
All inputs are finite; a program needn't handle non-finite values.
Results may differ from a plain program's by a relative error of at most 0.018.
Values may be sent and summed in bfloat16 or wider, within the bound.
A program may use at most 320 MiB of HBM per device.

v0:
```python
import math

import jax
import jax.numpy as jnp
from jax import lax
from jax.sharding import PartitionSpec as P

D = 2048
MID = 512
GATE = 128
CLASSES = 174
GRID = 7
HW = 49
STEP = 7


NORM_EPS = 1e-05
CLIP_LIMIT = 0.001
LEARN_RATE = 0.04
WEIGHT_DECAY = 0.05
BETA_ONE = 0.9
BETA_TWO = 0.999
ADAM_EPS = 1e-08


def matmul(left, right):
    return jnp.dot(left, right, preferred_element_type=jnp.float32)


def silu_slope(values):
    sig_val = jax.nn.sigmoid(values)
    return sig_val * (1.0 + values * (1.0 - sig_val))


def layout():
    block_layout = [
        (D, MID),
        (9, MID, MID),
        (MID, D),
        (MID, GATE),
        (GATE, MID),
        (2 * MID + D,),
        (2 * MID + D,),
    ]
    return block_layout + block_layout + [(D, CLASSES), (CLASSES,)]


def piece_at(flat, devices, position):
    shapes = layout()
    offset = 0
    for index_p in range(position):
        offset = offset + (math.prod(shapes[index_p]) + devices - 1) // devices
    extent = shapes[position]
    amount = math.prod(extent)
    piece_width = (amount + devices - 1) // devices
    shard_rows = flat.reshape(devices, -1)
    return shard_rows[:, offset : offset + piece_width].reshape(-1)[:amount].reshape(extent)


def carve(flat, devices):
    return [piece_at(flat, devices, position) for position in range(len(layout()))]


def pack(grads, devices):
    columns = []
    for values in grads:
        amount = values.shape[0]
        piece_width = (amount + devices - 1) // devices
        padded = jnp.pad(values, (0, devices * piece_width - amount))
        columns.append(padded.reshape(devices, piece_width))
    return jnp.concatenate(columns, axis=1).reshape(-1)


def grid_mean(values):
    leading = values.shape[:-2]
    channels = values.shape[-1]
    grids = values.reshape(leading + (GRID, GRID, channels))
    widths = [(0, 0)] * len(leading) + [(1, 1), (1, 1), (0, 0)]
    padded = jnp.pad(grids, widths)
    total = jnp.zeros_like(grids)
    for index_k in range(9):
        row_start = index_k // 3
        col_start = index_k % 3
        total = total + padded[..., row_start : row_start + GRID, col_start : col_start + GRID, :]
    return (total / 9.0).reshape(values.shape)


def grid_patches(values):
    channels = values.shape[-1]
    grids = values.reshape(-1, GRID, GRID, channels)
    padded = jnp.pad(grids, ((0, 0), (1, 1), (1, 1), (0, 0)))
    windows = []
    for index_k in range(9):
        row_start = index_k // 3
        col_start = index_k % 3
        windows.append(padded[:, row_start : row_start + GRID, col_start : col_start + GRID, :])
    return jnp.concatenate(windows, axis=-1).reshape(-1, 9 * channels)


def grid_fold(grad_patch, channels):
    pieces = grad_patch.reshape(-1, GRID, GRID, 9, channels)
    padded = jnp.pad(pieces, ((0, 0), (1, 1), (1, 1), (0, 0), (0, 0)))
    total = jnp.zeros((pieces.shape[0], GRID, GRID, channels), jnp.float32)
    for index_k in range(9):
        row_start = 2 - index_k // 3
        col_start = 2 - index_k % 3
        total = (
            total
            + padded[:, row_start : row_start + GRID, col_start : col_start + GRID, index_k, :]
        )
    return total.reshape(-1, channels)


def norm_forward(values, rows_mask, gain, shift):
    sums, squares, live_rows = lax.psum(
        (
            jnp.sum(values * rows_mask, axis=0),
            jnp.sum(values * values * rows_mask, axis=0),
            jnp.sum(rows_mask),
        ),
        ("seg", "clip"),
    )
    mean_val = sums / live_rows
    variance = squares / live_rows - mean_val * mean_val
    inv_std = lax.rsqrt(variance + NORM_EPS)
    normed = (values - mean_val) * inv_std
    return (normed * gain + shift, normed, inv_std, live_rows)


def norm_backward(grad_out, normed, inv_std, live_rows, rows_mask, gain):
    part_gain = jnp.sum(grad_out * normed, axis=0)
    part_shift = jnp.sum(grad_out, axis=0)
    total_gain, total_shift = lax.psum((part_gain, part_shift), ("seg", "clip"))
    grad_in = (
        gain * inv_std * (grad_out - rows_mask * (total_shift + normed * total_gain) / live_rows)
    )
    return (grad_in, part_gain, part_shift)


def gate_forward(reduced, masks):
    present, following, present_all, following_all, rows_mask = masks
    across = lax.all_to_all(reduced, "seg", split_axis=3, concat_axis=1, tiled=True)
    later = jnp.concatenate([across[:, 1:], jnp.zeros_like(across[:, :1])], axis=1)
    change = following_all[:, :, None, None] * (
        later.astype(jnp.float32) - across.astype(jnp.float32)
    )
    mixed_part = (change + grid_mean(change)).astype(jnp.bfloat16)
    mixed = lax.all_to_all(mixed_part, "seg", split_axis=1, concat_axis=3, tiled=True)
    return mixed


def gate_backward(d_mixed, masks):
    present, following, present_all, following_all, rows_mask = masks
    d_across = lax.all_to_all(d_mixed, "seg", split_axis=3, concat_axis=1, tiled=True).astype(
        jnp.float32
    )
    d_spread = d_across + grid_mean(d_across)
    earlier = jnp.concatenate([jnp.zeros_like(d_spread[:, :1]), d_spread[:, :-1]], axis=1)
    d_part = present_all[:, :, None, None] * earlier - following_all[:, :, None, None] * d_spread
    d_reduced = lax.all_to_all(
        d_part.astype(jnp.bfloat16), "seg", split_axis=1, concat_axis=3, tiled=True
    )
    return d_reduced


def block_forward(x_low, x_float, weights, masks):
    w_in, w_mid, w_out, w_red, w_exp, gain_low, shift_low = weights
    gains = gain_low.astype(jnp.float32)
    shifts = shift_low.astype(jnp.float32)
    rows_mask = masks[4]
    clip_local = masks[0].shape[0]
    slot_local = masks[0].shape[1]
    h_one = matmul(x_low, w_in)
    y_one, normed_one, inv_one, live_rows = norm_forward(
        h_one, rows_mask, gains[:MID], shifts[:MID]
    )
    a_one = jax.nn.silu(y_one)
    a_one_low = a_one.astype(jnp.bfloat16)
    reduced = (
        matmul(a_one_low, w_red).astype(jnp.bfloat16).reshape(clip_local, slot_local, HW, GATE)
    )
    mixed = gate_forward(reduced, masks)
    mixed_flat = mixed.reshape(-1, GATE)
    gate = jax.nn.sigmoid(matmul(mixed_flat, w_exp))
    gated = a_one * (1.0 + gate)
    patches = grid_patches(gated.astype(jnp.bfloat16))
    h_two = matmul(patches, w_mid.reshape(9 * MID, MID))
    y_two, normed_two, inv_two, unused_two = norm_forward(
        h_two, rows_mask, gains[MID : 2 * MID], shifts[MID : 2 * MID]
    )
    a_two_low = jax.nn.silu(y_two).astype(jnp.bfloat16)
    h_three = matmul(a_two_low, w_out)
    y_three, normed_three, inv_three, unused_three = norm_forward(
        h_three, rows_mask, gains[2 * MID :], shifts[2 * MID :]
    )
    pre = y_three + x_float
    kept = (
        x_low,
        a_one,
        a_one_low,
        y_one,
        normed_one,
        inv_one,
        gate,
        mixed_flat,
        patches,
        y_two,
        normed_two,
        inv_two,
        a_two_low,
        normed_three,
        inv_three,
        pre,
        live_rows,
    )
    return (jax.nn.silu(pre), kept)


def block_backward(d_out, kept, weights, masks):
    w_in, w_mid, w_out, w_red, w_exp, gain_low, shift_low = weights
    gains = gain_low.astype(jnp.float32)
    (
        x_low,
        a_one,
        a_one_low,
        y_one,
        normed_one,
        inv_one,
        gate,
        mixed_flat,
        patches,
        y_two,
        normed_two,
        inv_two,
        a_two_low,
        normed_three,
        inv_three,
        pre,
        live_rows,
    ) = kept
    rows_mask = masks[4]
    clip_local = masks[0].shape[0]
    slot_local = masks[0].shape[1]
    mid_matrix = w_mid.reshape(9 * MID, MID)
    d_pre = d_out * silu_slope(pre)
    d_h_three, gain_three, shift_three = norm_backward(
        d_pre, normed_three, inv_three, live_rows, rows_mask, gains[2 * MID :]
    )
    d_h_three_low = d_h_three.astype(jnp.bfloat16)
    g_out = matmul(a_two_low.T, d_h_three_low)
    d_a_two = matmul(d_h_three_low, w_out.T)
    d_y_two = d_a_two * silu_slope(y_two)
    d_h_two, gain_two, shift_two = norm_backward(
        d_y_two, normed_two, inv_two, live_rows, rows_mask, gains[MID : 2 * MID]
    )
    d_h_two_low = d_h_two.astype(jnp.bfloat16)
    g_mid = matmul(patches.T, d_h_two_low)
    d_gated = grid_fold(matmul(d_h_two_low, mid_matrix.T), MID)
    d_excite = (d_gated * a_one * gate * (1.0 - gate)).astype(jnp.bfloat16)
    g_exp = matmul(mixed_flat.T, d_excite)
    d_mixed = (
        matmul(d_excite, w_exp.T).astype(jnp.bfloat16).reshape(clip_local, slot_local, HW, GATE)
    )
    d_reduced_flat = gate_backward(d_mixed, masks).reshape(-1, GATE)
    g_red = matmul(a_one_low.T, d_reduced_flat)
    d_a_one = d_gated * (1.0 + gate) + matmul(d_reduced_flat, w_red.T)
    d_y_one = d_a_one * silu_slope(y_one)
    d_h_one, gain_one, shift_one = norm_backward(
        d_y_one, normed_one, inv_one, live_rows, rows_mask, gains[:MID]
    )
    d_h_one_low = d_h_one.astype(jnp.bfloat16)
    g_in = matmul(x_low.T, d_h_one_low)
    d_x = d_pre + matmul(d_h_one_low, w_in.T)
    grads = [
        g_in.reshape(-1),
        g_mid.reshape(-1),
        g_out.reshape(-1),
        g_red.reshape(-1),
        g_exp.reshape(-1),
        jnp.concatenate([gain_one, gain_two, gain_three]),
        jnp.concatenate([shift_one, shift_two, shift_three]),
    ]
    return (d_x, grads)


def on_device(inputs, clip_counts, labels, master, first_moment, second_moment):
    seg_count = lax.axis_size("seg")
    devices = lax.axis_size("seg") * lax.axis_size("clip")
    whole = lax.all_gather(master.astype(jnp.bfloat16), ("seg", "clip"), axis=0, tiled=True)
    pieces = carve(whole, devices)
    first_weights = pieces[0:7]
    second_weights = pieces[7:14]
    w_cls = pieces[14]
    b_cls = pieces[15].astype(jnp.float32)
    clip_local = inputs.shape[0]
    slot_local = inputs.shape[1]
    slot_ids = lax.axis_index("seg") * slot_local + jnp.arange(slot_local, dtype=jnp.int32)
    present = (slot_ids[None, :] < clip_counts[:, None]).astype(jnp.float32)
    following = (slot_ids[None, :] + 1 < clip_counts[:, None]).astype(jnp.float32)
    rows_mask = jnp.broadcast_to(present[:, :, None], (clip_local, slot_local, HW)).reshape(-1, 1)
    all_ids = jnp.arange(slot_local * seg_count, dtype=jnp.int32)
    present_all = (all_ids[None, :] < clip_counts[:, None]).astype(jnp.float32)
    following_all = (all_ids[None, :] + 1 < clip_counts[:, None]).astype(jnp.float32)
    masks = (present, following, present_all, following_all, rows_mask)
    flat_in = inputs.reshape(-1, D)
    middle, kept_first = block_forward(flat_in, flat_in.astype(jnp.float32), first_weights, masks)
    final, kept_second = block_forward(middle.astype(jnp.bfloat16), middle, second_weights, masks)
    block = final.reshape(clip_local, slot_local, HW, D)
    partial_value = jnp.sum(block * present[:, :, None, None], axis=(1, 2))
    pooled_sum = lax.psum(partial_value.astype(jnp.bfloat16), "seg").astype(jnp.float32)
    counts_float = clip_counts.astype(jnp.float32)
    pooled = pooled_sum / (HW * counts_float)[:, None]
    pooled_low = pooled.astype(jnp.bfloat16)
    logits = matmul(pooled_low, w_cls) + b_cls
    clips_total = clip_local * lax.axis_size("clip")
    onehot = (labels[:, None] == jnp.arange(CLASSES, dtype=jnp.int32)[None, :]).astype(jnp.float32)
    d_logits = (jax.nn.softmax(logits, axis=1) - onehot) / clips_total
    d_lin = d_logits.astype(jnp.bfloat16)
    g_cls = matmul(pooled_low.T, d_lin) / seg_count
    g_bias = jnp.sum(d_logits, axis=0) / seg_count
    d_pooled = matmul(d_lin, w_cls.T)
    scaled = d_pooled / (HW * counts_float)[:, None]
    d_block = jnp.broadcast_to(
        present[:, :, None, None] * scaled[:, None, None, :], (clip_local, slot_local, HW, D)
    ).reshape(-1, D)
    d_middle, grads_second = block_backward(d_block, kept_second, second_weights, masks)
    input_grad, grads_first = block_backward(d_middle, kept_first, first_weights, masks)
    grad_local = pack(grads_first + grads_second + [g_cls.reshape(-1), g_bias], devices)
    shard = master.shape[0]
    total = lax.psum(grad_local, ("seg", "clip"))
    norm = jnp.sqrt(jnp.sum(total * total))
    grad_mine = lax.dynamic_slice_in_dim(total, lax.axis_index(("seg", "clip")) * shard, shard)
    bias_grad = piece_at(total, devices, 15)
    factor = jnp.minimum(1.0, CLIP_LIMIT / (norm + 1e-06))
    clipped = grad_mine * factor
    new_first = BETA_ONE * first_moment + (1.0 - BETA_ONE) * clipped
    new_second = BETA_TWO * second_moment + (1.0 - BETA_TWO) * clipped * clipped
    first_hat = new_first / (1.0 - BETA_ONE**STEP)
    second_hat = new_second / (1.0 - BETA_TWO**STEP)
    new_master = master - LEARN_RATE * (
        first_hat / (jnp.sqrt(second_hat) + ADAM_EPS) + WEIGHT_DECAY * master
    )
    return (
        new_master,
        new_first,
        new_second,
        new_master.astype(jnp.bfloat16),
        input_grad.reshape(inputs.shape),
        norm.reshape(1),
        bias_grad,
    )


def solution(mesh):
    return jax.shard_map(
        on_device,
        mesh=mesh,
        in_specs=(
            P("clip", "seg", None, None),
            P("clip"),
            P("clip"),
            P(("seg", "clip")),
            P(("seg", "clip")),
            P(("seg", "clip")),
        ),
        out_specs=(
            P(("seg", "clip")),
            P(("seg", "clip")),
            P(("seg", "clip")),
            P(("seg", "clip")),
            P("clip", "seg", None, None),
            P(),
            P(),
        ),
        check_vma=False,
    )
```

profile of v0, /device:TPU:0, one launch (start us, length us, event | category | flops | bytes accessed | tf_op | source)
XLA Modules:
  0.0 2390.2 jit_solution(11477730303679217946)
XLA Ops:
  8.6 6.6 broadcast.195
  15.2 10.2 dynamic-update-slice
  26.3 10.3 copy.131
  36.5 7.1 reshape.429
  45.5 289.5 %all-reduce.31.cloned.1.call-done = bf16[9543872]{0:T(1024)(128)(2,1)} async-done(((bf16[9543872]{0:T(1024)(128)(2,1)}), bf16[9543872]{0:T(1024)(128)(2,1)}) %all-reduce.31.cloned.1.call-update) | async-done | bytes 19087760
  335.0 43.2 %reshape.428 = bf16[32,298246]{1,0:T(8,128)(2,1)} reshape(bf16[9543872]{0:T(1024)(128)(2,1)} %all-reduce.31.cloned.1.call-done) | data formatting | bytes 38175488 | tf_op jit(solution)/shard_map/reshape | solution.py:56
  382.3 6.2 fusion.120
  388.5 8.8 fusion.118
  409.3 6.1 reshape.494
  443.2 6.4 multiply_reduce_fusion.9
  449.6 40.5 %all-reduce.25 = (f32[512]{0:T(512)S(1)}, f32[]{:T(128)}, f32[512]{0:T(512)S(1)}) all-reduce(f32[512]{0:T(512)S(1)} %get-tuple-element.64, f32[]{:T(128)} %broadcast_reduce_fusion, f32[512]{0:T(512)S(1)} %get-tuple-element.63), channel_id=1, replica_groups=mesh['seg'=2,'clip'=16] {'seg','clip'}, use_global_device_ids=true, to_apply=%region_1.0 | all-reduce | flops 1025 | bytes 8200 | tf_op jit(solution)/shard_map/psum | solution.py:115
  522.5 6.1 all_to_all.115
  544.5 11.1 pad_slice_fusion.24
  588.6 14.9 multiply_reduce_fusion.17
  603.5 39.4 %all-reduce.24 = (f32[512]{0:T(512)S(1)}, f32[512]{0:T(512)S(1)}) all-reduce(f32[512]{0:T(512)S(1)} %get-tuple-element.62, f32[512]{0:T(512)S(1)} %get-tuple-element.61), channel_id=1, replica_groups=mesh['seg'=2,'clip'=16] {'seg','clip'}, use_global_device_ids=true, to_apply=%region_7.8 | all-reduce | flops 1024 | bytes 8192 | tf_op jit(solution)/shard_map/psum | solution.py:115
  644.2 8.9 multiply_reduce_fusion.7
  653.1 41.5 %all-reduce.23 = (f32[2048]{0:T(1024)S(1)}, f32[2048]{0:T(1024)S(1)}) all-reduce(f32[2048]{0:T(1024)S(1)} %get-tuple-element.52, f32[2048]{0:T(1024)S(1)} %get-tuple-element.51), channel_id=1, replica_groups=mesh['seg'=2,'clip'=16] {'seg','clip'}, use_global_device_ids=true, to_apply=%region_13.14 | all-reduce | flops 4096 | bytes 32768 | tf_op jit(solution)/shard_map/psum | solution.py:115
  697.2 9.0 fusion.1
  710.8 39.1 %all-reduce.22 = (f32[512]{0:T(512)S(1)}, f32[512]{0:T(512)S(1)}) all-reduce(f32[512]{0:T(512)S(1)} %get-tuple-element.60, f32[512]{0:T(512)S(1)} %get-tuple-element.59), channel_id=1, replica_groups=mesh['seg'=2,'clip'=16] {'seg','clip'}, use_global_device_ids=true, to_apply=%region_17.18 | all-reduce | flops 1024 | bytes 8192 | tf_op jit(solution)/shard_map/psum | solution.py:115
  804.3 11.1 pad_slice_fusion.16
  848.4 14.8 multiply_reduce_fusion.14
  863.2 41.0 %all-reduce.21 = (f32[512]{0:T(512)S(1)}, f32[512]{0:T(512)S(1)}) all-reduce(f32[512]{0:T(512)S(1)} %get-tuple-element.58, f32[512]{0:T(512)S(1)} %get-tuple-element.57), channel_id=1, replica_groups=mesh['seg'=2,'clip'=16] {'seg','clip'}, use_global_device_ids=true, to_apply=%region_21.22 | all-reduce | flops 1024 | bytes 8192 | tf_op jit(solution)/shard_map/psum | solution.py:115
  904.9 8.9 multiply_reduce_fusion.4
  913.8 39.7 %all-reduce.20 = (f32[2048]{0:T(1024)S(1)}, f32[2048]{0:T(1024)S(1)}) all-reduce(f32[2048]{0:T(1024)S(1)} %get-tuple-element.50, f32[2048]{0:T(1024)S(1)} %get-tuple-element.49), channel_id=1, replica_groups=mesh['seg'=2,'clip'=16] {'seg','clip'}, use_global_device_ids=true, to_apply=%region_23.24 | all-reduce | flops 4096 | bytes 32768 | tf_op jit(solution)/shard_map/psum | solution.py:115
  954.8 15.4 fusion
  970.2 10.1 reshape.440
  980.4 7.2 multiply_reduce_fusion.1
  994.3 7.1 broadcast_in_dim.5
  1001.4 10.1 reshape.441
  1011.5 18.2 fusion.111
  1029.6 41.3 %all-reduce.19 = (f32[2048]{0:T(1024)S(1)}, f32[2048]{0:T(1024)S(1)}) all-reduce(f32[2048]{0:T(1024)S(1)} %get-tuple-element.56, f32[2048]{0:T(1024)S(1)} %get-tuple-element.55), channel_id=1, replica_groups=mesh['seg'=2,'clip'=16] {'seg','clip'}, use_global_device_ids=true, to_apply=%region_33.34 | all-reduce | flops 4096 | bytes 32768 | tf_op jit(solution)/shard_map/psum | solution.py:133
  1070.9 11.7 multiply_convert_fusion.1
  1082.7 6.8 fusion.115
  1095.4 39.3 %all-reduce.18 = (f32[512]{0:T(512)S(1)}, f32[512]{0:T(512)S(1)}) all-reduce(f32[512]{0:T(512)S(1)} %get-tuple-element.72, f32[512]{0:T(512)S(1)} %get-tuple-element.71), channel_id=1, replica_groups=mesh['seg'=2,'clip'=16] {'seg','clip'}, use_global_device_ids=true, to_apply=%region_37.38 | all-reduce | flops 1024 | bytes 8192 | tf_op jit(solution)/shard_map/psum | solution.py:133
  1139.2 14.2 fusion.126
  1153.9 15.6 fusion.4
  1169.5 9.9 fusion.19
  1212.3 6.1 all_to_all.119
  1234.0 41.0 %all-reduce.17 = (f32[512]{0:T(512)S(1)}, f32[512]{0:T(512)S(1)}) all-reduce(f32[512]{0:T(512)S(1)} %get-tuple-element.70, f32[512]{0:T(512)S(1)} %get-tuple-element.69), channel_id=1, replica_groups=mesh['seg'=2,'clip'=16] {'seg','clip'}, use_global_device_ids=true, to_apply=%region_41.42 | all-reduce | flops 1024 | bytes 8192 | tf_op jit(solution)/shard_map/psum | solution.py:133
  1279.7 10.5 fusion.36
  1290.2 19.6 fusion.110
  1309.8 39.5 %all-reduce.16 = (f32[2048]{0:T(1024)S(1)}, f32[2048]{0:T(1024)S(1)}) all-reduce(f32[2048]{0:T(1024)S(1)} %get-tuple-element.54, f32[2048]{0:T(1024)S(1)} %get-tuple-element.53), channel_id=1, replica_groups=mesh['seg'=2,'clip'=16] {'seg','clip'}, use_global_device_ids=true, to_apply=%region_45.46 | all-reduce | flops 4096 | bytes 32768 | tf_op jit(solution)/shard_map/psum | solution.py:133
  1349.3 11.7 multiply_convert_fusion
  1361.1 6.8 fusion.113
  1373.8 41.4 %all-reduce.15 = (f32[512]{0:T(512)S(1)}, f32[512]{0:T(512)S(1)}) all-reduce(f32[512]{0:T(512)S(1)} %get-tuple-element.68, f32[512]{0:T(512)S(1)} %get-tuple-element.67), channel_id=1, replica_groups=mesh['seg'=2,'clip'=16] {'seg','clip'}, use_global_device_ids=true, to_apply=%region_49.50 | all-reduce | flops 1024 | bytes 8192 | tf_op jit(solution)/shard_map/psum | solution.py:133
  1419.7 14.2 fusion.124
  1434.4 15.6 fusion.2
  1450.1 9.7 fusion.27
  1492.2 6.3 all_to_all.121
  1513.6 39.1 %all-reduce.14 = (f32[512]{0:T(512)}, f32[512]{0:T(512)}) all-reduce(f32[512]{0:T(512)S(1)} %get-tuple-element.66, f32[512]{0:T(512)S(1)} %get-tuple-element.65), channel_id=1, replica_groups=mesh['seg'=2,'clip'=16] {'seg','clip'}, use_global_device_ids=true, to_apply=%region_53.54 | all-reduce | flops 1024 | bytes 8192 | tf_op jit(solution)/shard_map/psum | solution.py:133
  1563.9 8.1 reshape.456
  1584.6 8.1 reshape.449
  1599.2 8.3 convolution_bitcast_fusion
  1622.4 7.9 constant_dynamic-update-slice_fusion.23
  1636.9 14.8 dynamic-update-slice.8
  1651.8 28.8 %dynamic-update-slice.9 = f32[32,298246]{1,0:T(8,128)} dynamic-update-slice(f32[32,298246]{1,0:T(8,128)} %dynamic-update-slice.8, f32[32,73728]{1,0:T(8,128)} %reshape.456, s32[]{} %constant.121, s32[]{} %constant.129) | dynamic-update-slice | bytes 18874372
  1680.6 15.0 dynamic-update-slice.10
  1704.6 50.1 %reshape.464 = f32[9543872]{0:T(1024)} reshape(f32[32,298246]{1,0:T(8,128)} %constant_dynamic-update-slice_fusion.18) | data formatting | bytes 76350976 | tf_op jit(solution)/shard_map/reshape | solution.py:71
  1756.1 10.2 convolution_add_fusion
  1766.3 10.4 reshape.465
  1776.7 17.9 copy.160
  1794.5 517.6 %all-reduce.29.cloned.1.call-done = f32[9543872]{0:T(1024)} async-done(((f32[9543872]{0:T(1024)}), f32[9543872]{0:T(1024)}) %all-reduce.29.cloned.1.call-update) | async-done | bytes 38175504 | tf_op jit(solution)/shard_map/psum | solution.py:330
  2312.1 14.0 multiply_reduce_fusion
  2326.8 48.9 %reshape.467 = f32[32,298246]{1,0:T(8,128)} reshape(f32[9543872]{0:T(1024)} %all-reduce.29.cloned.1.call-done) | data formatting | bytes 76350976 | tf_op jit(solution)/shard_map/reshape | solution.py:56
  (431 shorter events, 423.8 us)
Async XLA Ops:
  7.2 327.8 %all-reduce.31.cloned.1.call-start = ((), (), s32[]{:S(2)}) async-start(), calls=%async_computation.9 | async-start | bytes 38178816
  25.4 2286.7 %all-reduce.29.cloned.1.call-start = ((), (), s32[]{:S(2)}) async-start(), calls=%async_computation.8 | async-start | bytes 76357632 | tf_op jit(solution)/shard_map/psum | solution.py:330
  26.1 17.5 copy-start.63
  45.5 732.4 %copy-start.65 = (f32[4,16]{1,0:T(4,128)}, f32[4,16]{1,0:T(4,128)S(1)}, u32[]{:S(2)}) copy-start(f32[4,16]{1,0:T(4,128)S(1)} %get-tuple-element.160) | copy-start | bytes 772
  380.4 415.7 %copy-start.85 = (f32[512]{0:T(512)}, f32[512]{0:T(512)S(1)}, u32[]{:S(2)}) copy-start(f32[512]{0:T(512)S(1)} %get-tuple-element.148) | copy-start | bytes 6148
  381.0 155.3 %copy-start.83 = (f32[512]{0:T(512)}, f32[512]{0:T(512)S(1)}, u32[]{:S(2)}) copy-start(f32[512]{0:T(512)S(1)} %get-tuple-element.153) | copy-start | bytes 6148
  381.1 263.1 %copy-start.102 = (f32[512]{0:T(512)}, f32[512]{0:T(512)S(1)}, u32[]{:S(2)}) copy-start(f32[512]{0:T(512)S(1)} %get-tuple-element.152) | copy-start | bytes 6148
  381.1 315.5 %copy-start.72 = (f32[2048]{0:T(1024)}, f32[2048]{0:T(1024)S(1)}, u32[]{:S(2)}) copy-start(f32[2048]{0:T(1024)S(1)} %slice.432) | copy-start | bytes 24580
  415.4 8.6 slice-start
  423.9 112.4 %copy-start.46 = (bf16[128,512]{1,0:T(8,128)(2,1)}, bf16[128,512]{1,0:T(8,128)(2,1)S(1)}, u32[]{:S(2)}) copy-start(bf16[128,512]{1,0:T(8,128)(2,1)S(1)} %reshape_reshape.29) | copy-start | bytes 393220
  424.0 67.4 %copy-start.56 = (bf16[512,128]{1,0:T(8,128)(2,1)}, bf16[512,128]{1,0:T(8,128)(2,1)S(1)}, u32[]{:S(2)}) copy-start(bf16[512,128]{1,0:T(8,128)(2,1)S(1)} %reshape_reshape.28) | copy-start | bytes 393220
  449.6 86.7 %copy-start.2 = (f32[512,1568]{0,1:T(8,128)}, f32[512,1568]{0,1:T(8,128)S(1)}, u32[]{:S(2)}) copy-start(f32[512,1568]{0,1:T(8,128)S(1)} %get-tuple-element.161) | copy-start | bytes 9633796
  491.4 44.9 %copy-start.75 = (f32[512]{0:T(512)}, f32[512]{0:T(512)S(1)}, u32[]{:S(2)}) copy-start(f32[512]{0:T(512)S(1)} %get-tuple-element.103) | copy-start | bytes 6148
  491.4 45.0 %copy-start.77 = (f32[512]{0:T(512)}, f32[512]{0:T(512)S(1)}, u32[]{:S(2)}) copy-start(f32[512]{0:T(512)S(1)} %get-tuple-element.155) | copy-start | bytes 6148
  491.4 45.0 %copy-start.87 = (f32[512]{0:T(512)}, f32[512]{0:T(512)S(1)}, u32[]{:S(2)}) copy-start(f32[512]{0:T(512)S(1)} %get-tuple-element.154) | copy-start | bytes 6148
  588.6 14.9 copy-start.52
  603.5 49.6 %copy-start.29 = (f32[1568,512]{1,0:T(8,128)}, f32[1568,512]{1,0:T(8,128)S(1)}, u32[]{:S(2)}) copy-start(f32[1568,512]{1,0:T(8,128)S(1)} %get-tuple-element.164) | copy-start | bytes 9633796
  644.2 8.9 copy-start.90
  644.2 8.9 copy-start.92
  644.2 8.9 copy-start.105
  697.2 9.0 copy-start.34
  706.2 44.9 %copy-start.58 = (bf16[512,128]{1,0:T(8,128)(2,1)S(1)}, bf16[512,128]{1,0:T(8,128)(2,1)}, u32[]{:S(2)}) copy-start(bf16[512,128]{1,0:T(8,128)(2,1)} %reshape_reshape.32) | copy-start | bytes 393220
  710.8 85.3 %copy-start.5 = (f32[1568,512]{1,0:T(8,128)}, f32[1568,512]{1,0:T(8,128)S(1)}, u32[]{:S(2)}) copy-start(f32[1568,512]{1,0:T(8,128)S(1)} %get-tuple-element.166) | copy-start | bytes 9633796
  751.1 45.0 %copy-start.79 = (f32[512]{0:T(512)}, f32[512]{0:T(512)S(1)}, u32[]{:S(2)}) copy-start(f32[512]{0:T(512)S(1)} %get-tuple-element.109) | copy-start | bytes 6148
  751.1 45.0 %copy-start.81 = (f32[512]{0:T(512)}, f32[512]{0:T(512)S(1)}, u32[]{:S(2)}) copy-start(f32[512]{0:T(512)S(1)} %get-tuple-element.157) | copy-start | bytes 6148
  751.1 45.0 %copy-start.95 = (f32[512]{0:T(512)}, f32[512]{0:T(512)S(1)}, u32[]{:S(2)}) copy-start(f32[512]{0:T(512)S(1)} %get-tuple-element.149) | copy-start | bytes 6148
  780.2 15.9 copy-start.48
  848.4 14.9 copy-start.53
  848.4 56.5 %copy-start.104 = (f32[512]{0:T(512)S(1)}, f32[512]{0:T(512)}, u32[]{:S(2)}) copy-start(f32[512]{0:T(512)} %get-tuple-element.147) | copy-start | bytes 6148
  863.2 50.6 %copy-start.31 = (f32[1568,512]{1,0:T(8,128)}, f32[1568,512]{1,0:T(8,128)S(1)}, u32[]{:S(2)}) copy-start(f32[1568,512]{1,0:T(8,128)S(1)} %get-tuple-element.169) | copy-start | bytes 9633796
  904.9 49.9 %copy-start.62 = (f32[2048]{0:T(1024)S(1)}, f32[2048]{0:T(1024)}, u32[]{:S(2)}) copy-start(f32[2048]{0:T(1024)} %slice.446) | copy-start | bytes 24580
  970.2 10.1 copy-start.64
  980.3 10.6 copy-start.28
  980.3 10.6 copy-start.98
  980.3 10.6 copy-start.99
  980.4 11.2 copy-start.100
  1070.9 11.7 copy-start.32
  1070.9 11.7 copy-start.36
  1209.9 16.2 copy-start.7
  1209.9 16.2 copy-start.59
  1231.5 43.4 %copy-start.94 = (f32[512]{0:T(512)S(1)}, f32[512]{0:T(512)}, u32[]{:S(2)}) copy-start(f32[512]{0:T(512)} %get-tuple-element.108) | copy-start | bytes 6148
  1279.6 10.6 copy-start.35
  1279.6 10.6 copy-start.55
  1279.6 10.6 copy-start.61
  1279.6 10.6 copy-start.71
  1279.6 10.6 copy-start.73
  1290.2 59.1 %copy-start.69 = (f32[2048]{0:T(1024)S(1)}, f32[2048]{0:T(1024)}, u32[]{:S(2)}) copy-start(f32[2048]{0:T(1024)} %get-tuple-element.106) | copy-start | bytes 24580
  1349.3 11.8 copy-start.30
  1349.3 11.8 copy-start.33
  1349.3 11.8 copy-start.91
  1349.3 11.8 copy-start.93
  1349.3 11.8 copy-start.103
  1349.3 11.8 copy-start.106
  1367.9 47.3 %copy-start.89 = (f32[512]{0:T(512)S(1)}, f32[512]{0:T(512)}, u32[]{:S(2)}) copy-start(f32[512]{0:T(512)} %get-tuple-element.104) | copy-start | bytes 6148
  1489.8 16.4 copy-start.4
  1489.8 16.4 copy-start.57
  1511.7 41.0 %copy-start.97 = (f32[174]{0:T(256)S(1)}, f32[174]{0:T(256)}, u32[]{:S(2)}) copy-start(f32[174]{0:T(256)} %fusion.98) | copy-start | bytes 2092
  1563.9 8.1 copy-start.41
  1584.6 8.1 copy-start.42
  1680.6 15.0 copy-start.44
  1680.6 17.0 copy-start.43
  1680.6 22.2 copy-start.26
  2326.8 50.4 %copy-start.27 = (f32[298246]{0:T(1024)S(1)}, f32[298246]{0:T(1024)}, u32[]{:S(2)}) copy-start(f32[298246]{0:T(1024)} %param.9) | copy-start | bytes 3578956
  2326.8 50.4 %copy-start.40 = (f32[298246]{0:T(1024)S(1)}, f32[298246]{0:T(1024)}, u32[]{:S(2)}) copy-start(f32[298246]{0:T(1024)} %param.10) | copy-start | bytes 3578956
  (46 other events, 140.6 us)
Sparse Core Ops, SparseCore 0:
  25.5 309.4 all-reduce.30
  1754.8 557.2 all-reduce.28
where the time goes:
time: 2400 us; the launch traced here: 2390 us
  waiting for transfers between devices  807 us (34%)
  local copies, waits for them, and re-layouts  655 us (27%)
  blocking collectives  531 us (22%)
  matrix products  225 us (9%)
  other arithmetic  155 us (6%)
    psum x1, waiting for transfers between devices, on_device(): total = lax.psum(grad_local, ('seg', 'clip'))  518 us
    unnamed x3, waiting for transfers between devices  289 us
    psum x6, blocking collectives, norm_backward(): total_gain, total_shift = lax.psum((part_gain, part_shift), ('seg', 'clip'))  241 us
    psum x6, blocking collectives, norm_forward(): lax.psum((jnp.sum(values * rows_mask, axis=0), jnp.sum(values * values *...  241 us
    dot_general x33, matrix products, matmul(): return jnp.dot(left, right, preferred_element_type=jnp.float32)  225 us
    unnamed x265, local copies, waits for them, and re-layouts  194 us
    reshape x2, local copies, waits for them, and re-layouts, piece_at(): shard_rows = flat.reshape(devices, -1)  92.1 us
    concatenate x18, local copies, waits for them, and re-layouts, grid_patches(): return jnp.concatenate(windows, axis=-1).reshape(-1, 9 * channels)  52.7 us
  transfers between devices with their start and end apart: 2, of which 2 were waited for; matrix products, arithmetic and copies ran while one was open for 2% of the time, Pallas kernels for 0%

commit v1 on v0

v1 whole, which is shorter than its diff:
```python
import functools
import math

import jax
import jax.numpy as jnp
from jax import lax
from jax.experimental import pallas as pl
from jax.experimental.pallas import tpu as pltpu
from jax.sharding import PartitionSpec as P

D = 2048
MID = 512
GATE = 128
CLASSES = 174
GRID = 7
HW = 49
STEP = 7
LANES = 128

NORM_EPS = 1e-05
CLIP_LIMIT = 0.001
LEARN_RATE = 0.04
WEIGHT_DECAY = 0.05
BETA_ONE = 0.9
BETA_TWO = 0.999
ADAM_EPS = 1e-08

AXES = ("seg", "clip")
MESH_ID = pl.DeviceIdType.MESH
BF16 = jnp.bfloat16
F32 = jnp.float32


def matmul(left, right):
    return jnp.dot(left, right, preferred_element_type=F32)


def silu_slope(values):
    sig_val = jax.nn.sigmoid(values)
    return sig_val * (1.0 + values * (1.0 - sig_val))


def small_sum_kernel(n_seg, n_clip, inner, x_ref, o_ref, mid, near, far, send_sem, recv_sem):
    seg = lax.axis_index("seg")
    clip = lax.axis_index("clip")
    outer = n_clip // inner
    group = clip // inner
    place = lax.rem(clip, inner)
    n_near = n_seg * inner - 1
    n_far = outer - 1

    def near_peer(i):
        return (
            lax.rem(seg + i // inner, n_seg),
            group * inner + lax.rem(place + lax.rem(i, inner), inner),
        )

    def far_peer(i):
        return (seg, lax.rem(group + i, outer) * inner + place)

    def copy_near(i):
        return pltpu.make_async_remote_copy(
            src_ref=x_ref,
            dst_ref=near.at[i - 1],
            send_sem=send_sem.at[i - 1],
            recv_sem=recv_sem.at[i - 1],
            device_id=near_peer(i),
            device_id_type=MESH_ID,
        )

    def copy_far(i):
        return pltpu.make_async_remote_copy(
            src_ref=mid,
            dst_ref=far.at[i - 1],
            send_sem=send_sem.at[n_near + i - 1],
            recv_sem=recv_sem.at[n_near + i - 1],
            device_id=far_peer(i),
            device_id_type=MESH_ID,
        )

    def repeat(first, last, action):
        if last - first <= 8:
            for i in range(first, last):
                action(i)
        else:

            def body(i, carry):
                action(i)
                return carry

            lax.fori_loop(first, last, body, 0)

    barrier = pltpu.get_barrier_semaphore()

    def greet(peer):
        pl.semaphore_signal(barrier, inc=1, device_id=peer, device_id_type=MESH_ID)

    repeat(1, n_near + 1, lambda i: greet(near_peer(i)))
    repeat(1, n_far + 1, lambda i: greet(far_peer(i)))
    pl.semaphore_wait(barrier, n_near + n_far)
    repeat(1, n_near + 1, lambda i: copy_near(i).start())
    repeat(1, n_near + 1, lambda i: copy_near(i).wait())
    mid[...] = x_ref[...] + jnp.sum(near[...], axis=0)
    repeat(1, n_far + 1, lambda i: copy_far(i).start())
    repeat(1, n_far + 1, lambda i: copy_far(i).wait())
    o_ref[...] = mid[...] + jnp.sum(far[...], axis=0)


def small_sum(values):
    n_seg = lax.axis_size("seg")
    n_clip = lax.axis_size("clip")
    inner = 4 if n_clip % 4 == 0 else 1
    n_near = n_seg * inner - 1
    n_far = n_clip // inner - 1
    rows = values.shape[0]
    return pl.pallas_call(
        functools.partial(small_sum_kernel, n_seg, n_clip, inner),
        out_shape=jax.ShapeDtypeStruct(values.shape, F32),
        in_specs=[pl.BlockSpec(memory_space=pltpu.VMEM)],
        out_specs=pl.BlockSpec(memory_space=pltpu.VMEM),
        scratch_shapes=[
            pltpu.VMEM(values.shape, F32),
            pltpu.VMEM((n_near,) + values.shape, F32),
            pltpu.VMEM((n_far,) + values.shape, F32),
            pltpu.SemaphoreType.DMA((n_near + n_far,)),
            pltpu.SemaphoreType.DMA((n_near + n_far,)),
        ],
        compiler_params=pltpu.CompilerParams(collective_id=rows // 8, has_side_effects=True),
        name="small_sum",
    )(values)


def sum_pair(first, second):
    channels = first.shape[0]
    stacked = jnp.concatenate([first.reshape(-1, LANES), second.reshape(-1, LANES)], axis=0)
    total = small_sum(stacked).reshape(2, channels)
    return total[0], total[1]


def scatter_kernel(n_clip, n_jobs, *refs):
    grads = refs[:n_jobs]
    outs = refs[n_jobs : 2 * n_jobs]
    ones = refs[2 * n_jobs : 3 * n_jobs]
    twos = refs[3 * n_jobs : 4 * n_jobs]
    threes = refs[4 * n_jobs : 5 * n_jobs]
    fours = refs[5 * n_jobs : 6 * n_jobs]
    send_sem, recv_sem = refs[6 * n_jobs :]
    seg = lax.axis_index("seg")
    clip = lax.axis_index("clip")
    depth = n_clip // 4
    z = clip // 4
    y = lax.rem(clip // 2, 2)
    x = lax.rem(clip, 2)
    first = (1 - seg) * y + seg * x
    second = (1 - seg) * x + seg * y
    step = 1 + seg
    jump = 2 - seg
    across_first = (seg, clip + jump * (1 - 2 * first))
    across_second = (seg, clip + step * (1 - 2 * second))
    other = (1 - seg, clip)
    per_job = 1 + 2 + 1 + (depth - 1)

    def along(i):
        return (seg, lax.rem(z + i, depth) * 4 + y * 2 + x)

    barrier = pltpu.get_barrier_semaphore()
    for peer in [other, across_first, across_second] + [along(i) for i in range(1, depth)]:
        pl.semaphore_signal(barrier, inc=1, device_id=peer, device_id_type=MESH_ID)
    pl.semaphore_wait(barrier, depth + 2)

    def remote(job, number, source, target, peer):
        index = job * per_job + number
        return pltpu.make_async_remote_copy(
            src_ref=source,
            dst_ref=target,
            send_sem=send_sem.at[index],
            recv_sem=recv_sem.at[index],
            device_id=peer,
            device_id_type=MESH_ID,
        )

    def core_copy(job):
        return remote(job, 0, grads[job].at[1 - seg], ones[job], other)

    def first_copy(job, k):
        source = ones[job].at[:, jump * (1 - first) + step * k]
        return remote(job, 1 + k, source, twos[job].at[:, k], across_first)

    def second_copy(job):
        return remote(job, 3, twos[job].at[:, 1 - second], threes[job], across_second)

    def line_copy(job, i):
        source = threes[job].at[lax.rem(z + i, depth)]
        return remote(job, 3 + i, source, fours[job].at[i - 1], along(i))

    for job in range(n_jobs):
        core_copy(job).start()
    for job in range(n_jobs):
        core_copy(job).wait()
        one = ones[job]

        def add_one(i, carry, job=job, one=one):
            zz = i // 4
            w = lax.rem(i, 4)
            total = one[zz, w].astype(F32) + grads[job][seg, zz, w].astype(F32)
            one[zz, w] = total.astype(BF16)
            return carry

        lax.fori_loop(0, 4 * depth, add_one, 0)
        for k in range(2):
            first_copy(job, k).start()
    for job in range(n_jobs):
        for k in range(2):
            first_copy(job, k).wait()
        one, two = ones[job], twos[job]

        def add_two(i, carry, one=one, two=two):
            zz = i // 2
            k = lax.rem(i, 2)
            total = two[zz, k].astype(F32) + one[zz, jump * first + step * k].astype(F32)
            two[zz, k] = total.astype(BF16)
            return carry

        lax.fori_loop(0, 2 * depth, add_two, 0)
        second_copy(job).start()
    for job in range(n_jobs):
        second_copy(job).wait()
        two, three = twos[job], threes[job]

        def add_three(zz, carry, two=two, three=three):
            three[zz] = (three[zz].astype(F32) + two[zz, second].astype(F32)).astype(BF16)
            return carry

        lax.fori_loop(0, depth, add_three, 0)
        for i in range(1, depth):
            line_copy(job, i).start()
    for job in range(n_jobs):
        for i in range(1, depth):
            line_copy(job, i).wait()
        total = threes[job][z].astype(F32)
        for i in range(1, depth):
            total = total + fours[job][i - 1].astype(F32)
        outs[job][...] = total


def reduce_scatter(grads):
    n_seg = lax.axis_size("seg")
    n_clip = lax.axis_size("clip")
    fits = n_seg == 2 and n_clip == 16 and all(g.shape[1] % 16 == 0 for g in grads)
    if not fits:
        return [lax.psum_scatter(g, AXES, scatter_dimension=0, tiled=True)[0].astype(F32) for g in grads]
    depth = n_clip // 4
    n_jobs = len(grads)
    sizes = [g.shape[1:] for g in grads]
    shaped = [g.reshape((n_seg, depth, 4) + s) for g, s in zip(grads, sizes)]
    vmem = pl.BlockSpec(memory_space=pltpu.VMEM)
    copies = n_jobs * (depth + 3)
    return pl.pallas_call(
        functools.partial(scatter_kernel, n_clip, n_jobs),
        out_shape=[jax.ShapeDtypeStruct(s, F32) for s in sizes],
        in_specs=[vmem] * n_jobs,
        out_specs=[vmem] * n_jobs,
        scratch_shapes=[pltpu.VMEM((depth, 4) + s, BF16) for s in sizes]
        + [pltpu.VMEM((depth, 2) + s, BF16) for s in sizes]
        + [pltpu.VMEM((depth,) + s, BF16) for s in sizes]
        + [pltpu.VMEM((depth - 1,) + s, BF16) for s in sizes]
        + [pltpu.SemaphoreType.DMA((copies,)), pltpu.SemaphoreType.DMA((copies,))],
        compiler_params=pltpu.CompilerParams(
            collective_id=20, has_side_effects=True, vmem_limit_bytes=60 * 1024 * 1024
        ),
        name="reduce_scatter",
    )(*shaped)


def layout():
    block_layout = [
        (D, MID),
        (9, MID, MID),
        (MID, D),
        (MID, GATE),
        (GATE, MID),
        (2 * MID + D,),
        (2 * MID + D,),
    ]
    return block_layout + block_layout + [(D, CLASSES), (CLASSES,)]


def widths(devices):
    return [(math.prod(extent) + devices - 1) // devices for extent in layout()]


def pad_rows(flat, rows):
    return jnp.pad(flat, (0, rows * LANES - flat.shape[0])).reshape(rows, LANES)


def small_rows(devices):
    wide = widths(devices)
    amount = sum(wide[3:7]) + sum(wide[10:14])
    amount_cls = wide[14] + wide[15]
    return [16 * ((a + 16 * LANES - 1) // (16 * LANES)) for a in (amount, amount_cls)]


def gather_parameters(master):
    devices = lax.axis_size("seg") * lax.axis_size("clip")
    wide = widths(devices)
    starts = [sum(wide[:i]) for i in range(len(wide))]
    low = master.astype(BF16)

    def part(i):
        return low[starts[i] : starts[i] + wide[i]]

    def gather(values):
        return lax.all_gather(values, AXES, axis=0, tiled=True)

    big = {}
    for base in (0, 7):
        for i, columns in ((0, MID), (1, MID), (2, D)):
            big[base + i] = gather(part(base + i).reshape(-1, columns))
    rows, rows_cls = small_rows(devices)
    small = gather(pad_rows(jnp.concatenate([part(i) for i in (3, 4, 5, 6, 10, 11, 12, 13)]), rows))
    small_cls = gather(pad_rows(jnp.concatenate([part(14), part(15)]), rows_cls))
    small = small.reshape(devices, rows * LANES)
    small_cls = small_cls.reshape(devices, rows_cls * LANES)
    shapes = layout()
    pieces = dict(big)

    def take(source, ids):
        offset = 0
        for i in ids:
            amount = math.prod(shapes[i])
            pieces[i] = source[:, offset : offset + wide[i]].reshape(-1)[:amount].reshape(shapes[i])
            offset += wide[i]

    take(small, (3, 4, 5, 6, 10, 11, 12, 13))
    take(small_cls, (14, 15))
    return [pieces[i] for i in range(16)]


def scatter_gradients(grads):
    devices = lax.axis_size("seg") * lax.axis_size("clip")
    wide = widths(devices)
    rows, rows_cls = small_rows(devices)

    def shards(i):
        flat = grads[i].reshape(-1)
        return jnp.pad(flat, (0, devices * wide[i] - flat.shape[0])).reshape(devices, wide[i])

    def pack(ids, n_rows):
        packed = jnp.concatenate([shards(i) for i in ids], axis=1).astype(BF16)
        return jnp.pad(packed, ((0, 0), (0, n_rows * LANES - packed.shape[1]))).reshape(devices, n_rows, LANES)

    smalls = (3, 4, 5, 6, 10, 11, 12, 13)
    jobs = []
    for base in (7, 0):
        for i in (2, 1, 0):
            columns = grads[base + i].shape[-1]
            jobs.append(grads[base + i].astype(BF16).reshape(devices, -1, columns))
    jobs.append(pack(smalls, rows))
    jobs.append(pack((14, 15), rows_cls))
    sums = reduce_scatter(jobs)
    mine = {}
    for k, i in enumerate((9, 8, 7, 2, 1, 0)):
        mine[i] = sums[k].reshape(-1)
    for ids, flat in ((smalls, sums[6].reshape(-1)), ((14, 15), sums[7].reshape(-1))):
        offset = 0
        for i in ids:
            mine[i] = flat[offset : offset + wide[i]]
            offset += wide[i]
    return jnp.concatenate([mine[i] for i in range(16)])


def grid_mean(values):
    channels = values.shape[-1]
    frames = values.shape[1]
    grids = values.reshape(GRID, GRID, frames, channels)
    padded = jnp.pad(grids, ((1, 1), (1, 1), (0, 0), (0, 0)))
    total = padded[:, 0:GRID] + padded[:, 1 : GRID + 1] + padded[:, 2 : GRID + 2]
    total = total[0:GRID] + total[1 : GRID + 1] + total[2 : GRID + 2]
    return (total / 9.0).reshape(values.shape)


def conv(values, kernel, numbers):
    return lax.conv_general_dilated(
        values, kernel, (1, 1), ((1, 1), (1, 1)), dimension_numbers=numbers, preferred_element_type=F32
    )


def norm_forward(values, rows_mask, live_rows, gain, shift):
    masked = values * rows_mask
    sums, squares = sum_pair(jnp.sum(masked, axis=0), jnp.sum(values * masked, axis=0))
    mean_val = sums / live_rows
    variance = squares / live_rows - mean_val * mean_val
    inv_std = lax.rsqrt(variance + NORM_EPS)
    normed = (values - mean_val) * inv_std
    return (normed * gain + shift, normed, inv_std)


def norm_backward(grad_out, normed, inv_std, live_rows, rows_mask, gain):
    part_gain = jnp.sum(grad_out * normed, axis=0)
    part_shift = jnp.sum(grad_out, axis=0)
    total_gain, total_shift = sum_pair(part_gain, part_shift)
    grad_in = gain * inv_std * (grad_out - rows_mask * (total_shift + normed * total_gain) / live_rows)
    return (grad_in, part_gain, part_shift)


def by_slot(values, clips):
    return values.reshape(HW, clips, -1, values.shape[-1])


def gate_forward(reduced, masks):
    following = masks[1][None, :, :, None]
    clips = masks[0].shape[0]
    slots = by_slot(reduced, clips)
    edge = lax.ppermute(slots[:, :, 0], "seg", [(i + 1, i) for i in range(lax.axis_size("seg") - 1)])
    later = jnp.concatenate([slots[:, :, 1:], edge[:, :, None]], axis=2)
    change = (following * (later.astype(F32) - slots.astype(F32))).reshape(reduced.shape)
    return (change + grid_mean(change)).astype(BF16)


def gate_backward(d_mixed, masks):
    present = masks[0][None, :, :, None]
    following = masks[1][None, :, :, None]
    clips = masks[0].shape[0]
    slots = by_slot(d_mixed, clips)
    edge = lax.ppermute(slots[:, :, -1], "seg", [(i, i + 1) for i in range(lax.axis_size("seg") - 1)])
    edge = edge.astype(F32)
    edge = edge + grid_mean(edge)
    wide = d_mixed.astype(F32)
    spread = by_slot(wide + grid_mean(wide), clips)
    earlier = jnp.concatenate([edge[:, :, None], spread[:, :, :-1]], axis=2)
    d_part = present * earlier - following * spread
    return d_part.astype(BF16).reshape(d_mixed.shape)


def block_forward(x_low, x_float, weights, masks, live_rows):
    w_in, w_mid, w_out, w_red, w_exp, gain_low, shift_low = weights
    gains = gain_low.astype(F32)
    shifts = shift_low.astype(F32)
    rows_mask = masks[2]
    frames = x_low.shape[0] // HW
    h_one = matmul(x_low, w_in)
    y_one, normed_one, inv_one = norm_forward(h_one, rows_mask, live_rows, gains[:MID], shifts[:MID])
    a_one = jax.nn.silu(y_one)
    a_one_low = a_one.astype(BF16)
    reduced = matmul(a_one_low, w_red).astype(BF16).reshape(HW, frames, GATE)
    mixed_flat = gate_forward(reduced, masks).reshape(-1, GATE)
    gate = jax.nn.sigmoid(matmul(mixed_flat, w_exp))
    gated = (a_one * (1.0 + gate)).astype(BF16).reshape(GRID, GRID, frames, MID)
    h_two = conv(gated, w_mid.reshape(3, 3, MID, MID), ("HWNC", "HWIO", "HWNC")).reshape(-1, MID)
    y_two, normed_two, inv_two = norm_forward(
        h_two, rows_mask, live_rows, gains[MID : 2 * MID], shifts[MID : 2 * MID]
    )
    a_two_low = jax.nn.silu(y_two).astype(BF16)
    h_three = matmul(a_two_low, w_out)
    y_three, normed_three, inv_three = norm_forward(
        h_three, rows_mask, live_rows, gains[2 * MID :], shifts[2 * MID :]
    )
    pre = y_three + x_float
    kept = (
        x_low,
        a_one,
        a_one_low,
        y_one,
        normed_one,
        inv_one,
        gate,
        mixed_flat,
        gated,
        y_two,
        normed_two,
        inv_two,
        a_two_low,
        normed_three,
        inv_three,
        pre,
    )
    return (jax.nn.silu(pre), kept)


def block_backward(d_out, kept, weights, masks, live_rows):
    w_in, w_mid, w_out, w_red, w_exp, gain_low, shift_low = weights
    gains = gain_low.astype(F32)
    (
        x_low,
        a_one,
        a_one_low,
        y_one,
        normed_one,
        inv_one,
        gate,
        mixed_flat,
        gated,
        y_two,
        normed_two,
        inv_two,
        a_two_low,
        normed_three,
        inv_three,
        pre,
    ) = kept
    rows_mask = masks[2]
    frames = x_low.shape[0] // HW
    d_pre = d_out * silu_slope(pre)
    d_h_three, gain_three, shift_three = norm_backward(
        d_pre, normed_three, inv_three, live_rows, rows_mask, gains[2 * MID :]
    )
    d_h_three_low = d_h_three.astype(BF16)
    g_out = matmul(a_two_low.T, d_h_three_low)
    d_a_two = matmul(d_h_three_low, w_out.T)
    d_y_two = d_a_two * silu_slope(y_two)
    d_h_two, gain_two, shift_two = norm_backward(
        d_y_two, normed_two, inv_two, live_rows, rows_mask, gains[MID : 2 * MID]
    )
    d_h_two_low = d_h_two.astype(BF16).reshape(GRID, GRID, frames, MID)
    g_mid = conv(gated, d_h_two_low, ("HWCN", "HWIO", "HWNC")).reshape(9 * MID, MID)
    turned = jnp.flip(w_mid.reshape(3, 3, MID, MID), (0, 1))
    d_gated = conv(d_h_two_low, turned, ("HWNC", "HWOI", "HWNC")).reshape(-1, MID)
    d_excite = (d_gated * a_one * gate * (1.0 - gate)).astype(BF16)
    g_exp = matmul(mixed_flat.T, d_excite)
    d_mixed = matmul(d_excite, w_exp.T).astype(BF16).reshape(HW, frames, GATE)
    d_reduced_flat = gate_backward(d_mixed, masks).reshape(-1, GATE)
    g_red = matmul(a_one_low.T, d_reduced_flat)
    d_a_one = d_gated * (1.0 + gate) + matmul(d_reduced_flat, w_red.T)
    d_y_one = d_a_one * silu_slope(y_one)
    d_h_one, gain_one, shift_one = norm_backward(
        d_y_one, normed_one, inv_one, live_rows, rows_mask, gains[:MID]
    )
    d_h_one_low = d_h_one.astype(BF16)
    g_in = matmul(x_low.T, d_h_one_low)
    d_x = d_pre + matmul(d_h_one_low, w_in.T)
    grads = [
        g_in,
        g_mid,
        g_out,
        g_red,
        g_exp,
        jnp.concatenate([gain_one, gain_two, gain_three]),
        jnp.concatenate([shift_one, shift_two, shift_three]),
    ]
    return (d_x, grads)


def on_device(inputs, clip_counts, labels, master, first_moment, second_moment):
    seg_count = lax.axis_size("seg")
    pieces = gather_parameters(master)
    first_weights = pieces[0:7]
    second_weights = pieces[7:14]
    w_cls = pieces[14]
    b_cls = pieces[15].astype(F32)
    clip_local, slot_local = inputs.shape[:2]
    frames = clip_local * slot_local
    slot_ids = lax.axis_index("seg") * slot_local + jnp.arange(slot_local, dtype=jnp.int32)
    present = (slot_ids[None, :] < clip_counts[:, None]).astype(F32)
    following = (slot_ids[None, :] + 1 < clip_counts[:, None]).astype(F32)
    rows_mask = jnp.broadcast_to(present.reshape(1, frames), (HW, frames)).reshape(-1, 1)
    masks = (present, following, rows_mask)
    live_part = jnp.full((8, LANES), HW * jnp.sum(present), F32)
    live_rows = small_sum(live_part)[0, 0]
    flat_in = inputs.reshape(frames, HW, D).transpose(1, 0, 2).reshape(-1, D)
    middle, kept_first = block_forward(flat_in, flat_in.astype(F32), first_weights, masks, live_rows)
    final, kept_second = block_forward(middle.astype(BF16), middle, second_weights, masks, live_rows)
    block = final.reshape(HW, clip_local, slot_local, D)
    partial_value = jnp.sum(block * present[None, :, :, None], axis=(0, 2))
    pooled_sum = lax.psum(partial_value.astype(BF16), "seg").astype(F32)
    counts_float = clip_counts.astype(F32)
    pooled = pooled_sum / (HW * counts_float)[:, None]
    pooled_low = pooled.astype(BF16)
    logits = matmul(pooled_low, w_cls) + b_cls
    clips_total = clip_local * lax.axis_size("clip")
    onehot = (labels[:, None] == jnp.arange(CLASSES, dtype=jnp.int32)[None, :]).astype(F32)
    d_logits = (jax.nn.softmax(logits, axis=1) - onehot) / clips_total
    d_lin = d_logits.astype(BF16)
    g_cls = matmul(pooled_low.T, d_lin) / seg_count
    g_bias = jnp.sum(d_logits, axis=0) / seg_count
    d_pooled = matmul(d_lin, w_cls.T)
    scaled = d_pooled / (HW * counts_float)[:, None]
    d_frame = present[:, :, None] * scaled[:, None, :]
    d_block = jnp.broadcast_to(d_frame.reshape(1, frames, D), (HW, frames, D)).reshape(-1, D)
    d_middle, grads_second = block_backward(d_block, kept_second, second_weights, masks, live_rows)
    input_grad, grads_first = block_backward(d_middle, kept_first, first_weights, masks, live_rows)
    grad_mine = scatter_gradients(grads_first + grads_second + [g_cls, g_bias])
    tail = jnp.concatenate(
        [
            jnp.pad(g_bias, (0, 8 * LANES - CLASSES)).reshape(8, LANES),
            jnp.full((8, LANES), jnp.sum(grad_mine * grad_mine), F32),
        ]
    )
    tail = small_sum(tail)
    norm = jnp.sqrt(tail[8, 0])
    bias_grad = tail[:8].reshape(-1)[:CLASSES]
    factor = jnp.minimum(1.0, CLIP_LIMIT / (norm + 1e-06))
    clipped = grad_mine * factor
    new_first = BETA_ONE * first_moment + (1.0 - BETA_ONE) * clipped
    new_second = BETA_TWO * second_moment + (1.0 - BETA_TWO) * clipped * clipped
    first_hat = new_first / (1.0 - BETA_ONE**STEP)
    second_hat = new_second / (1.0 - BETA_TWO**STEP)
    new_master = master - LEARN_RATE * (
        first_hat / (jnp.sqrt(second_hat) + ADAM_EPS) + WEIGHT_DECAY * master
    )
    grid_grad = input_grad.reshape(HW, frames, D).transpose(1, 0, 2)
    return (
        new_master,
        new_first,
        new_second,
        new_master.astype(BF16),
        grid_grad.reshape(inputs.shape),
        norm.reshape(1),
        bias_grad,
    )


def solution(mesh):
    return jax.shard_map(
        on_device,
        mesh=mesh,
        in_specs=(
            P("clip", "seg", None, None),
            P("clip"),
            P("clip"),
            P(AXES),
            P(AXES),
            P(AXES),
        ),
        out_specs=(
            P(AXES),
            P(AXES),
            P(AXES),
            P(AXES),
            P("clip", "seg", None, None),
            P(),
            P(),
        ),
        check_vma=False,
    )
```

time: 2400 us -> 948 us (0.40)
  waiting for transfers between devices: 807 us -> 21.4 us
  local copies, waits for them, and re-layouts: 655 us -> 104 us
  blocking collectives: 531 us -> 153 us
  Pallas kernels: 0 us -> 285 us
  matrix products: 225 us -> 200 us
    psum x1 -> x0, waiting for transfers between devices: 518 us -> none  [on_device(): total = lax.psum(grad_local, ('seg', 'clip'))]
    psum x13 -> x1, blocking collectives: 486 us -> 3.36 us  [on_device(): pooled_sum = lax.psum(partial_value.astype(BF16), 'seg').astype(F32)]
    unnamed x3 -> x6, waiting for transfers between devices: 289 us -> 0.12 us
    pallas_call x0 -> x15, Pallas kernels: none -> 285 us  [the longest x14 143 us: small_sum(): pl.pallas_call(functools.partial(small_sum_kernel, n_seg, n_clip, inner),...]
    reshape x37 -> x21, local copies, waits for them, and re-layouts: 257 us -> 15.1 us  [the longest x10 9.07 us: shards(): jnp.pad(flat, (0, devices * wide[i] - flat.shape[0]))]
    unnamed x265 -> x313, local copies, waits for them, and re-layouts: 194 us -> 40.2 us
    all_gather x0 -> x2, blocking collectives: none -> 149 us  [gather(): return lax.all_gather(values, AXES, axis=0, tiled=True)]
    dot_general x33 -> x27, matrix products: 225 us -> 129 us  [matmul(): return jnp.dot(left, right, preferred_element_type=F32)]
  transfers between devices with their start and end apart: 2 -> 10, of which waited for: 2 -> 1; matrix products, arithmetic and copies ran while one was open for 2% -> 16% of each run, Pallas kernels for 0% -> 6%
where the time goes in v1:
time: 948 us; the launch traced here: 939 us
  Pallas kernels  285 us (30%)
  matrix products  200 us (21%)
  blocking collectives  153 us (16%)
  other arithmetic  150 us (16%)
  local copies, waits for them, and re-layouts  104 us (11%)
  waiting for transfers between devices  21.4 us (2%)
  between operations  19.2 us (2%)
    all_gather x2, blocking collectives, gather(): return lax.all_gather(values, AXES, axis=0, tiled=True)  149 us
    pallas_call x14, Pallas kernels, small_sum(): pl.pallas_call(functools.partial(small_sum_kernel, n_seg, n_clip, inner),...  143 us
    pallas_call x1, Pallas kernels, reduce_scatter(): pl.pallas_call(functools.partial(scatter_kernel, n_clip, n_jobs), out_sha...  142 us
    dot_general x27, matrix products, matmul(): return jnp.dot(left, right, preferred_element_type=F32)  129 us
    conv_general_dilated x6, matrix products, conv(): lax.conv_general_dilated(values, kernel, (1, 1), ((1, 1), (1, 1)), dimens...  70.9 us
    unnamed x313, local copies, waits for them, and re-layouts  40.2 us
    mul x2, other arithmetic, block_forward(): return (jax.nn.silu(pre), kept)  24.2 us
    convert_element_type x2, other arithmetic, block_backward(): d_h_three_low = d_h_three.astype(BF16)  23.4 us
  transfers between devices with their start and end apart: 10, of which 1 were waited for; matrix products, arithmetic and copies ran while one was open for 16% of the time, Pallas kernels for 6%

profile of v1, /device:TPU:0, one launch (start us, length us, event | category | flops | bytes accessed | tf_op | source)
XLA Modules:
  0.0 938.6 jit_solution(5573796868816546844)
XLA Ops:
  13.6 75.9 %all_gather.25 = bf16[2560,128]{1,0:T(8,128)(2,1)S(1)} all-gather(bf16[80,128]{1,0:T(8,128)(2,1)S(1)} %fusion.72), channel_id=1, replica_groups=mesh['seg'=2,'clip'=16] {'seg','clip'}, dimensions={0}, use_global_device_ids=true | all-gather | bytes 675840 | tf_op jit(solution)/shard_map/all_gather | solution.py:313
  93.3 6.7 copy.18
  101.2 8.5 small_sum.15
  112.5 73.6 %all_gather.31 = bf16[3072,128]{1,0:T(8,128)(2,1)S(1)} all-gather(bf16[96,128]{1,0:T(8,128)(2,1)S(1)} %pad_bitcast_fusion.1), channel_id=1, replica_groups=mesh['seg'=2,'clip'=16] {'seg','clip'}, dimensions={0}, use_global_device_ids=true | all-gather | bytes 811008 | tf_op jit(solution)/shard_map/all_gather | solution.py:313
  187.3 6.4 multiply_reduce_fusion.8
  194.4 8.4 small_sum.14
  218.0 3.7 multiply_convert_fusion.9
  221.7 13.0 %multiply_reduce_fusion.7 = (f32[512]{0:T(512)S(1)}, f32[512]{0:T(512)S(1)}, f32[7,7,32,512]{3,2,1,0:T(8,128)S(1)}) fusion(f32[32]{0:T(128)} %copy-done.120, bf16[7,7,32,512]{3,2,1,0:T(8,128)(2,1)} %bitcast.446, bf16[3,3,512,512]{3,2,1,0:T(8,128)(2,1)} %bitcast.442), kind=kOutput, calls=%fused_computation.27 | convolution fusion | flops 6059785216 | bytes 9539712 | tf_op jit(solution)/shard_map/conv_general_dilated | solution.py:383
  235.4 12.5 %small_sum.16 = f32[8,128]{1,0:T(8,128)} custom-call(f32[8,128]{1,0:T(8,128)} %pad_maximum_fusion.11.x_ref), custom_call_target="tpu_custom_call" | custom-call | tf_op jit(solution)/shard_map/small_sum/pallas_call | solution.py:116
  251.4 2.1 fusion.21
  253.5 9.0 multiply_reduce_fusion.1
  263.1 9.5 %small_sum.17 = f32[32,128]{1,0:T(8,128)} custom-call(f32[32,128]{1,0:T(8,128)} %pad_maximum_fusion.2.x_ref), custom_call_target="tpu_custom_call" | custom-call | tf_op jit(solution)/shard_map/small_sum/pallas_call | solution.py:116
  276.6 14.0 %fusion.3 = f32[1568,2048]{1,0:T(8,128)} fusion(f32[2048]{0:T(1024)S(1)} %slice.513, f32[2048]{0:T(1024)S(1)} %get-tuple-element.99, f32[2048]{0:T(1024)S(1)} %fusion.77, f32[1568,2048]{1,0:T(8,128)} %get-tuple-element.122, f32[2048]{0:T(1024)S(1)} %get-tuple-element.61, bf16[4,8,49,2048]{3,1,0,2:T(8,128)(2,1)} %copy.18), kind=kLoop, calls=%fused_computation.18 | loop fusion | flops 32112640 | bytes 32145408 | tf_op jit(solution)/shard_map/jit(silu)/mul | solution.py:477
  290.7 7.8 multiply_reduce_fusion.6
  299.0 11.0 %small_sum.18 = f32[8,128]{1,0:T(8,128)} custom-call(f32[8,128]{1,0:T(8,128)} %pad_maximum_fusion.12.x_ref), custom_call_target="tpu_custom_call" | custom-call | tf_op jit(solution)/shard_map/small_sum/pallas_call | solution.py:116
  318.4 4.8 reshape_reshape.57
  328.6 3.4 multiply_convert_fusion.7
  332.0 11.5 %multiply_reduce_fusion.5 = (f32[512]{0:T(512)S(1)}, f32[512]{0:T(512)S(1)}, f32[7,7,32,512]{3,2,1,0:T(8,128)}) fusion(f32[32]{0:T(128)S(1)} %copy-done.121, bf16[7,7,32,512]{3,2,1,0:T(8,128)(2,1)} %bitcast.448, bf16[3,3,512,512]{3,2,1,0:T(8,128)(2,1)} %bitcast.444), kind=kOutput, calls=%fused_computation.23 | convolution fusion | flops 6059785216 | bytes 9539712 | tf_op jit(solution)/shard_map/conv_general_dilated | solution.py:383
  344.1 10.5 %small_sum.19 = f32[8,128]{1,0:T(8,128)} custom-call(f32[8,128]{1,0:T(8,128)} %pad_maximum_fusion.13.x_ref), custom_call_target="tpu_custom_call" | custom-call | tf_op jit(solution)/shard_map/small_sum/pallas_call | solution.py:116
  358.1 4.0 fusion.20
  362.1 21.2 %all-gather.17.cloned.1.call-done = bf16[512,2048]{1,0:T(8,128)(2,1)} async-done(((bf16[16,2048]{1,0:T(8,128)(2,1)}), bf16[512,2048]{1,0:T(8,128)(2,1)}) %all-gather.17.cloned.1.call-update) | async-done | bytes 2097168 | tf_op jit(solution)/shard_map/all_gather | solution.py:313
  383.4 8.9 multiply_reduce_fusion
  392.9 10.5 %small_sum.20 = f32[32,128]{1,0:T(8,128)} custom-call(f32[32,128]{1,0:T(8,128)} %pad_maximum_fusion.3.x_ref), custom_call_target="tpu_custom_call" | custom-call | tf_op jit(solution)/shard_map/small_sum/pallas_call | solution.py:116
  406.1 10.2 %fusion.2 = f32[1568,2048]{1,0:T(8,128)S(1)} fusion(f32[1568,2048]{1,0:T(8,128)} %fusion.3, f32[2048]{0:T(1024)S(1)} %slice.531, f32[2048]{0:T(1024)S(1)} %get-tuple-element.95, f32[2048]{0:T(1024)S(1)} %fusion.74, f32[1568,2048]{1,0:T(8,128)} %get-tuple-element.127, f32[2048]{0:T(1024)S(1)} %get-tuple-element.65), kind=kLoop, calls=%fused_computation.14 | loop fusion | flops 28901376 | bytes 38567936 | tf_op jit(solution)/shard_map/jit(silu)/mul | solution.py:477
  418.2 3.4 psum.7
  427.1 15.2 %multiply_reduce_fusion.3 = (f32[2048]{0:T(1024)S(1)}, f32[2048]{0:T(1024)S(1)}, f32[1568,2048]{1,0:T(8,128)}) fusion(f32[1568,2048]{1,0:T(8,128)} %get-tuple-element.127, f32[2048]{0:T(1024)S(1)} %fusion.74, f32[2048]{0:T(1024)S(1)} %get-tuple-element.65, f32[1568,2048]{1,0:T(8,128)} %fusion.3, f32[2048]{0:T(1024)S(1)} %slice.531, ...), kind=kLoop, calls=%fused_computation.11 | loop fusion | flops 51376128 | bytes 38846464 | tf_op jit(solution)/shard_map/reduce_sum | solution.py:399
  443.0 10.7 %small_sum.21 = f32[32,128]{1,0:T(8,128)} custom-call(f32[32,128]{1,0:T(8,128)} %pad_maximum_fusion.4.x_ref), custom_call_target="tpu_custom_call" | custom-call | tf_op jit(solution)/shard_map/small_sum/pallas_call | solution.py:116
  454.4 11.7 %multiply_convert_fusion.1 = bf16[1568,2048]{1,0:T(8,128)(2,1)S(1)} fusion(f32[1568,2048]{1,0:T(8,128)} %get-tuple-element.66, f32[1568,2048]{1,0:T(8,128)} %get-tuple-element.127, f32[]{:T(128)} %bitcast.5, f32[2048]{0:T(1024)S(1)} %get-tuple-element.92, f32[2048]{0:T(1024)S(1)} %get-tuple-element.91, f32[2048]{0:T(1024)S(1)} %fusion.74, ...), kind=kLoop, calls=%fused_computation.10 | loop fusion | flops 28901376 | bytes 32159876 | tf_op jit(solution)/shard_map/convert_element_type | solution.py:507
  466.2 6.7 multiply_reduce_fusion.12
  473.5 10.2 %small_sum.22 = f32[8,128]{1,0:T(8,128)} custom-call(f32[8,128]{1,0:T(8,128)} %pad_maximum_fusion.14.x_ref), custom_call_target="tpu_custom_call" | custom-call | tf_op jit(solution)/shard_map/small_sum/pallas_call | solution.py:116
  484.4 4.5 multiply_convert_fusion.5
  489.0 12.8 %fusion.117 = f32[7,7,32,512]{3,2,1,0:T(8,128)S(1)} fusion(bf16[7,7,32,512]{3,2,1,0:T(8,128)(2,1)S(1)} %bitcast.395, bf16[3,3,512,512]{3,2,1,0:T(8,128)(2,1)} %bitcast.445), kind=kOutput, calls=%fused_computation.310 | convolution fusion | flops 6056574976 | bytes 9535488 | tf_op jit(solution)/shard_map/conv_general_dilated | solution.py:383
  501.8 3.2 fusion.19
  506.4 10.5 %convolution_convert_fusion.4 = bf16[3,3,512,512]{3,2,1,0:T(8,128)(2,1)} fusion(bf16[7,7,32,512]{3,2,1,0:T(8,128)(2,1)S(1)} %bitcast.449, bf16[7,7,32,512]{3,2,1,0:T(8,128)(2,1)S(1)} %bitcast.396), kind=kOutput, calls=%fused_computation.95 | convolution fusion | flops 6058934272 | bytes 7929856 | tf_op jit(solution)/shard_map/conv_general_dilated | solution.py:383
  516.9 5.4 convolution_convert_fusion.2
  526.7 2.6 copy.27
  529.3 3.1 reshape.798
  540.9 2.9 convolution_convert_fusion.10
  543.8 3.2 multiply_reduce_fusion.11
  548.9 10.0 %small_sum.23 = f32[8,128]{1,0:T(8,128)} custom-call(f32[8,128]{1,0:T(8,128)} %pad_maximum_fusion.15.x_ref), custom_call_target="tpu_custom_call" | custom-call | tf_op jit(solution)/shard_map/small_sum/pallas_call | solution.py:116
  559.7 4.7 multiply_convert_fusion.4
  564.4 20.7 %multiply_reduce_fusion.2 = (f32[2048]{0:T(1024)S(1)}, f32[2048]{0:T(1024)S(1)}, f32[1568,2048]{1,0:T(8,128)}) fusion(f32[1568,2048]{1,0:T(8,128)} %get-tuple-element.122, f32[2048]{0:T(1024)S(1)} %copy-done.44, f32[2048]{0:T(1024)S(1)} %copy-done.38, bf16[1568,2048]{1,0:T(8,128)(2,1)} %bitcast.365, f32[2048]{0:T(1024)S(1)} %copy-done.61, ...), kind=kOutput, calls=%fused_computation.8 | convolution fusion | flops 3346132992 | bytes 48709632 | tf_op jit(solution)/shard_map/dot_general | solution.py:35
  585.8 10.5 %small_sum.24 = f32[32,128]{1,0:T(8,128)} custom-call(f32[32,128]{1,0:T(8,128)} %pad_maximum_fusion.5.x_ref), custom_call_target="tpu_custom_call" | custom-call | tf_op jit(solution)/shard_map/small_sum/pallas_call | solution.py:116
  597.0 11.7 %multiply_convert_fusion = bf16[1568,2048]{1,0:T(8,128)(2,1)S(1)} fusion(f32[1568,2048]{1,0:T(8,128)} %get-tuple-element.132, f32[1568,2048]{1,0:T(8,128)} %get-tuple-element.122, f32[2048]{0:T(1024)S(1)} %get-tuple-element.90, f32[2048]{0:T(1024)S(1)} %get-tuple-element.89, f32[2048]{0:T(1024)S(1)} %copy-done.55, f32[]{:T(128)} %bitcast.5, ...), kind=kLoop, calls=%fused_computation.7 | loop fusion | flops 28901376 | bytes 32159876 | tf_op jit(solution)/shard_map/convert_element_type | solution.py:507
  608.8 6.8 multiply_reduce_fusion.10
  616.2 10.3 %small_sum.25 = f32[8,128]{1,0:T(8,128)} custom-call(f32[8,128]{1,0:T(8,128)} %pad_maximum_fusion.16.x_ref), custom_call_target="tpu_custom_call" | custom-call | tf_op jit(solution)/shard_map/small_sum/pallas_call | solution.py:116
  627.3 3.5 multiply_convert_fusion.3
  630.8 12.6 %fusion.118 = f32[7,7,32,512]{3,2,1,0:T(8,128)S(1)} fusion(bf16[7,7,32,512]{3,2,1,0:T(8,128)(2,1)S(1)} %bitcast.397, bf16[3,3,512,512]{3,2,1,0:T(8,128)(2,1)} %bitcast.443), kind=kOutput, calls=%fused_computation.311 | convolution fusion | flops 6056574976 | bytes 9535488 | tf_op jit(solution)/shard_map/conv_general_dilated | solution.py:383
  643.5 3.4 fusion.16
  648.7 10.5 %convolution_convert_fusion.3 = bf16[3,3,512,512]{3,2,1,0:T(8,128)(2,1)} fusion(bf16[7,7,32,512]{3,2,1,0:T(8,128)(2,1)S(1)} %bitcast.447, bf16[7,7,32,512]{3,2,1,0:T(8,128)(2,1)S(1)} %bitcast.398), kind=kOutput, calls=%fused_computation.94 | convolution fusion | flops 6058934272 | bytes 7929856 | tf_op jit(solution)/shard_map/conv_general_dilated | solution.py:383
  659.2 5.5 convolution_convert_fusion.1
  664.7 5.2 fusion.30
  683.1 2.9 convolution_convert_fusion.12
  686.1 3.4 multiply_reduce_fusion.9
  690.7 10.1 %small_sum.26 = f32[8,128]{1,0:T(8,128)} custom-call(f32[8,128]{1,0:T(8,128)} %pad_maximum_fusion.17.x_ref), custom_call_target="tpu_custom_call" | custom-call | tf_op jit(solution)/shard_map/small_sum/pallas_call | solution.py:116
  708.0 3.5 multiply_convert_fusion.2
  712.6 7.0 fusion.33
  719.6 2.5 copy.26
  722.2 142.2 %reduce_scatter.1 = (f32[16,2048]{1,0:T(8,128)}, f32[144,512]{1,0:T(8,128)}, f32[64,512]{1,0:T(8,128)}, f32[16,2048]{1,0:T(8,128)}, f32[144,512]{1,0:T(8,128)}, ...) custom-call(bf16[2,4,4,16,2048]{4,3,2,1,0:T(8,128)(2,1)} %bitcast.392, ...), custom_call_target="tpu_custom_call" | custom-call | tf_op jit(solution)/shard_map/reduce_scatter/pallas_call | solution.py:258
  878.2 10.4 %concatenate.116 = f32[298246]{0:T(1024)S(1)} concatenate(f32[32768]{0:T(1024)S(1)} %bitcast.401, f32[73728]{0:T(1024)S(1)} %bitcast.399, f32[32768]{0:T(1024)} %bitcast.402, f32[2048]{0:T(1024)} %get-tuple-element.88, f32[2048]{0:T(1024)S(1)} %get-tuple-element.87, f32[192]{0:T(256)} %slice.558, f32[32768]{0:T(1024)} %bitcast.403, f32[73728]{0:T(1024)S(1)} %bitcast.400, ...), dimensions={0} | concatenate | bytes 2385968 | tf_op jit(solution)/shard_map/concatenate | solution.py:369
  890.8 10.3 %small_sum.27 = f32[16,128]{1,0:T(8,128)} custom-call(f32[16,128]{1,0:T(8,128)} %concatenate.117.x_ref), custom_call_target="tpu_custom_call" | custom-call | tf_op jit(solution)/shard_map/small_sum/pallas_call | solution.py:116
  902.9 10.1 %convolution_add_fusion = f32[1568,2048]{1,0:T(8,128)} fusion(f32[1568,2048]{1,0:T(8,128)} %get-tuple-element.132, bf16[1568,512]{1,0:T(8,128)(2,1)S(1)} %copy-done.5, bf16[2048,512]{1,0:T(8,128)(2,1)} %all-gather.7.cloned.1.call-done), kind=kOutput, calls=%fused_computation.21 | convolution fusion | flops 3291545600 | bytes 29392896 | tf_op jit(solution)/shard_map/dot_general | solution.py:35
  913.1 11.9 %copy.28 = f32[4,8,49,2048]{3,1,2,0:T(8,128)} copy(f32[4,8,49,2048]{3,1,0,2:T(8,128)} %bitcast.362) | data formatting | bytes 25690112
  926.3 3.9 fusion.106
  (517 shorter events, 132.5 us)
Async XLA Ops:
  7.2 179.3 %all-gather.7.cloned.1.call-start = ((), (), s32[]{:S(2)}) async-start(), calls=%async_computation | async-start | bytes 2162688 | tf_op jit(solution)/shard_map/all_gather | solution.py:313
  8.6 82.7 %copy-start.126 = (s32[4]{0:T(128)S(1)}, s32[4]{0:T(128)}, u32[]{:S(2)}) copy-start(s32[4]{0:T(128)} %param.7) | copy-start | bytes 52
  9.4 212.3 %all-gather.9.cloned.1.call-start = ((), (), s32[]{:S(2)}) async-start(), calls=%async_computation.1 | async-start | bytes 4866048 | tf_op jit(solution)/shard_map/all_gather | solution.py:313
  10.4 243.1 %all-gather.11.cloned.1.call-start = ((), (), s32[]{:S(2)}) async-start(), calls=%async_computation.2 | async-start | bytes 2162688 | tf_op jit(solution)/shard_map/all_gather | solution.py:313
  11.1 279.5 %all-gather.13.cloned.1.call-start = ((), (), s32[]{:S(2)}) async-start(), calls=%async_computation.3 | async-start | bytes 2162688 | tf_op jit(solution)/shard_map/all_gather | solution.py:313
  11.8 320.1 %all-gather.15.cloned.1.call-start = ((), (), s32[]{:S(2)}) async-start(), calls=%async_computation.4 | async-start | bytes 4866048 | tf_op jit(solution)/shard_map/all_gather | solution.py:313
  12.7 370.7 %all-gather.17.cloned.1.call-start = ((), (), s32[]{:S(2)}) async-start(), calls=%async_computation.5 | async-start | bytes 2162688 | tf_op jit(solution)/shard_map/all_gather | solution.py:313
  111.7 93.9 %copy-start.91 = (f32[512]{0:T(512)}, f32[512]{0:T(512)S(1)}, u32[]{:S(2)}) copy-start(f32[512]{0:T(512)S(1)} %get-tuple-element.102) | copy-start | bytes 6148
  111.7 93.8 %copy-start.84 = (f32[512]{0:T(512)}, f32[512]{0:T(512)S(1)}, u32[]{:S(2)}) copy-start(f32[512]{0:T(512)S(1)} %slice.498) | copy-start | bytes 6148
  111.8 93.7 %copy-start.39 = (bf16[512,128]{1,0:T(8,128)(2,1)}, bf16[512,128]{1,0:T(8,128)(2,1)S(1)}, u32[]{:S(2)}) copy-start(bf16[512,128]{1,0:T(8,128)(2,1)S(1)} %reshape_reshape.51) | copy-start | bytes 393220
  111.9 81.8 %copy-start.51 = (f32[3072]{0:T(1024)}, f32[3072]{0:T(1024)S(1)}, u32[]{:S(2)}) copy-start(f32[3072]{0:T(1024)S(1)} %reshape.819) | copy-start | bytes 36868
  193.7 23.5 %copy-start = (f32[1568,512]{1,0:T(8,128)}, f32[1568,512]{1,0:T(8,128)S(1)}, u32[]{:S(2)}) copy-start(f32[1568,512]{1,0:T(8,128)S(1)} %get-tuple-element.118) | copy-start | bytes 9633796
  208.3 5.9 collective-permute-start
  210.3 65.8 %copy-start.60 = (f32[2048]{0:T(1024)}, f32[2048]{0:T(1024)S(1)}, u32[]{:S(2)}) copy-start(f32[2048]{0:T(1024)S(1)} %slice.513) | copy-start | bytes 24580
  211.4 101.5 %copy-start.88 = (f32[512]{0:T(512)}, f32[512]{0:T(512)S(1)}, u32[]{:S(2)}) copy-start(f32[512]{0:T(512)S(1)} %slice.516) | copy-start | bytes 6148
  221.7 27.6 %copy-start.50 = (f32[8,128]{1,0:T(8,128)S(1)}, f32[8,128]{1,0:T(8,128)}, u32[]{:S(2)}) copy-start(f32[8,128]{1,0:T(8,128)} %small_sum.14) | copy-start | bytes 12292
  234.7 18.7 %copy-start.2 = (f32[7,7,32,512]{3,2,1,0:T(8,128)}, f32[7,7,32,512]{3,2,1,0:T(8,128)S(1)}, u32[]{:S(2)}) copy-start(f32[7,7,32,512]{3,2,1,0:T(8,128)S(1)} %get-tuple-element.121) | copy-start | bytes 9633796
  274.6 16.0 %copy-start.56 = (f32[2048]{0:T(1024)}, f32[2048]{0:T(1024)S(1)}, u32[]{:S(2)}) copy-start(f32[2048]{0:T(1024)S(1)} %get-tuple-element.99) | copy-start | bytes 24580
  290.6 22.3 %copy-start.41 = (bf16[512,128]{1,0:T(8,128)(2,1)S(1)}, bf16[512,128]{1,0:T(8,128)(2,1)}, u32[]{:S(2)}) copy-start(bf16[512,128]{1,0:T(8,128)(2,1)} %reshape_reshape.54) | copy-start | bytes 393220
  290.6 22.3 %copy-start.95 = (f32[512]{0:T(512)S(1)}, f32[512]{0:T(512)}, u32[]{:S(2)}) copy-start(f32[512]{0:T(512)} %get-tuple-element.98) | copy-start | bytes 6148
  312.9 14.9 %copy-start.71 = (f32[512]{0:T(512)}, f32[512]{0:T(512)S(1)}, u32[]{:S(2)}) copy-start(f32[512]{0:T(512)S(1)} %fusion.84) | copy-start | bytes 6148
  315.6 9.2 collective-permute-start.1
  332.0 24.0 %copy-start.49 = (f32[8,128]{1,0:T(8,128)S(1)}, f32[8,128]{1,0:T(8,128)}, u32[]{:S(2)}) copy-start(f32[8,128]{1,0:T(8,128)} %small_sum.18) | copy-start | bytes 12292
  358.1 108.0 %copy-start.133 = (f32[512]{0:T(512)}, f32[512]{0:T(512)S(1)}, u32[]{:S(2)}) copy-start(f32[512]{0:T(512)S(1)} %get-tuple-element.96) | copy-start | bytes 6148
  358.1 25.3 %copy-start.124 = (f32[512]{0:T(512)S(1)}, f32[512]{0:T(512)}, u32[]{:S(2)}) copy-start(f32[512]{0:T(512)} %get-tuple-element.97) | copy-start | bytes 6148
  442.4 23.8 %copy-start.45 = (f32[2048]{0:T(1024)}, f32[2048]{0:T(1024)S(1)}, u32[]{:S(2)}) copy-start(f32[2048]{0:T(1024)S(1)} %get-tuple-element.36) | copy-start | bytes 24580
  442.4 23.8 %copy-start.47 = (f32[2048]{0:T(1024)}, f32[2048]{0:T(1024)S(1)}, u32[]{:S(2)}) copy-start(f32[2048]{0:T(1024)S(1)} %get-tuple-element.37) | copy-start | bytes 24580
  454.4 11.8 %copy-start.23 = (f32[1568,512]{1,0:T(8,128)S(1)}, f32[1568,512]{1,0:T(8,128)}, u32[]{:S(2)}) copy-start(f32[1568,512]{1,0:T(8,128)} %fusion.20) | copy-start | bytes 9633796
  454.4 11.8 %copy-start.138 = (bf16[512,2048]{1,0:T(8,128)(2,1)S(1)}, bf16[512,2048]{1,0:T(8,128)(2,1)}, u32[]{:S(2)}) copy-start(bf16[512,2048]{1,0:T(8,128)(2,1)} %all-gather.17.cloned.1.call-done) | copy-start | bytes 6291460
  472.9 16.1 %copy-start.102 = (f32[512]{0:T(512)}, f32[512]{0:T(512)S(1)}, u32[]{:S(2)}) copy-start(f32[512]{0:T(512)S(1)} %get-tuple-element.52) | copy-start | bytes 6148
  472.9 16.1 %copy-start.104 = (f32[512]{0:T(512)}, f32[512]{0:T(512)S(1)}, u32[]{:S(2)}) copy-start(f32[512]{0:T(512)S(1)} %get-tuple-element.53) | copy-start | bytes 6148
  488.9 12.8 %copy-start.22 = (f32[1568,512]{1,0:T(8,128)S(1)}, f32[1568,512]{1,0:T(8,128)}, u32[]{:S(2)}) copy-start(f32[1568,512]{1,0:T(8,128)} %get-tuple-element.125) | copy-start | bytes 9633796
  488.9 12.8 %copy-start.72 = (f32[512]{0:T(512)S(1)}, f32[512]{0:T(512)}, u32[]{:S(2)}) copy-start(f32[512]{0:T(512)} %copy-done.71) | copy-start | bytes 6148
  505.6 19.3 %copy-start.6 = (bf16[1568,128]{1,0:T(8,128)(2,1)}, bf16[1568,128]{1,0:T(8,128)(2,1)S(1)}, u32[]{:S(2)}) copy-start(bf16[1568,128]{1,0:T(8,128)(2,1)S(1)} %convolution_convert_fusion.6) | copy-start | bytes 1204228
  523.1 14.7 %collective-permute-start.2 = (bf16[49,4,128]{2,1,0:T(4,128)(2,1)}, bf16[49,4,128]{2,1,0:T(4,128)(2,1)S(1)}, u32[]{:S(2)}, u32[]{:S(2)}) collective-permute-start(bf16[49,4,128]{2,1,0:T(4,128)(2,1)} %bitcast.357), channel_id=1, source_target_pairs={{0,16},{1,17},{2,18},{3,19},{4,20},{5,21},{6,22},{7,23},{8,24},{9,... | collective-permute-start | bytes 150536 | tf_op jit(solution)/shard_map/ppermute | solution.py:425
  543.8 15.8 %copy-start.100 = (f32[512]{0:T(512)S(1)}, f32[512]{0:T(512)}, u32[]{:S(2)}) copy-start(f32[512]{0:T(512)} %get-tuple-element.94) | copy-start | bytes 6148
  564.4 32.6 %copy-start.55 = (f32[2048]{0:T(1024)S(1)}, f32[2048]{0:T(1024)}, u32[]{:S(2)}) copy-start(f32[2048]{0:T(1024)} %get-tuple-element.60) | copy-start | bytes 24580
  597.0 11.7 %copy-start.132 = (f32[512]{0:T(512)S(1)}, f32[512]{0:T(512)}, u32[]{:S(2)}) copy-start(f32[512]{0:T(512)} %copy-done.131) | copy-start | bytes 6148
  608.8 18.4 %copy-start.3 = (f32[7,7,32,512]{3,2,1,0:T(8,128)S(1)}, f32[7,7,32,512]{3,2,1,0:T(8,128)}, u32[]{:S(2)}) copy-start(f32[7,7,32,512]{3,2,1,0:T(8,128)} %copy-done.2) | copy-start | bytes 9633796
  608.8 18.4 %copy-start.70 = (f32[512]{0:T(512)S(1)}, f32[512]{0:T(512)}, u32[]{:S(2)}) copy-start(f32[512]{0:T(512)} %copy-done.69) | copy-start | bytes 6148
  608.8 18.4 %copy-start.75 = (f32[512]{0:T(512)S(1)}, f32[512]{0:T(512)}, u32[]{:S(2)}) copy-start(f32[512]{0:T(512)} %copy-done.74) | copy-start | bytes 6148
  608.8 18.4 %copy-start.99 = (f32[512]{0:T(512)S(1)}, f32[512]{0:T(512)}, u32[]{:S(2)}) copy-start(f32[512]{0:T(512)} %get-tuple-element.58) | copy-start | bytes 6148
  630.8 12.7 %copy-start.1 = (f32[1568,512]{1,0:T(8,128)S(1)}, f32[1568,512]{1,0:T(8,128)}, u32[]{:S(2)}) copy-start(f32[1568,512]{1,0:T(8,128)} %copy-done) | copy-start | bytes 9633796
  630.8 12.7 %copy-start.19 = (f32[1568,512]{1,0:T(8,128)S(1)}, f32[1568,512]{1,0:T(8,128)}, u32[]{:S(2)}) copy-start(f32[1568,512]{1,0:T(8,128)} %get-tuple-element.120) | copy-start | bytes 9633796
  630.8 12.7 %copy-start.64 = (f32[512]{0:T(512)S(1)}, f32[512]{0:T(512)}, u32[]{:S(2)}) copy-start(f32[512]{0:T(512)} %copy-done.62) | copy-start | bytes 6148
  630.8 12.7 %copy-start.67 = (f32[512]{0:T(512)S(1)}, f32[512]{0:T(512)}, u32[]{:S(2)}) copy-start(f32[512]{0:T(512)} %copy-done.65) | copy-start | bytes 6148
  630.8 12.7 %copy-start.86 = (f32[512]{0:T(512)S(1)}, f32[512]{0:T(512)}, u32[]{:S(2)}) copy-start(f32[512]{0:T(512)} %copy-done.84) | copy-start | bytes 6148
  630.8 12.7 %copy-start.93 = (f32[512]{0:T(512)S(1)}, f32[512]{0:T(512)}, u32[]{:S(2)}) copy-start(f32[512]{0:T(512)} %copy-done.91) | copy-start | bytes 6148
  647.5 24.9 %copy-start.7 = (bf16[1568,128]{1,0:T(8,128)(2,1)}, bf16[1568,128]{1,0:T(8,128)(2,1)S(1)}, u32[]{:S(2)}) copy-start(bf16[1568,128]{1,0:T(8,128)(2,1)S(1)} %convolution_convert_fusion.5) | copy-start | bytes 1204228
  648.6 16.0 %slice-start = ((s8[12845056]{0:T(1024)(128)(4,1)}), s8[4194304]{0:T(1024)(128)(4,1)S(1)}, s32[]{:S(2)}) async-start(s8[12845056]{0:T(1024)(128)(4,1)} %bitcast.360), calls=%async_computation.6 | async-start | bytes 8388608
  648.6 16.0 %slice-start.1 = ((s8[12845056]{0:T(1024)(128)(4,1)}), s8[4194304]{0:T(1024)(128)(4,1)S(1)}, s32[]{:S(2)}) async-start(s8[12845056]{0:T(1024)(128)(4,1)} %bitcast.360), calls=%async_computation.7 | async-start | bytes 8388608
  648.7 16.0 %slice-start.2 = ((s8[12845056]{0:T(1024)(128)(4,1)}), s8[4194304]{0:T(1024)(128)(4,1)S(1)}, s32[]{:S(2)}) async-start(s8[12845056]{0:T(1024)(128)(4,1)} %bitcast.360), calls=%async_computation.8 | async-start | bytes 8388608
  670.6 9.3 collective-permute-start.3
  686.0 15.5 %copy-start.81 = (bf16[2048]{0:T(1024)(128)(2,1)S(1)}, bf16[2048]{0:T(1024)(128)(2,1)}, u32[]{:S(2)}) copy-start(bf16[2048]{0:T(1024)(128)(2,1)} %convert.94) | copy-start | bytes 12292
  686.1 15.5 %copy-start.117 = (bf16[512]{0:T(512)(128)(2,1)S(1)}, bf16[512]{0:T(512)(128)(2,1)}, u32[]{:S(2)}) copy-start(bf16[512]{0:T(512)(128)(2,1)} %convert.93) | copy-start | bytes 3076
  686.1 15.6 %copy-start.80 = (bf16[2048]{0:T(1024)(128)(2,1)S(1)}, bf16[2048]{0:T(1024)(128)(2,1)}, u32[]{:S(2)}) copy-start(bf16[2048]{0:T(1024)(128)(2,1)} %convert.91) | copy-start | bytes 12292
  686.1 15.6 %copy-start.116 = (bf16[512]{0:T(512)(128)(2,1)S(1)}, bf16[512]{0:T(512)(128)(2,1)}, u32[]{:S(2)}) copy-start(bf16[512]{0:T(512)(128)(2,1)} %convert.90) | copy-start | bytes 3076
  686.1 17.9 %copy-start.58 = (bf16[32,96]{1,0:T(8,128)(2,1)S(1)}, bf16[32,96]{1,0:T(8,128)(2,1)}, u32[]{:S(2)}) copy-start(bf16[32,96]{1,0:T(8,128)(2,1)} %reshape.797) | copy-start | bytes 18436
  686.1 17.9 %copy-start.59 = (bf16[32,96]{1,0:T(8,128)(2,1)S(1)}, bf16[32,96]{1,0:T(8,128)(2,1)}, u32[]{:S(2)}) copy-start(bf16[32,96]{1,0:T(8,128)(2,1)} %reshape.796) | copy-start | bytes 18436
  689.5 18.4 %copy-start.98 = (f32[512]{0:T(512)S(1)}, f32[512]{0:T(512)}, u32[]{:S(2)}) copy-start(f32[512]{0:T(512)} %get-tuple-element.93) | copy-start | bytes 6148
  864.3 25.2 %copy-start.82 = (f32[8,128]{1,0:T(8,128)S(1)}, f32[8,128]{1,0:T(8,128)}, u32[]{:S(2)}) copy-start(f32[8,128]{1,0:T(8,128)} %pad_bitcast_fusion.2) | copy-start | bytes 12292
  864.3 38.6 %copy-start.5 = (bf16[1568,512]{1,0:T(8,128)(2,1)S(1)}, bf16[1568,512]{1,0:T(8,128)(2,1)}, u32[]{:S(2)}) copy-start(bf16[1568,512]{1,0:T(8,128)(2,1)} %copy-done.4) | copy-start | bytes 4816900
  913.0 13.2 %copy-start.14 = (f32[298246]{0:T(1024)S(1)}, f32[298246]{0:T(1024)}, u32[]{:S(2)}) copy-start(f32[298246]{0:T(1024)} %param.9) | copy-start | bytes 3578956
  913.0 13.2 %copy-start.34 = (f32[298246]{0:T(1024)S(1)}, f32[298246]{0:T(1024)}, u32[]{:S(2)}) copy-start(f32[298246]{0:T(1024)} %param.10) | copy-start | bytes 3578956
  (95 other events, 403.9 us)
Sparse Core Ops, SparseCore 0:
  11.4 60.3 all-gather.6
  75.3 67.2 all-gather.8
  145.5 56.0 all-gather.10
  204.3 55.2 all-gather.12
  263.0 62.3 all-gather.14
  328.1 55.1 all-gather.16

commit v2 on v1

--- a/solution.py
+++ b/solution.py
@@ -369,6 +369,74 @@
     return jnp.concatenate([mine[i] for i in range(16)])
 
 
+def part_of(master, index):
+    devices = lax.axis_size("seg") * lax.axis_size("clip")
+    wide = widths(devices)
+    start = sum(wide[:index])
+    return master[start : start + wide[index]]
+
+
+def norm_table(master, live_part):
+    devices = lax.axis_size("seg") * lax.axis_size("clip")
+    me = lax.axis_index(AXES)
+    width = 2 * MID + D
+
+    def spread(indices, amount):
+        parts = jnp.stack([part_of(master, i) for i in indices]).astype(BF16).astype(F32)
+        table = jnp.zeros((len(indices), devices, parts.shape[1]), F32)
+        table = lax.dynamic_update_slice(table, parts[:, None, :], (0, me, 0))
+        return table.reshape(len(indices), -1)[:, :amount]
+
+    norms = spread((5, 6, 12, 13), width).reshape(-1, LANES)
+    bias = spread((15,), CLASSES)
+    bias = jnp.pad(bias.reshape(-1), (0, 2 * LANES - CLASSES)).reshape(2, LANES)
+    live = jnp.full((NORM_ROWS - norms.shape[0] - 2, LANES), live_part, F32)
+    return jnp.concatenate([norms, bias, live])
+
+
+def lanes_first(values):
+    lead = values.shape[:-2]
+    rows, columns = values.shape[-2:]
+    split = values.reshape(lead + (rows, columns // LANES, LANES))
+    return jnp.swapaxes(split, -3, -2).reshape(lead + (-1, LANES))
+
+
+def weight_shards(master):
+    devices = lax.axis_size("seg") * lax.axis_size("clip")
+    if lax.axis_size("seg") != 2 or devices != SMALL_SHARDS:
+        return None
+    low = master.astype(BF16)
+    shards = {}
+    small = []
+    for block in range(2):
+        base = 7 * block
+        shards["in%d" % block] = part_of(low, base).reshape(-1, MID)
+        shards["mid%d" % block] = part_of(low, base + 1).reshape(-1, MID)
+        shards["out%d" % block] = part_of(low, base + 2).reshape(-1, D)
+        small.append(part_of(low, base + 3).reshape(-1, GATE))
+        small.append(lanes_first(part_of(low, base + 4).reshape(-1, MID)))
+    shards["small"] = jnp.concatenate(small)
+    cls = part_of(low, 14).reshape(-1, CLASSES)
+    shards["cls"] = jnp.pad(cls, ((0, 0), (0, 2 * LANES - CLASSES)))
+    return shards
+
+
+def whole_weights(master):
+    pieces = gather_parameters(master)
+    whole = {}
+    small = []
+    for block in range(2):
+        w_in, w_mid, w_out, w_red, w_exp = pieces[7 * block : 7 * block + 5]
+        whole["in%d" % block] = w_in
+        whole["mid%d" % block] = w_mid.reshape(9 * MID, MID)
+        whole["out%d" % block] = w_out
+        small.append(w_red.reshape(SMALL_SHARDS, -1, GATE))
+        small.append(lanes_first(w_exp.reshape(SMALL_SHARDS, -1, MID)))
+    whole["small"] = jnp.concatenate(small, axis=1).reshape(-1, LANES)
+    whole["cls"] = jnp.pad(pieces[14], ((0, 0), (0, 2 * LANES - CLASSES)))
+    return whole
+
+
 def grid_mean(values):
     channels = values.shape[-1]
     frames = values.shape[1]
@@ -385,14 +453,501 @@
     )
 
 
-def norm_forward(values, rows_mask, live_rows, gain, shift):
-    masked = values * rows_mask
-    sums, squares = sum_pair(jnp.sum(masked, axis=0), jnp.sum(values * masked, axis=0))
-    mean_val = sums / live_rows
-    variance = squares / live_rows - mean_val * mean_val
-    inv_std = lax.rsqrt(variance + NORM_EPS)
-    normed = (values - mean_val) * inv_std
-    return (normed * gain + shift, normed, inv_std)
+class Links:
+    def __init__(self, n_seg, n_clip, send_sem, recv_sem):
+        self.n_seg = n_seg
+        self.n_clip = n_clip
+        self.inner = 4
+        self.outer = n_clip // 4
+        self.seg = lax.axis_index("seg")
+        self.clip = lax.axis_index("clip")
+        self.group = self.clip // 4
+        self.place = lax.rem(self.clip, 4)
+        y = self.place // 2
+        x = lax.rem(self.place, 2)
+        self.first = (1 - self.seg) * y + self.seg * x
+        self.second = (1 - self.seg) * x + self.seg * y
+        self.step = 1 + self.seg
+        self.jump = 2 - self.seg
+        self.across_first = (self.seg, self.clip + self.jump * (1 - 2 * self.first))
+        self.across_second = (self.seg, self.clip + self.step * (1 - 2 * self.second))
+        self.other = (1 - self.seg, self.clip)
+        self.send_sem = send_sem
+        self.recv_sem = recv_sem
+        self.used = 0
+
+    def take(self, count):
+        base = self.used
+        self.used += count
+        return base
+
+    def near_peer(self, i):
+        return (
+            lax.rem(self.seg + i // 4, self.n_seg),
+            self.group * 4 + lax.rem(self.place + lax.rem(i, 4), 4),
+        )
+
+    def far_peer(self, i):
+        return (self.seg, lax.rem(self.group + i, self.outer) * 4 + self.place)
+
+    def remote(self, index, source, target, peer):
+        return pltpu.make_async_remote_copy(
+            src_ref=source,
+            dst_ref=target,
+            send_sem=self.send_sem.at[index],
+            recv_sem=self.recv_sem.at[index],
+            device_id=peer,
+            device_id_type=MESH_ID,
+        )
+
+    def local(self, source, target):
+        return pltpu.make_async_copy(source, target, self.recv_sem.at[self.take(1)])
+
+    def meet(self):
+        barrier = pltpu.get_barrier_semaphore()
+        n_near = self.n_seg * 4 - 1
+        n_far = self.outer - 1
+
+        def greet(peer):
+            pl.semaphore_signal(barrier, inc=1, device_id=peer, device_id_type=MESH_ID)
+
+        repeat(1, n_near + 1, lambda i: greet(self.near_peer(i)))
+        repeat(1, n_far + 1, lambda i: greet(self.far_peer(i)))
+        pl.semaphore_wait(barrier, n_near + n_far)
+
+    def all_sum(self, source, middle, near, far):
+        n_near = self.n_seg * 4 - 1
+        n_far = self.outer - 1
+        base = self.take(n_near + n_far)
+
+        def close(i):
+            return self.remote(base + i - 1, source, near.at[i - 1], self.near_peer(i))
+
+        def distant(i):
+            return self.remote(base + n_near + i - 1, middle, far.at[i - 1], self.far_peer(i))
+
+        repeat(1, n_near + 1, lambda i: close(i).start())
+        repeat(1, n_near + 1, lambda i: close(i).wait())
+        middle[...] = source[...] + jnp.sum(near[...], axis=0)
+        repeat(1, n_far + 1, lambda i: distant(i).start())
+        repeat(1, n_far + 1, lambda i: distant(i).wait())
+        return middle[...] + jnp.sum(far[...], axis=0)
+
+
+def repeat(first, last, action):
+    if last - first <= 8:
+        for i in range(first, last):
+            action(i)
+    else:
+
+        def body(i, carry):
+            action(i)
+            return carry
+
+        lax.fori_loop(first, last, body, 0)
+
+
+def sum_scratch(n_seg, n_clip, shape):
+    return [
+        pltpu.VMEM(shape, F32),
+        pltpu.VMEM(shape, F32),
+        pltpu.VMEM((n_seg * 4 - 1,) + shape, F32),
+        pltpu.VMEM((n_clip // 4 - 1,) + shape, F32),
+    ]
+
+
+class Gather:
+    def __init__(self, links, shard, whole):
+        depth = links.outer
+        whole = whole.reshape((links.n_seg, depth, 4) + shard.shape)
+        base = links.take(depth + 3)
+        seg, z, place = links.seg, links.group, links.place
+        self.own = links.local(shard, whole.at[seg, z, place])
+        self.steps = [
+            [
+                links.remote(base + i - 1, shard, whole.at[seg, z, place], links.far_peer(i))
+                for i in range(1, depth)
+            ],
+            [
+                links.remote(
+                    base + depth - 1, whole.at[seg, :, place], whole.at[seg, :, place], links.across_second
+                )
+            ],
+            [],
+            [links.remote(base + depth + 2, whole.at[seg], whole.at[seg], links.other)],
+        ]
+        for k in range(2):
+            index = links.jump * links.first + links.step * k
+            self.steps[2].append(
+                links.remote(
+                    base + depth + k, whole.at[seg, :, index], whole.at[seg, :, index], links.across_first
+                )
+            )
+        self.at = -1
+
+    def advance(self, last=3):
+        if self.at >= 0:
+            for copy in self.steps[self.at]:
+                copy.wait()
+            if self.at == 0:
+                self.own.wait()
+        self.at += 1
+        if self.at == 0:
+            self.own.start()
+        if self.at <= 3:
+            for copy in self.steps[self.at]:
+                copy.start()
+
+    def finish(self):
+        while self.at <= 3:
+            self.advance()
+
+
+def row_vector(table, start, count):
+    return jnp.concatenate([table[start + k : start + k + 1, :] for k in range(count)], axis=1)
+
+
+def put_rows(target, start, vector, count):
+    width = vector.shape[1] // count
+    for k in range(count):
+        target[start + k : start + k + 1, :] = vector[:, k * width : (k + 1) * width]
+
+
+def fold(values):
+    return jnp.sum(values.reshape(-1, 8, values.shape[-1]), axis=0)
+
+
+def excite_weights(small, block):
+    shards = small.shape[0]
+    rows = small[:, 32 * block + 16 : 32 * block + 32].reshape(shards * 16, LANES)
+    deep = GATE // shards
+    line = lax.broadcasted_iota(jnp.int32, (GATE, shards * 16), 0)
+    column = lax.broadcasted_iota(jnp.int32, (GATE, shards * 16), 1)
+    parts = []
+    for k in range(MID // LANES):
+        wanted = (line // deep) * 16 + k * deep + lax.rem(line, deep)
+        pick = (column == wanted).astype(F32).astype(BF16)
+        parts.append(matmul(pick, rows))
+    return jnp.concatenate(parts, axis=1).astype(BF16)
+
+
+SMALL_SHARDS = 32
+NORM_ROWS = 104
+BLOCK_NORMS = 48
+
+
+def forward_kernel(n_seg, n_clip, block, jobs, plan, *refs):
+    refs = list(refs)
+
+    def pop(count=1):
+        taken = refs[:count]
+        del refs[:count]
+        return taken if count != 1 else taken[0]
+
+    last = block == 1
+    x_hbm, mask, following, norm_in = pop(4)
+    shards = dict(zip(jobs, [pop() for _ in jobs]))
+    given = dict(zip(plan, [pop() for _ in plan]))
+    wholes = dict(zip(jobs, [pop() for _ in jobs]))
+    h1_out, low_out, gate_out, mix_out, f_out, h2_out, a2_out, h3_out = pop(8)
+    out_hbm, norm_out, st1, st2, st3 = pop(5)
+    xv, w_in, w_mid, w_out, small = pop(5)
+    h1v, a1v, lowv, rv, edge, dpad, mixv, gatev, fpad, h2v, a2v, h3v = pop(12)
+    wide_sum, wide_square, w_exp = pop(3)
+    sums = [pop(4) for _ in range(4)]
+    pooled = pop() if last else None
+    send_sem, recv_sem = pop(2)
+    links = Links(n_seg, n_clip, send_sem, recv_sem)
+    frames = xv.shape[1]
+    live = norm_out if not last else norm_in
+    outgoing = []
+
+    def send_out(source, target):
+        copy = links.local(source, target)
+        copy.start()
+        outgoing.append(copy)
+
+    links.meet()
+    load_x = links.local(x_hbm, xv)
+    load_x.start()
+    gathers = {name: Gather(links, shards[name], wholes[name]) for name in jobs}
+
+    def load(name, target):
+        if name in gathers:
+            gathers[name].finish()
+            source = wholes[name]
+        else:
+            source = given[name]
+        copy = links.local(source.reshape(target.shape), target)
+        copy.start()
+        return copy
+
+    def push(*names):
+        for name in names:
+            if name in gathers and gathers[name].at <= 3:
+                gathers[name].advance()
+
+    own_in = "in%d" % block
+    own_mid = "mid%d" % block
+    own_out = "out%d" % block
+    if not last:
+        push(own_in, "small")
+        sums[0][0][...] = norm_in[...]
+        norm_out[...] = links.all_sum(*sums[0])
+        push(own_in, "small", own_mid)
+        dpad[...] = jnp.zeros_like(dpad)
+        fpad[...] = jnp.zeros_like(fpad)
+        push(own_in, "small")
+        push(own_in, "small", own_mid, own_out)
+    else:
+        push(own_mid)
+        dpad[...] = jnp.zeros_like(dpad)
+        fpad[...] = jnp.zeros_like(fpad)
+    wait_in = load(own_in, w_in)
+    wait_small = load("small", small)
+    wait_in.wait()
+    load_x.wait()
+    norms = live
+    base = BLOCK_NORMS * block
+    live_rows = norms[98:99, 0:1]
+    half = MID // LANES
+
+    def norm(index, tot, columns, start, out):
+        mean = jnp.concatenate([tot[k : k + 1] for k in range(4)], axis=1) / live_rows
+        square = jnp.concatenate([tot[4 + k : 5 + k] for k in range(4)], axis=1) / live_rows
+        inv = lax.rsqrt(square - mean * mean + NORM_EPS)
+        out[0:1, :] = mean
+        out[1:2, :] = inv
+        gain = row_vector(norms, base + start, columns // LANES)
+        shift = row_vector(norms, base + 24 + start, columns // LANES)
+        scale = gain * inv
+        return scale, shift - mean * scale
+
+    def masked_sums(values):
+        shaped = values.reshape(-1, frames, values.shape[-1])
+        masked = shaped * mask[...][None]
+        return fold(masked), fold(masked * shaped)
+
+    zeros = jnp.zeros((8, MID), F32)
+
+    def first(i, carry):
+        part = matmul(xv[pl.ds(GRID * i, GRID)].reshape(GRID * frames, D), w_in[...])
+        h1v[pl.ds(GRID * i, GRID)] = part.reshape(GRID, frames, MID)
+        one, two = masked_sums(part)
+        return (carry[0] + one, carry[1] + two)
+
+    one, two = lax.fori_loop(0, GRID, first, (zeros, zeros))
+    send_out(h1v, h1_out)
+    push(own_mid, own_out)
+    if not last:
+        push("in1")
+    stat = sums[1][0]
+    put_rows(stat, 0, jnp.sum(one, axis=0, keepdims=True), 4)
+    put_rows(stat, 4, jnp.sum(two, axis=0, keepdims=True), 4)
+    scale_one, shift_one = norm(0, links.all_sum(*sums[1]), MID, 0, st1)
+    push(own_mid)
+    wait_small.wait()
+    w_exp[...] = excite_weights(small, block)
+    red = small[:, 32 * block : 32 * block + 16].reshape(MID, GATE)
+
+    def second(i, carry):
+        for j in range(GRID):
+            y = h1v[GRID * i + j] * scale_one + shift_one
+            a = y * jax.nn.sigmoid(y)
+            a1v[GRID * i + j] = a
+            lowv[GRID * i + j] = a.astype(BF16)
+        part = matmul(lowv[pl.ds(GRID * i, GRID)].reshape(GRID * frames, MID), red)
+        rv[pl.ds(GRID * i, GRID)] = part.astype(BF16).reshape(GRID, frames, GATE)
+        return carry
+
+    lax.fori_loop(0, GRID, second, 0)
+    send_out(lowv, low_out)
+    swap = links.remote(links.take(1), rv.at[:, 0:16], edge, links.other)
+    swap.start()
+    if last:
+        push(own_mid)
+    push(own_out)
+    swap.wait()
+    clips = frames // 8
+    turn = frames - clips
+    row = lax.broadcasted_iota(jnp.int32, (frames, GATE), 0)
+
+    def change(i, carry):
+        for j in range(GRID):
+            now = rv[GRID * i + j].astype(F32)
+            rest = edge[GRID * i + j].astype(F32)
+            rest = jnp.concatenate([rest] * (frames // 16), axis=0)
+            later = jnp.where(row < turn, pltpu.roll(now, turn, 0), pltpu.roll(rest, turn, 0))
+            dpad[i + 1, j + 1] = following[...] * (later - now)
+        return carry
+
+    lax.fori_loop(0, GRID, change, 0)
+
+    def excite(i, carry):
+        for j in range(GRID):
+            total = jnp.zeros((frames, GATE), F32)
+            for k in range(9):
+                total = total + dpad[i + k // 3, j + k % 3]
+            mixv[GRID * i + j] = (dpad[i + 1, j + 1] + total / 9.0).astype(BF16)
+        e = matmul(mixv[pl.ds(GRID * i, GRID)].reshape(GRID * frames, GATE), w_exp[...])
+        e = e.reshape(GRID, frames, MID)
+        for j in range(GRID):
+            gate = jax.nn.sigmoid(e[j])
+            gatev[GRID * i + j] = gate.astype(BF16)
+            fpad[i + 1, j + 1] = (a1v[GRID * i + j] * (1.0 + gate)).astype(BF16)
+        return carry
+
+    lax.fori_loop(0, GRID, excite, 0)
+    send_out(mixv, mix_out)
+    send_out(gatev, gate_out)
+    send_out(fpad.at[pl.ds(1, GRID), pl.ds(1, GRID)], f_out)
+    wait_mid = load(own_mid, w_mid)
+    push(own_out, "in1", "cls")
+    wait_mid.wait()
+
+    def third(i, carry):
+        part = None
+        for k in range(9):
+            window = fpad[i + k // 3, pl.ds(k % 3, GRID)].reshape(GRID * frames, MID)
+            term = matmul(window, w_mid[k])
+            part = term if part is None else part + term
+        h2v[pl.ds(GRID * i, GRID)] = part.reshape(GRID, frames, MID)
+        one, two = masked_sums(part)
+        return (carry[0] + one, carry[1] + two)
+
+    one, two = lax.fori_loop(0, GRID, third, (zeros, zeros))
+    send_out(h2v, h2_out)
+    stat = sums[2][0]
+    put_rows(stat, 0, jnp.sum(one, axis=0, keepdims=True), 4)
+    put_rows(stat, 4, jnp.sum(two, axis=0, keepdims=True), 4)
+    push(own_out)
+    scale_two, shift_two = norm(1, links.all_sum(*sums[2]), MID, half, st2)
+    wait_out = load(own_out, w_out)
+    push("in1", "cls")
+    wait_out.wait()
+    wide_sum[...] = jnp.zeros_like(wide_sum)
+    wide_square[...] = jnp.zeros_like(wide_square)
+
+    def fourth(i, carry):
+        for j in range(GRID):
+            y = h2v[GRID * i + j] * scale_two + shift_two
+            a2v[GRID * i + j] = (y * jax.nn.sigmoid(y)).astype(BF16)
+        rows = a2v[pl.ds(GRID * i, GRID)].reshape(GRID * frames, MID)
+        for k in range(4):
+            part = matmul(rows, w_out[:, k * MID : (k + 1) * MID])
+            h3v[pl.ds(GRID * i, GRID), :, k * MID : (k + 1) * MID] = part.astype(BF16).reshape(
+                GRID, frames, MID
+            )
+            one, two = masked_sums(part)
+            wide_sum[:, k * MID : (k + 1) * MID] += one
+            wide_square[:, k * MID : (k + 1) * MID] += two
+        return carry
+
+    lax.fori_loop(0, GRID, fourth, 0)
+    send_out(a2v, a2_out)
+    send_out(h3v, h3_out)
+    push("in1", "cls")
+    stat = sums[3][0]
+    put_rows(stat, 0, jnp.sum(wide_sum[...], axis=0, keepdims=True), 4)
+    put_rows(stat, 4, jnp.sum(wide_square[...], axis=0, keepdims=True), 4)
+    scale_three, shift_three = norm(2, links.all_sum(*sums[3]), D, 2 * half, st3)
+    push("cls")
+    if last:
+        pooled[...] = jnp.zeros_like(pooled)
+        norm_out[...] = jnp.zeros_like(norm_out)
+
+    def fifth(p, carry):
+        for k in range(4):
+            span = slice(k * MID, (k + 1) * MID)
+            pre = h3v[p, :, span].astype(F32) * scale_three[:, span] + shift_three[:, span]
+            pre = pre + xv[p, :, span].astype(F32)
+            value = pre * jax.nn.sigmoid(pre)
+            if last:
+                pooled[:, span] += value * mask[...]
+            else:
+                xv[p, :, span] = value.astype(BF16)
+        return carry
+
+    lax.fori_loop(0, HW, fifth, 0)
+    send_out(pooled if last else xv, out_hbm)
+    for name in jobs:
+        gathers[name].finish()
+    for copy in outgoing:
+        copy.wait()
+
+
+def forward_block(block, x, mask, following, norms, shards, given):
+    n_seg = lax.axis_size("seg")
+    n_clip = lax.axis_size("clip")
+    cells, frames, width = x.shape
+    jobs = list(shards)
+    plan = list(given)
+    any_spec = pl.BlockSpec(memory_space=pl.ANY)
+    vmem = pl.BlockSpec(memory_space=pltpu.VMEM)
+    depth = n_clip // 4
+
+    def grid_shape(columns):
+        return (cells, frames, columns)
+
+    last = block == 1
+    devices = n_seg * n_clip
+    outs = [jax.ShapeDtypeStruct((devices * shards[n].shape[0], shards[n].shape[1]), BF16) for n in jobs]
+    outs += [
+        jax.ShapeDtypeStruct(grid_shape(MID), F32),
+        jax.ShapeDtypeStruct(grid_shape(MID), BF16),
+        jax.ShapeDtypeStruct(grid_shape(MID), BF16),
+        jax.ShapeDtypeStruct(grid_shape(GATE), BF16),
+        jax.ShapeDtypeStruct((GRID, GRID, frames, MID), BF16),
+        jax.ShapeDtypeStruct(grid_shape(MID), F32),
+        jax.ShapeDtypeStruct(grid_shape(MID), BF16),
+        jax.ShapeDtypeStruct(grid_shape(D), BF16),
+        jax.ShapeDtypeStruct((frames, D), F32) if last else jax.ShapeDtypeStruct(x.shape, BF16),
+        jax.ShapeDtypeStruct(norms.shape, F32),
+        jax.ShapeDtypeStruct((8, MID), F32),
+        jax.ShapeDtypeStruct((8, MID), F32),
+        jax.ShapeDtypeStruct((8, D), F32),
+    ]
+    out_specs = [any_spec] * (len(jobs) + 9) + [vmem] * 4
+
+    shapes = [(D, MID), (9, MID, MID), (MID, D), (SMALL_SHARDS, 4 * 16, LANES)]
+    scratch = [pltpu.VMEM(x.shape, BF16)]
+    scratch += [pltpu.VMEM(s, BF16) for s in shapes]
+    scratch += [
+        pltpu.VMEM(grid_shape(MID), F32),
+        pltpu.VMEM(grid_shape(MID), F32),
+        pltpu.VMEM(grid_shape(MID), BF16),
+        pltpu.VMEM(grid_shape(GATE), BF16),
+        pltpu.VMEM((cells, 16, GATE), BF16),
+        pltpu.VMEM((GRID + 2, GRID + 2, frames, GATE), F32),
+        pltpu.VMEM(grid_shape(GATE), BF16),
+        pltpu.VMEM(grid_shape(MID), BF16),
+        pltpu.VMEM((GRID + 2, GRID + 2, frames, MID), BF16),
+        pltpu.VMEM(grid_shape(MID), F32),
+        pltpu.VMEM(grid_shape(MID), BF16),
+        pltpu.VMEM(grid_shape(D), BF16),
+        pltpu.VMEM((8, D), F32),
+        pltpu.VMEM((8, D), F32),
+        pltpu.VMEM((GATE, MID), BF16),
+    ]
+    for shape in (norms.shape, (8, LANES), (8, LANES), (8, MID)):
+        scratch += sum_scratch(n_seg, n_clip, shape)
+    if last:
+        scratch.append(pltpu.VMEM((frames, D), F32))
+    count = 4 * (n_seg * 4 + depth) + len(jobs) * (depth + 4) + 32
+    scratch += [pltpu.SemaphoreType.DMA((count,)), pltpu.SemaphoreType.DMA((count,))]
+    results = pl.pallas_call(
+        functools.partial(forward_kernel, n_seg, n_clip, block, jobs, plan),
+        out_shape=outs,
+        in_specs=[any_spec, vmem, vmem, vmem] + [any_spec] * (len(jobs) + len(plan)),
+        out_specs=out_specs,
+        scratch_shapes=scratch,
+        compiler_params=pltpu.CompilerParams(
+            collective_id=30 + block, has_side_effects=True, vmem_limit_bytes=60 * 1024 * 1024
+        ),
+        name="forward_block",
+    )(x, mask, following, norms, *[shards[n] for n in jobs], *[given[n] for n in plan])
+    wholes = dict(zip(jobs, results[: len(jobs)]))
+    return wholes, results[len(jobs) :]
 
 
 def norm_backward(grad_out, normed, inv_std, live_rows, rows_mask, gain):
@@ -403,113 +958,48 @@
     return (grad_in, part_gain, part_shift)
 
 
-def by_slot(values, clips):
-    return values.reshape(HW, clips, -1, values.shape[-1])
-
-
-def gate_forward(reduced, masks):
-    following = masks[1][None, :, :, None]
-    clips = masks[0].shape[0]
-    slots = by_slot(reduced, clips)
-    edge = lax.ppermute(slots[:, :, 0], "seg", [(i + 1, i) for i in range(lax.axis_size("seg") - 1)])
-    later = jnp.concatenate([slots[:, :, 1:], edge[:, :, None]], axis=2)
-    change = (following * (later.astype(F32) - slots.astype(F32))).reshape(reduced.shape)
-    return (change + grid_mean(change)).astype(BF16)
-
-
 def gate_backward(d_mixed, masks):
-    present = masks[0][None, :, :, None]
-    following = masks[1][None, :, :, None]
-    clips = masks[0].shape[0]
-    slots = by_slot(d_mixed, clips)
-    edge = lax.ppermute(slots[:, :, -1], "seg", [(i, i + 1) for i in range(lax.axis_size("seg") - 1)])
+    present = masks[0].T[None, :, :, None]
+    following = masks[1].T[None, :, :, None]
+    slots = d_mixed.reshape(HW, masks[0].shape[1], masks[0].shape[0], GATE)
+    edge = lax.ppermute(slots[:, -1], "seg", [(i, i + 1) for i in range(lax.axis_size("seg") - 1)])
     edge = edge.astype(F32)
     edge = edge + grid_mean(edge)
     wide = d_mixed.astype(F32)
-    spread = by_slot(wide + grid_mean(wide), clips)
-    earlier = jnp.concatenate([edge[:, :, None], spread[:, :, :-1]], axis=2)
+    spread = (wide + grid_mean(wide)).reshape(slots.shape)
+    earlier = jnp.concatenate([edge[:, None], spread[:, :-1]], axis=1)
     d_part = present * earlier - following * spread
     return d_part.astype(BF16).reshape(d_mixed.shape)
 
 
-def block_forward(x_low, x_float, weights, masks, live_rows):
-    w_in, w_mid, w_out, w_red, w_exp, gain_low, shift_low = weights
-    gains = gain_low.astype(F32)
-    shifts = shift_low.astype(F32)
+def block_backward(d_out, x_low, kept, weights, norms, masks, live_rows):
+    w_in, w_mid, w_out, w_red, w_exp = weights
+    gains, shifts = norms
+    h_one, a_one_low, gate, mixed, gated, h_two, a_two_low, h_three, st_one, st_two, st_three = kept
     rows_mask = masks[2]
-    frames = x_low.shape[0] // HW
-    h_one = matmul(x_low, w_in)
-    y_one, normed_one, inv_one = norm_forward(h_one, rows_mask, live_rows, gains[:MID], shifts[:MID])
+    frames = x_low.shape[1]
+    x_low = x_low.reshape(-1, D)
+    normed_three = (h_three.reshape(-1, D).astype(F32) - st_three[0]) * st_three[1]
+    pre = normed_three * gains[2 * MID :] + shifts[2 * MID :] + x_low.astype(F32)
+    normed_two = (h_two.reshape(-1, MID) - st_two[0]) * st_two[1]
+    y_two = normed_two * gains[MID : 2 * MID] + shifts[MID : 2 * MID]
+    normed_one = (h_one.reshape(-1, MID) - st_one[0]) * st_one[1]
+    y_one = normed_one * gains[:MID] + shifts[:MID]
     a_one = jax.nn.silu(y_one)
-    a_one_low = a_one.astype(BF16)
-    reduced = matmul(a_one_low, w_red).astype(BF16).reshape(HW, frames, GATE)
-    mixed_flat = gate_forward(reduced, masks).reshape(-1, GATE)
-    gate = jax.nn.sigmoid(matmul(mixed_flat, w_exp))
-    gated = (a_one * (1.0 + gate)).astype(BF16).reshape(GRID, GRID, frames, MID)
-    h_two = conv(gated, w_mid.reshape(3, 3, MID, MID), ("HWNC", "HWIO", "HWNC")).reshape(-1, MID)
-    y_two, normed_two, inv_two = norm_forward(
-        h_two, rows_mask, live_rows, gains[MID : 2 * MID], shifts[MID : 2 * MID]
-    )
-    a_two_low = jax.nn.silu(y_two).astype(BF16)
-    h_three = matmul(a_two_low, w_out)
-    y_three, normed_three, inv_three = norm_forward(
-        h_three, rows_mask, live_rows, gains[2 * MID :], shifts[2 * MID :]
-    )
-    pre = y_three + x_float
-    kept = (
-        x_low,
-        a_one,
-        a_one_low,
-        y_one,
-        normed_one,
-        inv_one,
-        gate,
-        mixed_flat,
-        gated,
-        y_two,
-        normed_two,
-        inv_two,
-        a_two_low,
-        normed_three,
-        inv_three,
-        pre,
-    )
-    return (jax.nn.silu(pre), kept)
-
-
-def block_backward(d_out, kept, weights, masks, live_rows):
-    w_in, w_mid, w_out, w_red, w_exp, gain_low, shift_low = weights
-    gains = gain_low.astype(F32)
-    (
-        x_low,
-        a_one,
-        a_one_low,
-        y_one,
-        normed_one,
-        inv_one,
-        gate,
-        mixed_flat,
-        gated,
-        y_two,
-        normed_two,
-        inv_two,
-        a_two_low,
-        normed_three,
-        inv_three,
-        pre,
-    ) = kept
-    rows_mask = masks[2]
-    frames = x_low.shape[0] // HW
+    a_one_low = a_one_low.reshape(-1, MID)
+    a_two_low = a_two_low.reshape(-1, MID)
+    gate = gate.reshape(-1, MID).astype(F32)
+    mixed_flat = mixed.reshape(-1, GATE)
     d_pre = d_out * silu_slope(pre)
     d_h_three, gain_three, shift_three = norm_backward(
-        d_pre, normed_three, inv_three, live_rows, rows_mask, gains[2 * MID :]
+        d_pre, normed_three, st_three[1], live_rows, rows_mask, gains[2 * MID :]
     )
     d_h_three_low = d_h_three.astype(BF16)
     g_out = matmul(a_two_low.T, d_h_three_low)
     d_a_two = matmul(d_h_three_low, w_out.T)
     d_y_two = d_a_two * silu_slope(y_two)
     d_h_two, gain_two, shift_two = norm_backward(
-        d_y_two, normed_two, inv_two, live_rows, rows_mask, gains[MID : 2 * MID]
+        d_y_two, normed_two, st_two[1], live_rows, rows_mask, gains[MID : 2 * MID]
     )
     d_h_two_low = d_h_two.astype(BF16).reshape(GRID, GRID, frames, MID)
     g_mid = conv(gated, d_h_two_low, ("HWCN", "HWIO", "HWNC")).reshape(9 * MID, MID)
@@ -523,7 +1013,7 @@
     d_a_one = d_gated * (1.0 + gate) + matmul(d_reduced_flat, w_red.T)
     d_y_one = d_a_one * silu_slope(y_one)
     d_h_one, gain_one, shift_one = norm_backward(
-        d_y_one, normed_one, inv_one, live_rows, rows_mask, gains[:MID]
+        d_y_one, normed_one, st_one[1], live_rows, rows_mask, gains[:MID]
     )
     d_h_one_low = d_h_one.astype(BF16)
     g_in = matmul(x_low.T, d_h_one_low)
@@ -542,25 +1032,63 @@
 
 def on_device(inputs, clip_counts, labels, master, first_moment, second_moment):
     seg_count = lax.axis_size("seg")
-    pieces = gather_parameters(master)
-    first_weights = pieces[0:7]
-    second_weights = pieces[7:14]
-    w_cls = pieces[14]
-    b_cls = pieces[15].astype(F32)
     clip_local, slot_local = inputs.shape[:2]
     frames = clip_local * slot_local
     slot_ids = lax.axis_index("seg") * slot_local + jnp.arange(slot_local, dtype=jnp.int32)
     present = (slot_ids[None, :] < clip_counts[:, None]).astype(F32)
     following = (slot_ids[None, :] + 1 < clip_counts[:, None]).astype(F32)
-    rows_mask = jnp.broadcast_to(present.reshape(1, frames), (HW, frames)).reshape(-1, 1)
+    rows_mask = jnp.broadcast_to(present.T.reshape(1, frames), (HW, frames)).reshape(-1, 1)
     masks = (present, following, rows_mask)
-    live_part = jnp.full((8, LANES), HW * jnp.sum(present), F32)
-    live_rows = small_sum(live_part)[0, 0]
-    flat_in = inputs.reshape(frames, HW, D).transpose(1, 0, 2).reshape(-1, D)
-    middle, kept_first = block_forward(flat_in, flat_in.astype(F32), first_weights, masks, live_rows)
-    final, kept_second = block_forward(middle.astype(BF16), middle, second_weights, masks, live_rows)
-    block = final.reshape(HW, clip_local, slot_local, D)
-    partial_value = jnp.sum(block * present[None, :, :, None], axis=(0, 2))
+    frame_mask = jnp.broadcast_to(present.T.reshape(frames, 1), (frames, MID))
+    frame_following = jnp.broadcast_to(following.T.reshape(frames, 1), (frames, GATE))
+    table = norm_table(master, HW * jnp.sum(present))
+    x_low = inputs.transpose(2, 1, 0, 3).reshape(HW, frames, D)
+    shards = weight_shards(master)
+    if shards is None:
+        weights = whole_weights(master)
+        jobs = ((), ())
+    else:
+        weights = {}
+        jobs = (("in0", "small", "mid0", "out0", "in1"), ("mid1", "out1", "cls"))
+    kept = []
+    flowing = x_low
+    flows = []
+    for block in range(2):
+        flows.append(flowing)
+        names = ("in%d" % block, "small", "mid%d" % block, "out%d" % block)
+        given = {name: weights[name] for name in names if name not in jobs[block]}
+        gathered, results = forward_block(
+            block,
+            flowing,
+            frame_mask,
+            frame_following,
+            table,
+            {name: shards[name] for name in jobs[block]},
+            given,
+        )
+        weights.update(gathered)
+        if block == 0:
+            table = results[9]
+        kept.append(results[:8] + results[10:])
+        flowing = results[8]
+    live_rows = table[98, 0]
+    small = weights["small"].reshape(SMALL_SHARDS, 4, 16, LANES)
+    block_weights = []
+    for block in range(2):
+        w_exp = small[:, 2 * block + 1].reshape(SMALL_SHARDS, MID // LANES, GATE // SMALL_SHARDS, LANES)
+        block_weights.append(
+            (
+                weights["in%d" % block],
+                weights["mid%d" % block],
+                weights["out%d" % block],
+                small[:, 2 * block].reshape(MID, GATE),
+                jnp.swapaxes(w_exp, 1, 2).reshape(GATE, MID),
+            )
+        )
+    tables = [table[BLOCK_NORMS * b : BLOCK_NORMS * (b + 1)].reshape(2, -1) for b in range(2)]
+    w_cls = weights["cls"][:, :CLASSES]
+    b_cls = table[96:98].reshape(-1)[:CLASSES]
+    partial_value = jnp.sum(flowing.reshape(slot_local, clip_local, D), axis=0)
     pooled_sum = lax.psum(partial_value.astype(BF16), "seg").astype(F32)
     counts_float = clip_counts.astype(F32)
     pooled = pooled_sum / (HW * counts_float)[:, None]
@@ -574,11 +1102,14 @@
     g_bias = jnp.sum(d_logits, axis=0) / seg_count
     d_pooled = matmul(d_lin, w_cls.T)
     scaled = d_pooled / (HW * counts_float)[:, None]
-    d_frame = present[:, :, None] * scaled[:, None, :]
-    d_block = jnp.broadcast_to(d_frame.reshape(1, frames, D), (HW, frames, D)).reshape(-1, D)
-    d_middle, grads_second = block_backward(d_block, kept_second, second_weights, masks, live_rows)
-    input_grad, grads_first = block_backward(d_middle, kept_first, first_weights, masks, live_rows)
-    grad_mine = scatter_gradients(grads_first + grads_second + [g_cls, g_bias])
+    d_frame = present.T[:, :, None] * scaled[None]
+    d_flow = jnp.broadcast_to(d_frame.reshape(1, frames, D), (HW, frames, D)).reshape(-1, D)
+    grads = [None, None]
+    for block in (1, 0):
+        d_flow, grads[block] = block_backward(
+            d_flow, flows[block], kept[block], block_weights[block], tables[block], masks, live_rows
+        )
+    grad_mine = scatter_gradients(grads[0] + grads[1] + [g_cls, g_bias])
     tail = jnp.concatenate(
         [
             jnp.pad(g_bias, (0, 8 * LANES - CLASSES)).reshape(8, LANES),
@@ -597,7 +1128,7 @@
     new_master = master - LEARN_RATE * (
         first_hat / (jnp.sqrt(second_hat) + ADAM_EPS) + WEIGHT_DECAY * master
     )
-    grid_grad = input_grad.reshape(HW, frames, D).transpose(1, 0, 2)
+    grid_grad = d_flow.reshape(HW, slot_local, clip_local, D).transpose(2, 1, 0, 3)
     return (
         new_master,
         new_first,

time: 948 us -> 841 us (0.89)
  blocking collectives: 153 us -> 3.59 us
  Pallas kernels: 285 us -> 424 us
  matrix products: 200 us -> 144 us
  other arithmetic: 150 us -> 109 us
  local copies, waits for them, and re-layouts: 104 us -> 142 us
  waiting for transfers between devices: 21.4 us -> 0.01 us
  between operations: 19.2 us -> 5.45 us
    pallas_call x0 -> x2, Pallas kernels: none -> 211 us  [forward_block(): pl.pallas_call(functools.partial(forward_kernel, n_seg, n_clip, block, jo...]
    all_gather x2 -> x0, blocking collectives: 149 us -> none  [gather(): return lax.all_gather(values, AXES, axis=0, tiled=True)]
    pallas_call x14 -> x7, Pallas kernels: 143 us -> 71.2 us  [small_sum(): pl.pallas_call(functools.partial(small_sum_kernel, n_seg, n_clip, inner),...]
    reshape x9 -> x15, local copies, waits for them, and re-layouts: 4.77 us -> 49.8 us  [the longest x2 32.4 us: on_device(): d_flow.reshape(HW, slot_local, clip_local, D).transpose(2, 1, 0, 3)]
    dot_general x27 -> x19, matrix products: 129 us -> 101 us  [matmul(): return jnp.dot(left, right, preferred_element_type=F32)]
    conv_general_dilated x6 -> x4, matrix products: 70.9 us -> 43.2 us  [conv(): lax.conv_general_dilated(values, kernel, (1, 1), ((1, 1), (1, 1)), dimens...]
    unnamed x313 -> x277, local copies, waits for them, and re-layouts: 40.2 us -> 15.1 us
    mul x7, other arithmetic: 33 us -> 11.4 us  [the longest x2 4.59 us: block_backward(): d_a_one = d_gated * (1.0 + gate) + matmul(d_reduced_flat, w_red.T)]
  transfers between devices with their start and end apart: 10 -> 2, of which waited for: 1 -> 0; matrix products, arithmetic and copies ran while one was open for 16% -> 10% of each run, Pallas kernels for 6% -> 0%
where the time goes in v2:
time: 841 us; the launch traced here: 832 us
  Pallas kernels  424 us (50%)
  matrix products  144 us (17%)
  local copies, waits for them, and re-layouts  142 us (17%)
  other arithmetic  109 us (13%)
    pallas_call x2, Pallas kernels, forward_block(): pl.pallas_call(functools.partial(forward_kernel, n_seg, n_clip, block, jo...  211 us
    pallas_call x1, Pallas kernels, reduce_scatter(): pl.pallas_call(functools.partial(scatter_kernel, n_clip, n_jobs), out_sha...  142 us
    dot_general x19, matrix products, matmul(): return jnp.dot(left, right, preferred_element_type=F32)  101 us
    pallas_call x7, Pallas kernels, small_sum(): pl.pallas_call(functools.partial(small_sum_kernel, n_seg, n_clip, inner),...  71.2 us
    conv_general_dilated x4, matrix products, conv(): lax.conv_general_dilated(values, kernel, (1, 1), ((1, 1), (1, 1)), dimens...  43.2 us
    reshape x2, local copies, waits for them, and re-layouts, on_device(): d_flow.reshape(HW, slot_local, clip_local, D).transpose(2, 1, 0, 3)  32.4 us
    convert_element_type x2, other arithmetic, block_backward(): d_h_three_low = d_h_three.astype(BF16)  25.4 us
  transfers between devices with their start and end apart: 2, of which 0 were waited for; matrix products, arithmetic and copies ran while one was open for 10% of the time, Pallas kernels for 0%

profile of v2, /device:TPU:0, one launch (start us, length us, event | category | flops | bytes accessed | tf_op | source)
XLA Modules:
  0.0 831.6 jit_solution(2298938838637759376)
XLA Ops:
  2.4 11.8 %copy.45 = bf16[49,8,4,2048]{3,2,1,0:T(4,128)(2,1)} copy(bf16[49,8,4,2048]{3,1,0,2:T(8,128)(2,1)} %bitcast.354) | data formatting | bytes 12845056 | tf_op jit(solution)/shard_map/transpose | solution.py:1045
  14.2 11.1 %reshape.811.refs_0_ = bf16[49,32,2048]{2,1,0:T(8,128)(2,1)} reshape(bf16[49,8,4,2048]{3,2,1,0:T(4,128)(2,1)} %copy.45) | data formatting | bytes 12845056 | tf_op jit(solution)/shard_map/reshape | solution.py:1045
  33.3 115.9 %forward_block.2 = (bf16[2048,512]{1,0:T(8,128)(2,1)}, bf16[2048,128]{1,0:T(8,128)(2,1)}, bf16[4608,512]{1,0:T(8,128)(2,1)}, bf16[512,2048]{1,0:T(8,128)(2,1)}, ...) custom-call(bf16[49,32,2048]{2,1,0:T(8,128)(2,1)} %reshape.811.refs_, ...), custom_call_target="tpu_custom_call" | custom-call | tf_op jit(solution)/shard_map/forward_block/pallas_call | solution.py:938
  156.1 95.2 %forward_block.3 = (bf16[4608,512]{1,0:T(8,128)(2,1)}, bf16[512,2048]{1,0:T(8,128)(2,1)}, bf16[2048,256]{1,0:T(8,128)(2,1)}, f32[49,32,512]{2,1,0:T(8,128)}, bf1...) custom-call(bf16[49,32,2048]{2,1,0:T(8,128)(2,1)} %get-tuple-element, ...), custom_call_target="tpu_custom_call" | custom-call | tf_op jit(solution)/shard_map/forward_block/pallas_call | solution.py:938
  252.4 3.6 psum.7
  256.0 1.6 fusion.67
  257.8 1.6 convolution_divide_fusion
  260.7 13.2 %multiply_reduce_fusion = (f32[2048]{0:T(1024)S(1)}, f32[2048]{0:T(1024)S(1)}, f32[49,32,2048]{2,1,0:T(8,128)}) fusion(bf16[49,32,2048]{2,1,0:T(8,128)(2,1)} %get-tuple-element.56, f32[2048]{0:T(1024)S(1)} %bitcast.402, f32[2048]{0:T(1024)S(1)} %bitcast.399, bf16[49,32,2048]{2,1,0:T(8,128)(2,1)} %get-tuple-element.48.refs_0_, ...), kind=kLoop, calls=%fused_computation.20 | loop fusion | flops 57798656 | bytes 26001408 | tf_op jit(solution)/shard_map/reduce_sum | solution.py:954
  274.5 10.5 %small_sum.7 = f32[32,128]{1,0:T(8,128)} custom-call(f32[32,128]{1,0:T(8,128)} %pad_maximum_fusion.3.x_ref), custom_call_target="tpu_custom_call" | custom-call | tf_op jit(solution)/shard_map/small_sum/pallas_call | solution.py:116
  288.5 15.2 %multiply_convert_fusion = (bf16[1568,2048]{1,0:T(8,128)(2,1)S(1)}, f32[1568,2048]{1,0:T(8,128)}) fusion(bf16[49,32,2048]{2,1,0:T(8,128)(2,1)} %get-tuple-element.56, f32[]{:T(128)} %bitcast.27, f32[2048]{0:T(1024)S(1)} %copy-done.52, f32[2048]{0:T(1024)S(1)} %copy-done.50, f32[1568]{0:T(1024)S(1)} %mul.654, f32[2048]{0:T(1024)S(1)} %bitcast.403, ...), kind=kLoop, calls=%fused_computation.18 | loop fusion | flops 70647808 | bytes 32438404 | tf_op jit(solution)/shard_map/convert_element_type | solution.py:997
  303.8 6.8 multiply_reduce_fusion.4
  311.2 9.9 %small_sum.8 = f32[8,128]{1,0:T(8,128)} custom-call(f32[8,128]{1,0:T(8,128)} %pad_maximum_fusion.9.x_ref), custom_call_target="tpu_custom_call" | custom-call | tf_op jit(solution)/shard_map/small_sum/pallas_call | solution.py:116
  321.9 1.8 fusion.64
  325.3 4.1 multiply_convert_fusion.10
  329.4 12.9 %multiply_convert_fusion.9 = (bf16[7,7,32,512]{3,2,1,0:T(8,128)(2,1)S(1)}, f32[7,7,32,512]{3,2,1,0:T(8,128)}) fusion(f32[7,7,32,512]{3,2,1,0:T(8,128)S(1)} %bitcast.344, f32[512]{0:T(512)S(1)} %copy-done.109, f32[512]{0:T(512)S(1)} %copy-done.107, f32[512]{0:T(512)S(1)} %bitcast.433, f32[512]{0:T(512)S(1)} %bitcast.429, ...), kind=kOutput, calls=%fused_computation.50 | convolution fusion | flops 6067814400 | bytes 15966208 | tf_op jit(solution)/shard_map/conv_general_dilated | solution.py:451
  343.6 1.9 collective-permute-start
  345.5 2.1 fusion.19
  350.4 10.6 %convolution_convert_fusion.4 = bf16[3,3,512,512]{3,2,1,0:T(8,128)(2,1)} fusion(bf16[7,7,32,512]{3,2,1,0:T(8,128)(2,1)S(1)} %copy-done.128, bf16[7,7,32,512]{3,2,1,0:T(8,128)(2,1)S(1)} %bitcast.373), kind=kOutput, calls=%fused_computation.57 | convolution fusion | flops 6058934272 | bytes 7929856 | tf_op jit(solution)/shard_map/conv_general_dilated | solution.py:451
  363.4 2.1 broadcast_add_fusion
  366.8 2.2 copy.56
  369.0 3.1 reshape.878
  372.2 11.8 %bitcast_convert_fusion = bf16[512,2048]{1,0:T(8,128)(2,1)} fusion(bf16[49,32,512]{2,1,0:T(8,128)(2,1)} %get-tuple-element.52, f32[49,32,2048]{2,1,0:T(8,128)} %get-tuple-element.107, bf16[49,32,2048]{2,1,0:T(8,128)(2,1)} %get-tuple-element.56, f32[]{:T(128)} %bitcast.27, f32[2048]{0:T(1024)S(1)} %copy-done.53, f32[2048]{0:T(1024)S(1)} %copy-done.51, ...), kind=kOutput, calls=%fused_computation.26 | convolution fusion | flops 3321495552 | bytes 23011460 | tf_op jit(solution)/shard_map/dot_general | solution.py:35
  384.0 2.3 bitcast_multiply_fusion.2
  386.3 1.5 slice_multiply_fusion.4
  391.6 2.1 fusion.18
  394.6 2.1 fusion.17
  397.3 11.1 %reshape_reshape.46 = bf16[1568,2048]{1,0:T(8,128)(2,1)} reshape(bf16[49,8,4,2048]{3,2,1,0:T(4,128)(2,1)} %copy.45) | data formatting | bytes 12845056 | tf_op jit(solution)/shard_map/reshape;reshape | solution.py:981
  414.9 2.3 copy.64
  420.3 1.6 fusion.35
  421.9 5.4 multiply_reduce_fusion.3
  429.0 10.0 %small_sum.9 = f32[8,128]{1,0:T(8,128)} custom-call(f32[8,128]{1,0:T(8,128)} %pad_maximum_fusion.10.x_ref), custom_call_target="tpu_custom_call" | custom-call | tf_op jit(solution)/shard_map/small_sum/pallas_call | solution.py:116
  439.8 4.5 multiply_convert_fusion.8
  444.3 8.7 %convolution_convert_fusion.2 = bf16[2048,512]{1,0:T(8,128)(2,1)} fusion(bf16[1568,2048]{1,0:T(8,128)(2,1)} %bitcast.341, bf16[1568,512]{1,0:T(8,128)(2,1)S(1)} %multiply_convert_fusion.8), kind=kOutput, calls=%fused_computation.55 | convolution fusion | flops 3289382912 | bytes 10125312 | tf_op jit(solution)/shard_map/dot_general | solution.py:35
  453.1 22.4 %fusion.6 = (f32[2048]{0:T(1024)S(1)}, f32[2048]{0:T(1024)S(1)}, f32[1568,2048]{1,0:T(8,128)}) fusion(bf16[49,32,2048]{2,1,0:T(8,128)(2,1)} %get-tuple-element.67, f32[2048]{0:T(1024)S(1)} %bitcast.413, f32[2048]{0:T(1024)S(1)} %bitcast.411, bf16[1568,2048]{1,0:T(8,128)(2,1)} %reshape_reshape.46, f32[2048]{0:T(1024)S(1)} %copy-done.85, ...), kind=kOutput, calls=%fused_computation.7 | convolution fusion | flops 3358978048 | bytes 48709632 | tf_op jit(solution)/shard_map/dot_general | solution.py:35
  476.1 10.3 %small_sum.10 = f32[32,128]{1,0:T(8,128)} custom-call(f32[32,128]{1,0:T(8,128)} %pad_maximum_fusion.4.x_ref), custom_call_target="tpu_custom_call" | custom-call | tf_op jit(solution)/shard_map/small_sum/pallas_call | solution.py:116
  487.1 10.2 %fusion.13 = bf16[1568,2048]{1,0:T(8,128)(2,1)S(1)} fusion(f32[1568,2048]{1,0:T(8,128)} %get-tuple-element.189, bf16[49,32,2048]{2,1,0:T(8,128)(2,1)} %get-tuple-element.67, f32[2048]{0:T(1024)S(1)} %get-tuple-element.159, f32[2048]{0:T(1024)S(1)} %get-tuple-element.158, f32[2048]{0:T(1024)S(1)} %bitcast.414, f32[2048]{0:T(1024)S(1)} %bitcast.412, ...), kind=kLoop, calls=%fused_computation.23 | loop fusion | flops 32112640 | bytes 25737348 | tf_op jit(solution)/shard_map/convert_element_type | solution.py:997
  497.4 5.2 convolution_convert_fusion.1
  502.6 6.9 multiply_reduce_fusion.2
  510.1 10.1 %small_sum.11 = f32[8,128]{1,0:T(8,128)} custom-call(f32[8,128]{1,0:T(8,128)} %pad_maximum_fusion.11.x_ref), custom_call_target="tpu_custom_call" | custom-call | tf_op jit(solution)/shard_map/small_sum/pallas_call | solution.py:116
  521.0 5.0 multiply_convert_fusion.7
  526.1 10.6 %convolution_convert_fusion.3 = bf16[3,3,512,512]{3,2,1,0:T(8,128)(2,1)} fusion(bf16[7,7,32,512]{3,2,1,0:T(8,128)(2,1)S(1)} %copy-done.125, bf16[7,7,32,512]{3,2,1,0:T(8,128)(2,1)S(1)} %bitcast.374), kind=kOutput, calls=%fused_computation.56 | convolution fusion | flops 6058934272 | bytes 7929856 | tf_op jit(solution)/shard_map/conv_general_dilated | solution.py:451
  536.8 9.1 %multiply_convert_fusion.6 = (bf16[7,7,32,512]{3,2,1,0:T(8,128)(2,1)S(1)}, f32[7,7,32,512]{3,2,1,0:T(8,128)S(1)}) fusion(f32[7,7,32,512]{3,2,1,0:T(8,128)S(1)} %bitcast.343, f32[512]{0:T(512)S(1)} %copy-done.104, f32[512]{0:T(512)S(1)} %copy-done.103, f32[512]{0:T(512)S(1)} %bitcast.427, f32[512]{0:T(512)S(1)} %bitcast.422, ...), kind=kOutput, calls=%fused_computation.45 | convolution fusion | flops 6067814400 | bytes 15966208 | tf_op jit(solution)/shard_map/conv_general_dilated | solution.py:451
  548.6 1.4 collective-permute-start.1
  552.5 2.3 bitcast_multiply_fusion.1
  559.3 1.6 reshape.873
  563.8 1.5 pad_maximum_fusion.1
  565.3 1.7 fusion.32
  567.1 5.1 multiply_reduce_fusion.1
  572.8 10.2 %small_sum.12 = f32[8,128]{1,0:T(8,128)} custom-call(f32[8,128]{1,0:T(8,128)} %pad_maximum_fusion.12.x_ref), custom_call_target="tpu_custom_call" | custom-call | tf_op jit(solution)/shard_map/small_sum/pallas_call | solution.py:116
  583.8 3.5 multiply_convert_fusion.5
  588.4 7.0 fusion.21
  595.5 2.5 copy.55
  598.0 2.1 convolution_convert_fusion.10
  601.8 141.8 %reduce_scatter.1 = (f32[16,2048]{1,0:T(8,128)}, f32[144,512]{1,0:T(8,128)}, f32[64,512]{1,0:T(8,128)}, f32[16,2048]{1,0:T(8,128)}, f32[144,512]{1,0:T(8,128)}, ...) custom-call(bf16[2,4,4,16,2048]{4,3,2,1,0:T(8,128)(2,1)} %bitcast.366, ...), custom_call_target="tpu_custom_call" | custom-call | tf_op jit(solution)/shard_map/reduce_scatter/pallas_call | solution.py:258
  743.7 1.4 slice_bitcast_fusion.3
  749.2 1.6 copy.67
  750.7 1.6 copy.68
  753.4 1.6 copy.70
  757.6 10.4 %concatenate.91 = f32[298246]{0:T(1024)S(1)} concatenate(f32[32768]{0:T(1024)S(1)} %bitcast.380, f32[73728]{0:T(1024)S(1)} %bitcast.376, f32[32768]{0:T(1024)} %bitcast.381, f32[2048]{0:T(1024)} %get-tuple-element.151, f32[2048]{0:T(1024)S(1)} %get-tuple-element.150, f32[192]{0:T(256)} %slice.536, f32[32768]{0:T(1024)} %bitcast.382, f32[73728]{0:T(1024)S(1)} %bitcast.377, ...), dimensions={0} | concatenate | bytes 2385968 | tf_op jit(solution)/shard_map/concatenate | solution.py:369
  770.1 10.1 %small_sum.13 = f32[16,128]{1,0:T(8,128)} custom-call(f32[16,128]{1,0:T(8,128)} %concatenate.92.x_ref), custom_call_target="tpu_custom_call" | custom-call | tf_op jit(solution)/shard_map/small_sum/pallas_call | solution.py:116
  782.8 10.2 %convolution_add_fusion = f32[1568,2048]{1,0:T(8,128)} fusion(f32[1568,2048]{1,0:T(8,128)} %get-tuple-element.189, bf16[1568,512]{1,0:T(8,128)(2,1)S(1)} %copy-done.8, bf16[2048,512]{1,0:T(8,128)(2,1)} %get-tuple-element.88), kind=kOutput, calls=%fused_computation.24 | convolution fusion | flops 3291545600 | bytes 29392896 | tf_op jit(solution)/shard_map/dot_general | solution.py:35
  793.0 15.3 %reshape.889 = f32[49,8,4,2048]{3,2,1,0:T(4,128)} reshape(f32[1568,2048]{1,0:T(8,128)} %convolution_add_fusion) | data formatting | bytes 25690112 | tf_op jit(solution)/shard_map/reshape | solution.py:1131
  808.4 17.1 %copy.80 = f32[49,8,4,2048]{3,1,0,2:T(8,128)} copy(f32[49,8,4,2048]{3,2,1,0:T(4,128)} %reshape.889) | data formatting | bytes 25690112 | tf_op jit(solution)/shard_map/reshape | solution.py:1131
  826.1 3.9 fusion.60
  (421 shorter events, 81.8 us)
Async XLA Ops:
  14.2 11.1 %copy-start.95 = (s32[4]{0:T(128)S(1)}, s32[4]{0:T(128)}, u32[]{:S(2)}) copy-start(s32[4]{0:T(128)} %param.7) | copy-start | bytes 52
  25.4 232.4 %copy-start.129 = (f32[4]{0:T(128)}, f32[4]{0:T(128)S(1)}, u32[]{:S(2)}) copy-start(f32[4]{0:T(128)S(1)} %convert_multiply_fusion) | copy-start | bytes 52
  31.3 255.0 %copy-start.93 = (f32[32]{0:T(128)}, f32[32]{0:T(128)S(1)}, u32[]{:S(2)}) copy-start(f32[32]{0:T(128)S(1)} %get-tuple-element.181) | copy-start | bytes 388
  156.1 101.7 %copy-start.121 = (s32[4]{0:T(128)S(1)}, s32[4]{0:T(128)}, u32[]{:S(2)}) copy-start(s32[4]{0:T(128)} %param.8) | copy-start | bytes 52
  260.6 27.7 %copy-start.35 = (f32[1,2048]{1,0:T(1,128)}, f32[1,2048]{1,0:T(1,128)S(1)}, u32[]{:S(2)}) copy-start(f32[1,2048]{1,0:T(1,128)S(1)} %get-tuple-element.130) | copy-start | bytes 24580
  260.6 27.7 %copy-start.37 = (f32[1,2048]{1,0:T(1,128)}, f32[1,2048]{1,0:T(1,128)S(1)}, u32[]{:S(2)}) copy-start(f32[1,2048]{1,0:T(1,128)S(1)} %get-tuple-element.131) | copy-start | bytes 24580
  260.6 27.7 %copy-start.48 = (f32[1,2048]{1,0:T(1,128)}, f32[1,2048]{1,0:T(1,128)S(1)}, u32[]{:S(2)}) copy-start(f32[1,2048]{1,0:T(1,128)S(1)} %get-tuple-element.129) | copy-start | bytes 24580
  260.7 27.1 %copy-start.6 = (f32[49,32,512]{2,1,0:T(8,128)S(1)}, f32[49,32,512]{2,1,0:T(8,128)}, u32[]{:S(2)}) copy-start(f32[49,32,512]{2,1,0:T(8,128)} %get-tuple-element.60) | copy-start | bytes 9633796
  273.9 11.2 %copy-start.39 = (f32[2048]{0:T(1024)}, f32[2048]{0:T(1024)S(1)}, u32[]{:S(2)}) copy-start(f32[2048]{0:T(1024)S(1)} %get-tuple-element.92) | copy-start | bytes 24580
  273.9 11.2 %copy-start.41 = (f32[2048]{0:T(1024)}, f32[2048]{0:T(1024)S(1)}, u32[]{:S(2)}) copy-start(f32[2048]{0:T(1024)S(1)} %get-tuple-element.91) | copy-start | bytes 24580
  287.8 16.0 %copy-start.70 = (f32[1,512]{1,0:T(1,128)}, f32[1,512]{1,0:T(1,128)S(1)}, u32[]{:S(2)}) copy-start(f32[1,512]{1,0:T(1,128)S(1)} %get-tuple-element.165) | copy-start | bytes 6148
  288.5 15.3 %copy-start.111 = (f32[512]{0:T(512)S(1)}, f32[512]{0:T(512)}, u32[]{:S(2)}) copy-start(f32[512]{0:T(512)} %get-tuple-element.133) | copy-start | bytes 6148
  288.5 15.3 %copy-start.112 = (f32[512]{0:T(512)S(1)}, f32[512]{0:T(512)}, u32[]{:S(2)}) copy-start(f32[512]{0:T(512)} %get-tuple-element.142) | copy-start | bytes 6148
  288.5 15.3 %copy-start.124 = (bf16[512,2048]{1,0:T(8,128)(2,1)S(1)}, bf16[512,2048]{1,0:T(8,128)(2,1)}, u32[]{:S(2)}) copy-start(bf16[512,2048]{1,0:T(8,128)(2,1)} %get-tuple-element.59) | copy-start | bytes 6291460
  303.8 20.1 %copy-start.88 = (f32[4,128]{1,0:T(4,128)S(1)}, f32[4,128]{1,0:T(4,128)}, u32[]{:S(2)}) copy-start(f32[4,128]{1,0:T(4,128)} %get-tuple-element.141) | copy-start | bytes 6148
  303.8 21.5 %copy-start.83 = (f32[1,512]{1,0:T(1,128)S(1)}, f32[1,512]{1,0:T(1,128)}, u32[]{:S(2)}) copy-start(f32[1,512]{1,0:T(1,128)} %get-tuple-element.163) | copy-start | bytes 6148
  325.3 20.2 %copy-start.62 = (f32[1,512]{1,0:T(1,128)}, f32[1,512]{1,0:T(1,128)S(1)}, u32[]{:S(2)}) copy-start(f32[1,512]{1,0:T(1,128)S(1)} %get-tuple-element.161) | copy-start | bytes 6148
  325.3 20.2 %copy-start.64 = (f32[1,512]{1,0:T(1,128)}, f32[1,512]{1,0:T(1,128)S(1)}, u32[]{:S(2)}) copy-start(f32[1,512]{1,0:T(1,128)S(1)} %get-tuple-element.162) | copy-start | bytes 6148
  342.9 18.6 %copy-start.12 = (bf16[1568,128]{1,0:T(8,128)(2,1)}, bf16[1568,128]{1,0:T(8,128)(2,1)S(1)}, u32[]{:S(2)}) copy-start(bf16[1568,128]{1,0:T(8,128)(2,1)S(1)} %convolution_convert_fusion.6) | copy-start | bytes 1204228
  343.6 73.6 %collective-permute-start = (bf16[49,4,128]{2,1,0:T(4,128)(2,1)}, bf16[49,4,128]{2,1,0:T(4,128)(2,1)}, u32[]{:S(2)}, u32[]{:S(2)}) collective-permute-start(bf16[49,4,128]{2,1,0:T(4,128)(2,1)} %slice_bitcast_fusion.1), channel_id=1, source_target_pairs={{0,16},{1,17},{2,18},{3,19},{4,20},{5,21},{6,22},{7,23},{8,24},{9,... | collective-permute-start | bytes 150536 | tf_op jit(solution)/shard_map/ppermute | solution.py:965
  365.5 6.6 copy-start.36
  365.5 6.6 copy-start.38
  365.5 6.6 copy-start.49
  365.5 6.6 copy-start.51
  365.6 6.6 copy-start.53
  365.6 6.6 copy-start.94
  372.2 11.8 %copy-start.17 = (f32[7,7,32,512]{3,2,1,0:T(8,128)S(1)}, f32[7,7,32,512]{3,2,1,0:T(8,128)}, u32[]{:S(2)}) copy-start(f32[7,7,32,512]{3,2,1,0:T(8,128)} %get-tuple-element.187) | copy-start | bytes 9633796
  384.0 6.7 copy-start.18
  384.0 7.6 copy-start.1
  397.3 11.2 %copy-start.42 = (f32[2048]{0:T(1024)S(1)}, f32[2048]{0:T(1024)}, u32[]{:S(2)}) copy-start(f32[2048]{0:T(1024)} %copy-done.41) | copy-start | bytes 24580
  397.3 12.3 %copy-start.40 = (f32[2048]{0:T(1024)S(1)}, f32[2048]{0:T(1024)}, u32[]{:S(2)}) copy-start(f32[2048]{0:T(1024)} %copy-done.39) | copy-start | bytes 24580
  413.7 6.6 copy-start.33
  413.7 6.6 copy-start.34
  414.8 5.4 copy-start.10
  414.8 7.0 copy-start.4
  414.8 7.0 copy-start.32
  414.8 7.0 copy-start.63
  414.8 7.0 copy-start.65
  414.9 7.0 copy-start.108
  414.9 7.0 copy-start.110
  421.8 5.5 copy-start.27
  421.9 17.9 %copy-start.81 = (f32[1,512]{1,0:T(1,128)S(1)}, f32[1,512]{1,0:T(1,128)}, u32[]{:S(2)}) copy-start(f32[1,512]{1,0:T(1,128)} %get-tuple-element.160) | copy-start | bytes 6148
  444.2 8.8 %copy-start.22 = (bf16[1568,512]{1,0:T(8,128)(2,1)}, bf16[1568,512]{1,0:T(8,128)(2,1)S(1)}, u32[]{:S(2)}) copy-start(bf16[1568,512]{1,0:T(8,128)(2,1)S(1)} %multiply_convert_fusion.8) | copy-start | bytes 4816900
  444.2 8.8 %copy-start.44 = (f32[1,2048]{1,0:T(1,128)S(1)}, f32[1,2048]{1,0:T(1,128)}, u32[]{:S(2)}) copy-start(f32[1,2048]{1,0:T(1,128)} %get-tuple-element.127) | copy-start | bytes 24580
  444.3 8.8 %copy-start.45 = (f32[1,2048]{1,0:T(1,128)S(1)}, f32[1,2048]{1,0:T(1,128)}, u32[]{:S(2)}) copy-start(f32[1,2048]{1,0:T(1,128)} %get-tuple-element.128) | copy-start | bytes 24580
  444.3 8.8 %copy-start.84 = (f32[2048]{0:T(1024)S(1)}, f32[2048]{0:T(1024)}, u32[]{:S(2)}) copy-start(f32[2048]{0:T(1024)} %get-tuple-element.146) | copy-start | bytes 24580
  444.3 8.8 %copy-start.85 = (f32[2048]{0:T(1024)S(1)}, f32[2048]{0:T(1024)}, u32[]{:S(2)}) copy-start(f32[2048]{0:T(1024)} %get-tuple-element.147) | copy-start | bytes 24580
  453.1 34.1 %copy-start.43 = (f32[1,2048]{1,0:T(1,128)S(1)}, f32[1,2048]{1,0:T(1,128)}, u32[]{:S(2)}) copy-start(f32[1,2048]{1,0:T(1,128)} %get-tuple-element.126) | copy-start | bytes 24580
  487.1 10.2 %copy-start.126 = (bf16[49,32,512]{2,1,0:T(8,128)(2,1)S(1)}, bf16[49,32,512]{2,1,0:T(8,128)(2,1)}, u32[]{:S(2)}) copy-start(bf16[49,32,512]{2,1,0:T(8,128)(2,1)} %get-tuple-element.65) | copy-start | bytes 4816900
  502.6 18.4 %copy-start.82 = (f32[1,512]{1,0:T(1,128)S(1)}, f32[1,512]{1,0:T(1,128)}, u32[]{:S(2)}) copy-start(f32[1,512]{1,0:T(1,128)} %get-tuple-element.155) | copy-start | bytes 6148
  521.0 15.7 %slice-start = ((s8[4718592]{0:T(1024)(128)(4,1)}), s8[4194304]{0:T(1024)(128)(4,1)S(1)}, s32[]{:S(2)}) async-start(s8[4718592]{0:T(1024)(128)(4,1)} %bitcast.471), calls=%async_computation | async-start | bytes 8388608
  526.0 10.7 %copy-start.20 = (bf16[49,32,512]{2,1,0:T(8,128)(2,1)S(1)}, bf16[49,32,512]{2,1,0:T(8,128)(2,1)}, u32[]{:S(2)}) copy-start(bf16[49,32,512]{2,1,0:T(8,128)(2,1)} %get-tuple-element.74) | copy-start | bytes 4816900
  526.0 10.7 %copy-start.60 = (f32[1,512]{1,0:T(1,128)S(1)}, f32[1,512]{1,0:T(1,128)}, u32[]{:S(2)}) copy-start(f32[1,512]{1,0:T(1,128)} %copy-done.59) | copy-start | bytes 6148
  526.0 10.7 %copy-start.103 = (f32[512]{0:T(512)S(1)}, f32[512]{0:T(512)}, u32[]{:S(2)}) copy-start(f32[512]{0:T(512)} %get-tuple-element.136) | copy-start | bytes 6148
  526.0 10.7 %copy-start.104 = (f32[512]{0:T(512)S(1)}, f32[512]{0:T(512)}, u32[]{:S(2)}) copy-start(f32[512]{0:T(512)} %get-tuple-element.137) | copy-start | bytes 6148
  526.1 10.7 %slice-start.1 = ((s8[4718592]{0:T(1024)(128)(4,1)}), s8[524288]{0:T(1024)(128)(4,1)S(1)}, s32[]{:S(2)}) async-start(s8[4718592]{0:T(1024)(128)(4,1)} %bitcast.471), calls=%async_computation.1 | async-start | bytes 1048576
  546.9 5.5 copy-start.11
  548.6 15.1 %collective-permute-start.1 = (bf16[49,4,128]{2,1,0:T(4,128)(2,1)}, bf16[49,4,128]{2,1,0:T(4,128)(2,1)S(1)}, u32[]{:S(2)}, u32[]{:S(2)}) collective-permute-start(bf16[49,4,128]{2,1,0:T(4,128)(2,1)} %slice_bitcast_fusion), channel_id=1, source_target_pairs={{0,16},{1,17},{2,18},{3,19},{4,20},{5,21},{6,22},{7,23},{8,24},{9,... | collective-permute-start | bytes 150536 | tf_op jit(solution)/shard_map/ppermute | solution.py:965
  567.1 16.7 %copy-start.61 = (f32[1,512]{1,0:T(1,128)S(1)}, f32[1,512]{1,0:T(1,128)}, u32[]{:S(2)}) copy-start(f32[1,512]{1,0:T(1,128)} %copy-done.59) | copy-start | bytes 6148
  567.1 16.7 %copy-start.80 = (f32[1,512]{1,0:T(1,128)S(1)}, f32[1,512]{1,0:T(1,128)}, u32[]{:S(2)}) copy-start(f32[1,512]{1,0:T(1,128)} %get-tuple-element.152) | copy-start | bytes 6148
  743.7 25.2 %copy-start.75 = (f32[8,128]{1,0:T(8,128)S(1)}, f32[8,128]{1,0:T(8,128)}, u32[]{:S(2)}) copy-start(f32[8,128]{1,0:T(8,128)} %pad_bitcast_fusion.1) | copy-start | bytes 12292
  743.7 39.1 %copy-start.8 = (bf16[1568,512]{1,0:T(8,128)(2,1)S(1)}, bf16[1568,512]{1,0:T(8,128)(2,1)}, u32[]{:S(2)}) copy-start(bf16[1568,512]{1,0:T(8,128)(2,1)} %copy-done.7) | copy-start | bytes 4816900
  808.3 17.7 %copy-start.14 = (f32[298246]{0:T(1024)S(1)}, f32[298246]{0:T(1024)}, u32[]{:S(2)}) copy-start(f32[298246]{0:T(1024)} %param.9) | copy-start | bytes 3578956
  808.4 17.7 %copy-start.23 = (f32[298246]{0:T(1024)S(1)}, f32[298246]{0:T(1024)}, u32[]{:S(2)}) copy-start(f32[298246]{0:T(1024)} %param.10) | copy-start | bytes 3578956
  (71 other events, 220.3 us)

commit v3 on v2

--- a/solution.py
+++ b/solution.py
@@ -33,11 +33,6 @@
 
 def matmul(left, right):
     return jnp.dot(left, right, preferred_element_type=F32)
-
-
-def silu_slope(values):
-    sig_val = jax.nn.sigmoid(values)
-    return sig_val * (1.0 + values * (1.0 - sig_val))
 
 
 def small_sum_kernel(n_seg, n_clip, inner, x_ref, o_ref, mid, near, far, send_sem, recv_sem):
@@ -128,13 +123,6 @@
         compiler_params=pltpu.CompilerParams(collective_id=rows // 8, has_side_effects=True),
         name="small_sum",
     )(values)
-
-
-def sum_pair(first, second):
-    channels = first.shape[0]
-    stacked = jnp.concatenate([first.reshape(-1, LANES), second.reshape(-1, LANES)], axis=0)
-    total = small_sum(stacked).reshape(2, channels)
-    return total[0], total[1]
 
 
 def scatter_kernel(n_clip, n_jobs, *refs):
@@ -435,16 +423,6 @@
     whole["small"] = jnp.concatenate(small, axis=1).reshape(-1, LANES)
     whole["cls"] = jnp.pad(pieces[14], ((0, 0), (0, 2 * LANES - CLASSES)))
     return whole
-
-
-def grid_mean(values):
-    channels = values.shape[-1]
-    frames = values.shape[1]
-    grids = values.reshape(GRID, GRID, frames, channels)
-    padded = jnp.pad(grids, ((1, 1), (1, 1), (0, 0), (0, 0)))
-    total = padded[:, 0:GRID] + padded[:, 1 : GRID + 1] + padded[:, 2 : GRID + 2]
-    total = total[0:GRID] + total[1 : GRID + 1] + total[2 : GRID + 2]
-    return (total / 9.0).reshape(values.shape)
 
 
 def conv(values, kernel, numbers):
@@ -762,22 +740,19 @@
 
     lax.fori_loop(0, GRID, second, 0)
     send_out(lowv, low_out)
-    swap = links.remote(links.take(1), rv.at[:, 0:16], edge, links.other)
+    swap = links.remote(links.take(1), rv, edge, links.other)
     swap.start()
     if last:
         push(own_mid)
     push(own_out)
     swap.wait()
-    clips = frames // 8
-    turn = frames - clips
-    row = lax.broadcasted_iota(jnp.int32, (frames, GATE), 0)
+    row = lax.rem(lax.broadcasted_iota(jnp.int32, (frames, GATE), 0), 8)
 
     def change(i, carry):
         for j in range(GRID):
             now = rv[GRID * i + j].astype(F32)
             rest = edge[GRID * i + j].astype(F32)
-            rest = jnp.concatenate([rest] * (frames // 16), axis=0)
-            later = jnp.where(row < turn, pltpu.roll(now, turn, 0), pltpu.roll(rest, turn, 0))
+            later = jnp.where(row < 7, pltpu.roll(now, frames - 1, 0), pltpu.roll(rest, 7, 0))
             dpad[i + 1, j + 1] = following[...] * (later - now)
         return carry
 
@@ -917,7 +892,7 @@
         pltpu.VMEM(grid_shape(MID), F32),
         pltpu.VMEM(grid_shape(MID), BF16),
         pltpu.VMEM(grid_shape(GATE), BF16),
-        pltpu.VMEM((cells, 16, GATE), BF16),
+        pltpu.VMEM(grid_shape(GATE), BF16),
         pltpu.VMEM((GRID + 2, GRID + 2, frames, GATE), F32),
         pltpu.VMEM(grid_shape(GATE), BF16),
         pltpu.VMEM(grid_shape(MID), BF16),
@@ -950,84 +925,298 @@
     return wholes, results[len(jobs) :]
 
 
-def norm_backward(grad_out, normed, inv_std, live_rows, rows_mask, gain):
-    part_gain = jnp.sum(grad_out * normed, axis=0)
-    part_shift = jnp.sum(grad_out, axis=0)
-    total_gain, total_shift = sum_pair(part_gain, part_shift)
-    grad_in = gain * inv_std * (grad_out - rows_mask * (total_shift + normed * total_gain) / live_rows)
-    return (grad_in, part_gain, part_shift)
-
-
-def gate_backward(d_mixed, masks):
-    present = masks[0].T[None, :, :, None]
-    following = masks[1].T[None, :, :, None]
-    slots = d_mixed.reshape(HW, masks[0].shape[1], masks[0].shape[0], GATE)
-    edge = lax.ppermute(slots[:, -1], "seg", [(i, i + 1) for i in range(lax.axis_size("seg") - 1)])
-    edge = edge.astype(F32)
-    edge = edge + grid_mean(edge)
-    wide = d_mixed.astype(F32)
-    spread = (wide + grid_mean(wide)).reshape(slots.shape)
-    earlier = jnp.concatenate([edge[:, None], spread[:, :-1]], axis=1)
-    d_part = present * earlier - following * spread
-    return d_part.astype(BF16).reshape(d_mixed.shape)
-
-
-def block_backward(d_out, x_low, kept, weights, norms, masks, live_rows):
-    w_in, w_mid, w_out, w_red, w_exp = weights
-    gains, shifts = norms
-    h_one, a_one_low, gate, mixed, gated, h_two, a_two_low, h_three, st_one, st_two, st_three = kept
-    rows_mask = masks[2]
-    frames = x_low.shape[1]
-    x_low = x_low.reshape(-1, D)
-    normed_three = (h_three.reshape(-1, D).astype(F32) - st_three[0]) * st_three[1]
-    pre = normed_three * gains[2 * MID :] + shifts[2 * MID :] + x_low.astype(F32)
-    normed_two = (h_two.reshape(-1, MID) - st_two[0]) * st_two[1]
-    y_two = normed_two * gains[MID : 2 * MID] + shifts[MID : 2 * MID]
-    normed_one = (h_one.reshape(-1, MID) - st_one[0]) * st_one[1]
-    y_one = normed_one * gains[:MID] + shifts[:MID]
-    a_one = jax.nn.silu(y_one)
-    a_one_low = a_one_low.reshape(-1, MID)
-    a_two_low = a_two_low.reshape(-1, MID)
-    gate = gate.reshape(-1, MID).astype(F32)
-    mixed_flat = mixed.reshape(-1, GATE)
-    d_pre = d_out * silu_slope(pre)
-    d_h_three, gain_three, shift_three = norm_backward(
-        d_pre, normed_three, st_three[1], live_rows, rows_mask, gains[2 * MID :]
-    )
-    d_h_three_low = d_h_three.astype(BF16)
-    g_out = matmul(a_two_low.T, d_h_three_low)
-    d_a_two = matmul(d_h_three_low, w_out.T)
-    d_y_two = d_a_two * silu_slope(y_two)
-    d_h_two, gain_two, shift_two = norm_backward(
-        d_y_two, normed_two, st_two[1], live_rows, rows_mask, gains[MID : 2 * MID]
-    )
-    d_h_two_low = d_h_two.astype(BF16).reshape(GRID, GRID, frames, MID)
-    g_mid = conv(gated, d_h_two_low, ("HWCN", "HWIO", "HWNC")).reshape(9 * MID, MID)
-    turned = jnp.flip(w_mid.reshape(3, 3, MID, MID), (0, 1))
-    d_gated = conv(d_h_two_low, turned, ("HWNC", "HWOI", "HWNC")).reshape(-1, MID)
-    d_excite = (d_gated * a_one * gate * (1.0 - gate)).astype(BF16)
-    g_exp = matmul(mixed_flat.T, d_excite)
-    d_mixed = matmul(d_excite, w_exp.T).astype(BF16).reshape(HW, frames, GATE)
-    d_reduced_flat = gate_backward(d_mixed, masks).reshape(-1, GATE)
-    g_red = matmul(a_one_low.T, d_reduced_flat)
-    d_a_one = d_gated * (1.0 + gate) + matmul(d_reduced_flat, w_red.T)
-    d_y_one = d_a_one * silu_slope(y_one)
-    d_h_one, gain_one, shift_one = norm_backward(
-        d_y_one, normed_one, st_one[1], live_rows, rows_mask, gains[:MID]
-    )
-    d_h_one_low = d_h_one.astype(BF16)
-    g_in = matmul(x_low.T, d_h_one_low)
-    d_x = d_pre + matmul(d_h_one_low, w_in.T)
-    grads = [
-        g_in,
-        g_mid,
-        g_out,
-        g_red,
-        g_exp,
-        jnp.concatenate([gain_one, gain_two, gain_three]),
-        jnp.concatenate([shift_one, shift_two, shift_three]),
+def backward_kernel(n_seg, n_clip, block, *refs):
+    refs = list(refs)
+
+    def pop(count=1):
+        taken = refs[:count]
+        del refs[:count]
+        return taken if count != 1 else taken[0]
+
+    last = block == 1
+    h3_hbm, x_hbm, d_in, h2_hbm, h1_hbm, gate_hbm = pop(6)
+    in_hbm, mid_hbm, out_hbm, small_hbm = pop(4)
+    norms, st1, st2, st3, mask, present, following = pop(7)
+    dh3_out, dh2_out, de_out, dr_out, dh1_out, dx_out, norm_grads = pop(7)
+    dv, h3v, xv, h2v, h1v, gatev, dyv, pad2, dsv, edge, pad_s, pad_e = pop(12)
+    drv, dh1v, w_in, w_mid, w_out, small, w_exp = pop(7)
+    sum_gain, sum_shift = pop(2)
+    sums = [pop(4) for _ in range(3)]
+    send_sem, recv_sem = pop(2)
+    links = Links(n_seg, n_clip, send_sem, recv_sem)
+    frames = xv.shape[1]
+    outgoing = []
+
+    def send_out(source, target):
+        copy = links.local(source, target)
+        copy.start()
+        outgoing.append(copy)
+
+    def load(source, target):
+        copy = links.local(source.reshape(target.shape), target)
+        copy.start()
+        return copy
+
+    loads_one = [load(h3_hbm, h3v), load(x_hbm, xv)]
+    if not last:
+        loads_one.append(load(d_in, dv))
+    loads_two = [load(out_hbm, w_out), load(h2_hbm, h2v)]
+    loads_three = [load(mid_hbm, w_mid), load(h1_hbm, h1v), load(gate_hbm, gatev), load(small_hbm, small)]
+    loads_four = [load(in_hbm, w_in)]
+    links.meet()
+    base = BLOCK_NORMS * block
+    live_rows = norms[98:99, 0:1]
+    half = MID // LANES
+    pad2[...] = jnp.zeros_like(pad2)
+    pad_s[...] = jnp.zeros_like(pad_s)
+    pad_e[...] = jnp.zeros_like(pad_e)
+    sum_gain[...] = jnp.zeros_like(sum_gain)
+    sum_shift[...] = jnp.zeros_like(sum_shift)
+
+    def vectors(start, columns, stats):
+        gain = row_vector(norms, base + start, columns // LANES)
+        shift = row_vector(norms, base + 24 + start, columns // LANES)
+        return gain, shift, stats[0:1, :], stats[1:2, :]
+
+    def totals(index, start, columns, gain_rows, shift_rows):
+        stat = sums[index][0]
+        put_rows(stat, 0, jnp.sum(gain_rows, axis=0, keepdims=True), 4)
+        put_rows(stat, 4, jnp.sum(shift_rows, axis=0, keepdims=True), 4)
+        tot = links.all_sum(*sums[index])
+        gain = jnp.concatenate([tot[k : k + 1] for k in range(4)], axis=1)
+        shift = jnp.concatenate([tot[4 + k : 5 + k] for k in range(4)], axis=1)
+        put_rows(norm_grads, start, gain, columns // LANES)
+        put_rows(norm_grads, 24 + start, shift, columns // LANES)
+        return gain / live_rows, shift / live_rows
+
+    def slope_of(values):
+        sig = jax.nn.sigmoid(values)
+        return sig, sig * (1.0 + values * (1.0 - sig))
+
+    def dot_t(left, right):
+        return lax.dot_general(left, right, (((1,), (1,)), ((), ())), preferred_element_type=F32)
+
+    for copy in loads_one:
+        copy.wait()
+    gain3, shift3, mean3, inv3 = vectors(2 * half, D, st3)
+
+    def first(p, carry):
+        for k in range(4):
+            span = slice(k * MID, (k + 1) * MID)
+            n = (h3v[p, :, span].astype(F32) - mean3[:, span]) * inv3[:, span]
+            pre = n * gain3[:, span] + shift3[:, span] + xv[p, :, span].astype(F32)
+            grad = d_in[:, span] if last else dv[p, :, span]
+            grad = grad * slope_of(pre)[1]
+            dv[p, :, span] = grad
+            sum_gain[:, span] += fold(grad * n)
+            sum_shift[:, span] += fold(grad)
+        return carry
+
+    lax.fori_loop(0, HW, first, 0)
+    part_gain, part_shift = totals(0, 2 * half, D, sum_gain[...], sum_shift[...])
+    factor3 = gain3 * inv3
+    for copy in loads_two:
+        copy.wait()
+    gain2, shift2, mean2, inv2 = vectors(half, MID, st2)
+    zeros = jnp.zeros((8, MID), F32)
+
+    def second(i, carry):
+        for j in range(GRID):
+            p = GRID * i + j
+            for k in range(4):
+                span = slice(k * MID, (k + 1) * MID)
+                n = (h3v[p, :, span].astype(F32) - mean3[:, span]) * inv3[:, span]
+                rest = mask[...] * (part_shift[:, span] + n * part_gain[:, span])
+                h3v[p, :, span] = (factor3[:, span] * (dv[p, :, span] - rest)).astype(BF16)
+        d_a = dot_t(h3v[pl.ds(GRID * i, GRID)].reshape(GRID * frames, D), w_out[...])
+        d_a = d_a.reshape(GRID, frames, MID)
+        one, two = carry
+        for j in range(GRID):
+            n = (h2v[GRID * i + j] - mean2) * inv2
+            grad = d_a[j] * slope_of(n * gain2 + shift2)[1]
+            dyv[GRID * i + j] = grad
+            one = one + fold(grad * n)
+            two = two + fold(grad)
+        return (one, two)
+
+    one, two = lax.fori_loop(0, GRID, second, (zeros, zeros))
+    send_out(h3v, dh3_out)
+    part_gain2, part_shift2 = totals(1, half, MID, one, two)
+    factor2 = gain2 * inv2
+
+    def third(i, carry):
+        for j in range(GRID):
+            p = GRID * i + j
+            n = (h2v[p] - mean2) * inv2
+            rest = mask[...] * (part_shift2 + n * part_gain2)
+            pad2[i + 1, j + 1] = (factor2 * (dyv[p] - rest)).astype(BF16)
+        return carry
+
+    lax.fori_loop(0, GRID, third, 0)
+    send_out(pad2.at[pl.ds(1, GRID), pl.ds(1, GRID)], dh2_out)
+    for copy in loads_three:
+        copy.wait()
+    w_exp[...] = excite_weights(small, block)
+    red = small[:, 32 * block : 32 * block + 16].reshape(MID, GATE)
+    gain1, shift1, mean1, inv1 = vectors(0, MID, st1)
+
+    def fourth(i, carry):
+        part = None
+        for k in range(9):
+            window = pad2[i + 2 - k // 3, pl.ds(2 - k % 3, GRID)].reshape(GRID * frames, MID)
+            term = dot_t(window, w_mid[k])
+            part = term if part is None else part + term
+        part = part.reshape(GRID, frames, MID)
+        for j in range(GRID):
+            p = GRID * i + j
+            y = (h1v[p] - mean1) * inv1 * gain1 + shift1
+            a = y * jax.nn.sigmoid(y)
+            gate = gatev[p].astype(F32)
+            dyv[p] = part[j] * (1.0 + gate)
+            gatev[p] = (part[j] * a * gate * (1.0 - gate)).astype(BF16)
+        d_s = dot_t(gatev[pl.ds(GRID * i, GRID)].reshape(GRID * frames, MID), w_exp[...])
+        d_s = d_s.astype(BF16).reshape(GRID, frames, GATE)
+        dsv[pl.ds(GRID * i, GRID)] = d_s
+        for j in range(GRID):
+            pad_s[i + 1, j + 1] = d_s[j].astype(F32)
+        return carry
+
+    lax.fori_loop(0, GRID, fourth, 0)
+    swap = links.remote(links.take(1), dsv, edge, links.other)
+    swap.start()
+    send_out(gatev, de_out)
+    swap.wait()
+
+    def unpack(i, carry):
+        for j in range(GRID):
+            pad_e[i + 1, j + 1] = edge[GRID * i + j].astype(F32)
+        return carry
+
+    lax.fori_loop(0, GRID, unpack, 0)
+    row = lax.rem(lax.broadcasted_iota(jnp.int32, (frames, GATE), 0), 8)
+    from_other = links.seg.astype(F32)
+
+    def fifth(i, carry):
+        for j in range(GRID):
+            near = jnp.zeros((frames, GATE), F32)
+            far = jnp.zeros((frames, GATE), F32)
+            for k in range(9):
+                near = near + pad_s[i + k // 3, j + k % 3]
+                far = far + pad_e[i + k // 3, j + k % 3]
+            near = pad_s[i + 1, j + 1] + near / 9.0
+            far = (pad_e[i + 1, j + 1] + far / 9.0) * from_other
+            earlier = jnp.where(row > 0, pltpu.roll(near, 1, 0), pltpu.roll(far, frames - 7, 0))
+            drv[GRID * i + j] = (present[...] * earlier - following[...] * near).astype(BF16)
+        d_a = dot_t(drv[pl.ds(GRID * i, GRID)].reshape(GRID * frames, GATE), red)
+        d_a = d_a.reshape(GRID, frames, MID)
+        one, two = carry
+        for j in range(GRID):
+            p = GRID * i + j
+            n = (h1v[p] - mean1) * inv1
+            grad = (dyv[p] + d_a[j]) * slope_of(n * gain1 + shift1)[1]
+            dyv[p] = grad
+            one = one + fold(grad * n)
+            two = two + fold(grad)
+        return (one, two)
+
+    one, two = lax.fori_loop(0, GRID, fifth, (zeros, zeros))
+    send_out(drv, dr_out)
+    part_gain1, part_shift1 = totals(2, 0, MID, one, two)
+    factor1 = gain1 * inv1
+    for copy in loads_four:
+        copy.wait()
+
+    def sixth(i, carry):
+        for j in range(GRID):
+            p = GRID * i + j
+            n = (h1v[p] - mean1) * inv1
+            rest = mask[...] * (part_shift1 + n * part_gain1)
+            dh1v[p] = (factor1 * (dyv[p] - rest)).astype(BF16)
+        rows = dh1v[pl.ds(GRID * i, GRID)].reshape(GRID * frames, MID)
+        for k in range(4):
+            span = slice(k * MID, (k + 1) * MID)
+            part = dot_t(rows, w_in[span, :])
+            dv[pl.ds(GRID * i, GRID), :, span] += part.reshape(GRID, frames, MID)
+        return carry
+
+    lax.fori_loop(0, GRID, sixth, 0)
+    send_out(dh1v, dh1_out)
+    send_out(dv, dx_out)
+    for copy in outgoing:
+        copy.wait()
+
+
+def backward_block(block, h3, x, d_in, h2, h1, gate, weights, norms, stats, masks):
+    n_seg = lax.axis_size("seg")
+    n_clip = lax.axis_size("clip")
+    cells, frames, width = x.shape
+    any_spec = pl.BlockSpec(memory_space=pl.ANY)
+    vmem = pl.BlockSpec(memory_space=pltpu.VMEM)
+    last = block == 1
+
+    def grid_shape(columns):
+        return (cells, frames, columns)
+
+    outs = [
+        jax.ShapeDtypeStruct(grid_shape(D), BF16),
+        jax.ShapeDtypeStruct((GRID, GRID, frames, MID), BF16),
+        jax.ShapeDtypeStruct(grid_shape(MID), BF16),
+        jax.ShapeDtypeStruct(grid_shape(GATE), BF16),
+        jax.ShapeDtypeStruct(grid_shape(MID), BF16),
+        jax.ShapeDtypeStruct(grid_shape(D), F32),
+        jax.ShapeDtypeStruct((BLOCK_NORMS, LANES), F32),
     ]
-    return (d_x, grads)
+    scratch = [
+        pltpu.VMEM(grid_shape(D), F32),
+        pltpu.VMEM(grid_shape(D), BF16),
+        pltpu.VMEM(grid_shape(D), BF16),
+        pltpu.VMEM(grid_shape(MID), F32),
+        pltpu.VMEM(grid_shape(MID), F32),
+        pltpu.VMEM(grid_shape(MID), BF16),
+        pltpu.VMEM(grid_shape(MID), F32),
+        pltpu.VMEM((GRID + 2, GRID + 2, frames, MID), BF16),
+        pltpu.VMEM(grid_shape(GATE), BF16),
+        pltpu.VMEM(grid_shape(GATE), BF16),
+        pltpu.VMEM((GRID + 2, GRID + 2, frames, GATE), F32),
+        pltpu.VMEM((GRID + 2, GRID + 2, frames, GATE), F32),
+        pltpu.VMEM(grid_shape(GATE), BF16),
+        pltpu.VMEM(grid_shape(MID), BF16),
+        pltpu.VMEM((D, MID), BF16),
+        pltpu.VMEM((9, MID, MID), BF16),
+        pltpu.VMEM((MID, D), BF16),
+        pltpu.VMEM((SMALL_SHARDS, 64, LANES), BF16),
+        pltpu.VMEM((GATE, MID), BF16),
+        pltpu.VMEM((8, D), F32),
+        pltpu.VMEM((8, D), F32),
+    ]
+    for shape in ((8, MID), (8, LANES), (8, LANES)):
+        scratch += sum_scratch(n_seg, n_clip, shape)
+    count = 3 * (n_seg * 4 + n_clip // 4) + 32
+    scratch += [pltpu.SemaphoreType.DMA((count,)), pltpu.SemaphoreType.DMA((count,))]
+    d_spec = vmem if last else any_spec
+    return pl.pallas_call(
+        functools.partial(backward_kernel, n_seg, n_clip, block),
+        out_shape=outs,
+        in_specs=[any_spec, any_spec, d_spec] + [any_spec] * 7 + [vmem] * 7,
+        out_specs=[any_spec] * 6 + [vmem],
+        scratch_shapes=scratch,
+        compiler_params=pltpu.CompilerParams(
+            collective_id=40 + block, has_side_effects=True, vmem_limit_bytes=62 * 1024 * 1024
+        ),
+        name="backward_block",
+    )(h3, x, d_in, h2, h1, gate, *weights, norms, *stats, *masks)
+
+
+def weight_gradients(x, kept, steps):
+    gated, a_low, mixed, a_two = kept
+    d_three, d_two, d_excite, d_reduced, d_one = steps
+    return [
+        matmul(x.reshape(-1, D).T, d_one.reshape(-1, MID)),
+        conv(gated, d_two, ("HWCN", "HWIO", "HWNC")).reshape(9 * MID, MID),
+        matmul(a_two.reshape(-1, MID).T, d_three.reshape(-1, D)),
+        matmul(a_low.reshape(-1, MID).T, d_reduced.reshape(-1, GATE)),
+        matmul(mixed.reshape(-1, GATE).T, d_excite.reshape(-1, MID)),
+    ]
 
 
 def on_device(inputs, clip_counts, labels, master, first_moment, second_moment):
@@ -1037,12 +1226,10 @@
     slot_ids = lax.axis_index("seg") * slot_local + jnp.arange(slot_local, dtype=jnp.int32)
     present = (slot_ids[None, :] < clip_counts[:, None]).astype(F32)
     following = (slot_ids[None, :] + 1 < clip_counts[:, None]).astype(F32)
-    rows_mask = jnp.broadcast_to(present.T.reshape(1, frames), (HW, frames)).reshape(-1, 1)
-    masks = (present, following, rows_mask)
-    frame_mask = jnp.broadcast_to(present.T.reshape(frames, 1), (frames, MID))
-    frame_following = jnp.broadcast_to(following.T.reshape(frames, 1), (frames, GATE))
+    frame_mask = jnp.broadcast_to(present.reshape(frames, 1), (frames, MID))
+    frame_following = jnp.broadcast_to(following.reshape(frames, 1), (frames, GATE))
     table = norm_table(master, HW * jnp.sum(present))
-    x_low = inputs.transpose(2, 1, 0, 3).reshape(HW, frames, D)
+    x_low = inputs.reshape(frames, HW, D).transpose(1, 0, 2)
     shards = weight_shards(master)
     if shards is None:
         weights = whole_weights(master)
@@ -1071,24 +1258,9 @@
             table = results[9]
         kept.append(results[:8] + results[10:])
         flowing = results[8]
-    live_rows = table[98, 0]
-    small = weights["small"].reshape(SMALL_SHARDS, 4, 16, LANES)
-    block_weights = []
-    for block in range(2):
-        w_exp = small[:, 2 * block + 1].reshape(SMALL_SHARDS, MID // LANES, GATE // SMALL_SHARDS, LANES)
-        block_weights.append(
-            (
-                weights["in%d" % block],
-                weights["mid%d" % block],
-                weights["out%d" % block],
-                small[:, 2 * block].reshape(MID, GATE),
-                jnp.swapaxes(w_exp, 1, 2).reshape(GATE, MID),
-            )
-        )
-    tables = [table[BLOCK_NORMS * b : BLOCK_NORMS * (b + 1)].reshape(2, -1) for b in range(2)]
     w_cls = weights["cls"][:, :CLASSES]
     b_cls = table[96:98].reshape(-1)[:CLASSES]
-    partial_value = jnp.sum(flowing.reshape(slot_local, clip_local, D), axis=0)
+    partial_value = jnp.sum(flowing.reshape(clip_local, slot_local, D), axis=1)
     pooled_sum = lax.psum(partial_value.astype(BF16), "seg").astype(F32)
     counts_float = clip_counts.astype(F32)
     pooled = pooled_sum / (HW * counts_float)[:, None]
@@ -1102,13 +1274,27 @@
     g_bias = jnp.sum(d_logits, axis=0) / seg_count
     d_pooled = matmul(d_lin, w_cls.T)
     scaled = d_pooled / (HW * counts_float)[:, None]
-    d_frame = present.T[:, :, None] * scaled[None]
-    d_flow = jnp.broadcast_to(d_frame.reshape(1, frames, D), (HW, frames, D)).reshape(-1, D)
+    d_flow = (present[:, :, None] * scaled[:, None]).reshape(frames, D)
+    masks = (frame_mask, frame_mask[:, :GATE], frame_following)
     grads = [None, None]
     for block in (1, 0):
-        d_flow, grads[block] = block_backward(
-            d_flow, flows[block], kept[block], block_weights[block], tables[block], masks, live_rows
+        h_one, a_low, gate, mixed, gated, h_two, a_two, h_three, st_one, st_two, st_three = kept[block]
+        *steps, d_flow, norm_sums = backward_block(
+            block,
+            h_three,
+            flows[block],
+            d_flow,
+            h_two,
+            h_one,
+            gate,
+            [weights[name + str(block)] for name in ("in", "mid", "out")] + [weights["small"]],
+            table,
+            (st_one, st_two, st_three),
+            masks,
         )
+        grads[block] = weight_gradients(flows[block], (gated, a_low, mixed, a_two), steps)
+        devices = seg_count * lax.axis_size("clip")
+        grads[block] += [norm_sums[:24].reshape(-1) / devices, norm_sums[24:].reshape(-1) / devices]
     grad_mine = scatter_gradients(grads[0] + grads[1] + [g_cls, g_bias])
     tail = jnp.concatenate(
         [
@@ -1128,7 +1314,7 @@
     new_master = master - LEARN_RATE * (
         first_hat / (jnp.sqrt(second_hat) + ADAM_EPS) + WEIGHT_DECAY * master
     )
-    grid_grad = d_flow.reshape(HW, slot_local, clip_local, D).transpose(2, 1, 0, 3)
+    grid_grad = d_flow.transpose(1, 0, 2).reshape(inputs.shape)
     return (
         new_master,
         new_first,

time: 841 us -> 646 us (0.77)
  other arithmetic: 109 us -> 9.96 us
  local copies, waits for them, and re-layouts: 142 us -> 53.8 us
  matrix products: 144 us -> 57.9 us
  Pallas kernels: 424 us -> 508 us
    pallas_call x0 -> x2, Pallas kernels: none -> 146 us  [backward_block(): pl.pallas_call(functools.partial(backward_kernel, n_seg, n_clip, block),...]
    dot_general x19 -> x11, matrix products: 101 us -> 37.1 us  [matmul(): return jnp.dot(left, right, preferred_element_type=F32)]
    pallas_call x7 -> x1, Pallas kernels: 71.2 us -> 9.63 us  [small_sum(): pl.pallas_call(functools.partial(small_sum_kernel, n_seg, n_clip, inner),...]
    convert_element_type x8 -> x0, other arithmetic: 45.7 us -> none  [the longest x2 25.4 us: block_backward(): d_h_three_low = d_h_three.astype(BF16)]
    reshape x4 -> x0, local copies, waits for them, and re-layouts: 44.6 us -> none  [the longest x2 32.4 us: on_device(): d_flow.reshape(HW, slot_local, clip_local, D).transpose(2, 1, 0, 3)]
    conv_general_dilated x4 -> x2, matrix products: 43.2 us -> 20.8 us  [conv(): lax.conv_general_dilated(values, kernel, (1, 1), ((1, 1), (1, 1)), dimens...]
    mul x13 -> x1, other arithmetic: 19.4 us -> 0.81 us  [on_device(): d_flow = (present[:, :, None] * scaled[:, None]).reshape(frames, D)]
    another operation x2 -> x1, local copies, waits for them, and re-layouts: 13.4 us -> 0.51 us  [the longest x1 11.1 us: block_backward(): x_low = x_low.reshape(-1, D)]
  transfers between devices with their start and end apart: 2 -> 0, of which waited for: 0 -> 0; matrix products, arithmetic and copies ran while one was open for 10% -> 0% of each run, Pallas kernels for 0% -> 0%
where the time goes in v3:
time: 646 us; the launch traced here: 637 us
  Pallas kernels  508 us (79%)
  matrix products  57.9 us (9%)
  local copies, waits for them, and re-layouts  53.8 us (8%)
  other arithmetic  9.96 us (2%)
    pallas_call x2, Pallas kernels, forward_block(): pl.pallas_call(functools.partial(forward_kernel, n_seg, n_clip, block, jo...  211 us
    pallas_call x2, Pallas kernels, backward_block(): pl.pallas_call(functools.partial(backward_kernel, n_seg, n_clip, block),...  146 us
    pallas_call x1, Pallas kernels, reduce_scatter(): pl.pallas_call(functools.partial(scatter_kernel, n_clip, n_jobs), out_sha...  142 us
    dot_general x11, matrix products, matmul(): return jnp.dot(left, right, preferred_element_type=F32)  37.1 us
    unnamed x57, local copies, waits for them, and re-layouts  24.7 us
    conv_general_dilated x2, matrix products, conv(): lax.conv_general_dilated(values, kernel, (1, 1), ((1, 1), (1, 1)), dimens...  20.8 us

profile of v3, /device:TPU:0, one launch (start us, length us, event | category | flops | bytes accessed | tf_op | source)
XLA Modules:
  0.0 637.3 jit_solution(6681960613377469395)
XLA Ops:
  0.7 6.8 %copy.80 = bf16[4,8,49,2048]{3,1,0,2:T(8,128)(2,1)} copy(bf16[4,8,49,2048]{3,1,2,0:T(8,128)(2,1)} %param.6) | data formatting | bytes 12845056 | tf_op args[0]
  7.9 0.7 broadcast_in_dim.15.refs_1_.refs_14_
  8.6 0.7 broadcast_in_dim.16.refs_2_.refs_16_
  9.8 0.7 convert_reduce_fusion
  11.2 0.7 maximum_maximum_fusion.refs_3_
  11.9 0.1 fusion.27
  12.0 0.7 reshape.337.refs_4_
  12.8 0.6 pad_maximum_fusion.refs_5_
  13.4 0.1 fusion.28
  13.6 0.8 reshape.342.refs_6_
  14.3 0.7 reshape.343.refs_7_
  15.0 0.7 reshape.344.refs_8_
  15.7 116.0 %forward_block.2 = (bf16[2048,512]{1,0:T(8,128)(2,1)}, bf16[2048,128]{1,0:T(8,128)(2,1)}, bf16[4608,512]{1,0:T(8,128)(2,1)}, bf16[512,2048]{1,0:T(8,128)(2,1)}, ...) custom-call(bf16[49,32,2048]{2,1,0:T(8,128)(2,1)} %bitcast.134, ...), custom_call_target="tpu_custom_call" | custom-call | tf_op jit(solution)/shard_map/forward_block/pallas_call | solution.py:913
  131.6 0.8 reshape.345.refs_4_
  132.4 0.7 reshape.346.refs_5_
  133.1 0.2 reshape.347
  133.3 0.6 pad.27.refs_6_
  133.9 95.1 %forward_block.3 = (bf16[4608,512]{1,0:T(8,128)(2,1)}, bf16[512,2048]{1,0:T(8,128)(2,1)}, bf16[2048,256]{1,0:T(8,128)(2,1)}, f32[49,32,512]{2,1,0:T(8,128)}, bf1...) custom-call(bf16[49,32,2048]{2,1,0:T(8,128)(2,1)} %get-tuple-element, ...), custom_call_target="tpu_custom_call" | custom-call | tf_op jit(solution)/shard_map/forward_block/pallas_call | solution.py:913
  229.0 0.8 slice_bitcast_fusion.6
  229.8 1.0 bitcast_reduce_fusion
  230.8 3.4 psum.7
  234.2 1.6 fusion.29
  235.8 0.2 fusion.15
  236.0 0.4 convolution_divide_fusion
  236.4 0.8 bitcast_multiply_fusion.refs_2_
  237.2 0.7 slice.142.refs_15_
  237.9 70.4 %backward_block.2 = (bf16[49,32,2048]{2,1,0:T(8,128)(2,1)}, bf16[7,7,32,512]{3,2,1,0:T(8,128)(2,1)}, bf16[49,32,512]{2,1,0:T(8,128)(2,1)}, bf16[49,32,128]{2,1,0...) custom-call(bf16[49,32,2048]{2,1,0:T(8,128)(2,1)} %get-tuple-element.67.refs_0_, ...), custom_call_target="tpu_custom_call" | custom-call | tf_op jit(solution)/shard_map/backward_block/pallas_call | solution.py:1197
  308.3 8.8 %bitcast_convert_fusion.3 = bf16[512,2048]{1,0:T(8,128)(2,1)} fusion(bf16[49,32,512]{2,1,0:T(8,128)(2,1)} %get-tuple-element.66, bf16[49,32,2048]{2,1,0:T(8,128)(2,1)} %get-tuple-element.78), kind=kOutput, calls=%fused_computation.4 | convolution fusion | flops 3289382912 | bytes 10125312 | tf_op jit(solution)/shard_map/dot_general | solution.py:35
  317.1 10.4 %convolution_convert_fusion.1 = bf16[3,3,512,512]{3,2,1,0:T(8,128)(2,1)} fusion(bf16[7,7,32,512]{3,2,1,0:T(8,128)(2,1)S(1)} %copy-done.13, bf16[7,7,32,512]{3,2,1,0:T(8,128)(2,1)S(1)} %copy-done.17), kind=kOutput, calls=%fused_computation.6 | convolution fusion | flops 6058934272 | bytes 7929856 | tf_op jit(solution)/shard_map/conv_general_dilated | solution.py:429
  327.5 5.4 bitcast_convert_fusion.2
  333.0 75.3 %backward_block.3 = (bf16[49,32,2048]{2,1,0:T(8,128)(2,1)}, bf16[7,7,32,512]{3,2,1,0:T(8,128)(2,1)}, bf16[49,32,512]{2,1,0:T(8,128)(2,1)}, bf16[49,32,128]{2,1,0...) custom-call(bf16[49,32,2048]{2,1,0:T(8,128)(2,1)} %get-tuple-element.83.refs_0_, ...), custom_call_target="tpu_custom_call" | custom-call | tf_op jit(solution)/shard_map/backward_block/pallas_call | solution.py:1197
  408.3 8.8 %bitcast_convert_fusion.1 = bf16[512,2048]{1,0:T(8,128)(2,1)} fusion(bf16[49,32,512]{2,1,0:T(8,128)(2,1)} %get-tuple-element.82, bf16[49,32,2048]{2,1,0:T(8,128)(2,1)} %get-tuple-element.94), kind=kOutput, calls=%fused_computation.2 | convolution fusion | flops 3289382912 | bytes 10125312 | tf_op jit(solution)/shard_map/dot_general | solution.py:35
  417.1 10.4 %convolution_convert_fusion = bf16[3,3,512,512]{3,2,1,0:T(8,128)(2,1)} fusion(bf16[7,7,32,512]{3,2,1,0:T(8,128)(2,1)S(1)} %copy-done.12, bf16[7,7,32,512]{3,2,1,0:T(8,128)(2,1)S(1)} %copy-done.15), kind=kOutput, calls=%fused_computation.5 | convolution fusion | flops 6058934272 | bytes 7929856 | tf_op jit(solution)/shard_map/conv_general_dilated | solution.py:429
  427.5 4.2 fusion
  431.8 2.8 copy.43
  434.5 2.3 fusion.5
  436.9 1.4 fusion.6
  438.6 2.3 fusion.7
  441.0 1.4 fusion.8
  442.7 0.4 concatenate.31
  443.2 0.9 copy.70
  444.2 0.6 broadcast_multiply_fusion
  444.9 0.5 fusion.1
  445.4 0.5 copy.52
  445.9 1.2 reshape.354
  447.1 1.0 copy.71
  448.1 141.7 %reduce_scatter.1 = (f32[16,2048]{1,0:T(8,128)}, f32[144,512]{1,0:T(8,128)}, f32[64,512]{1,0:T(8,128)}, f32[16,2048]{1,0:T(8,128)}, f32[144,512]{1,0:T(8,128)}, ...) custom-call(bf16[2,4,4,16,2048]{4,3,2,1,0:T(8,128)(2,1)} %bitcast.146, ...), custom_call_target="tpu_custom_call" | custom-call | tf_op jit(solution)/shard_map/reduce_scatter/pallas_call | solution.py:246
  589.9 1.0 copy.72
  590.9 1.0 copy.73
  591.9 0.9 copy.74
  592.9 1.3 slice_bitcast_fusion.1
  594.2 0.7 slice.176
  594.9 0.9 copy.75
  595.9 0.7 slice.177
  596.6 0.5 slice.178
  597.2 7.6 %concatenate.33 = f32[298246]{0:T(1024)S(1)} concatenate(f32[32768]{0:T(1024)S(1)} %bitcast.151, f32[73728]{0:T(1024)S(1)} %bitcast.149, f32[32768]{0:T(1024)S(1)} %bitcast.152, f32[2048]{0:T(1024)} %get-tuple-element.150, f32[2048]{0:T(1024)} %get-tuple-element.149, f32[192]{0:T(256)S(1)} %slice.176, f32[32768]{0:T(1024)S(1)} %bitcast.153, f32[73728]{0:T(1024)S(1)} %bitcast.150, ...), dimensions={0} | concatenate | bytes 2385968 | tf_op jit(solution)/shard_map/concatenate | solution.py:357
  604.7 0.7 pad_bitcast_fusion.1
  605.4 0.9 multiply_reduce_fusion
  606.3 1.2 concatenate.34.x_ref
  607.6 9.6 %small_sum.1 = f32[16,128]{1,0:T(8,128)} custom-call(f32[16,128]{1,0:T(8,128)} %concatenate.34.x_ref), custom_call_target="tpu_custom_call" | custom-call | tf_op jit(solution)/shard_map/small_sum/pallas_call | solution.py:111
  617.2 1.2 slice.156
  619.1 4.2 fusion.25
  623.3 11.8 %copy.53 = f32[4,8,49,2048]{3,1,2,0:T(8,128)} copy(f32[4,8,49,2048]{3,1,0,2:T(8,128)} %bitcast.138) | data formatting | bytes 25690112
  635.1 0.6 slice.158
  (95 shorter events, 2.2 us)
Async XLA Ops:
  0.6 8.7 %copy-start = (f32[298246]{0:T(1024)S(1)}, f32[298246]{0:T(1024)}, u32[]{:S(2)}) copy-start(f32[298246]{0:T(1024)} %param.9) | copy-start | bytes 3578956
  0.6 6.9 %copy-start.10 = (s32[4]{0:T(128)S(1)}, s32[4]{0:T(128)}, u32[]{:S(2)}) copy-start(s32[4]{0:T(128)} %param.7) | copy-start | bytes 52
  229.0 7.0 %copy-start.11 = (s32[4]{0:T(128)S(1)}, s32[4]{0:T(128)}, u32[]{:S(2)}) copy-start(s32[4]{0:T(128)} %param.8) | copy-start | bytes 52
  229.0 7.0 %copy-start.18 = (bf16[2048,256]{1,0:T(8,128)(2,1)S(1)}, bf16[2048,256]{1,0:T(8,128)(2,1)}, u32[]{:S(2)}) copy-start(bf16[2048,256]{1,0:T(8,128)(2,1)} %get-tuple-element.69) | copy-start | bytes 3145732
  308.2 8.8 %copy-start.13 = (bf16[7,7,32,512]{3,2,1,0:T(8,128)(2,1)S(1)}, bf16[7,7,32,512]{3,2,1,0:T(8,128)(2,1)}, u32[]{:S(2)}) copy-start(bf16[7,7,32,512]{3,2,1,0:T(8,128)(2,1)} %get-tuple-element.79) | copy-start | bytes 4816900
  308.2 8.8 %copy-start.17 = (bf16[7,7,32,512]{3,2,1,0:T(8,128)(2,1)S(1)}, bf16[7,7,32,512]{3,2,1,0:T(8,128)(2,1)}, u32[]{:S(2)}) copy-start(bf16[7,7,32,512]{3,2,1,0:T(8,128)(2,1)} %get-tuple-element.80) | copy-start | bytes 4816900
  308.2 19.3 %slice-start = ((s8[6422528]{0:T(1024)(128)(4,1)}), s8[4194304]{0:T(1024)(128)(4,1)S(1)}, s32[]{:S(2)}) async-start(s8[6422528]{0:T(1024)(128)(4,1)} %bitcast.136), calls=%async_computation | async-start | bytes 8388608
  317.1 10.5 %slice-start.1 = ((s8[6422528]{0:T(1024)(128)(4,1)}), s8[2228224]{0:T(1024)(128)(4,1)S(1)}, s32[]{:S(2)}) async-start(s8[6422528]{0:T(1024)(128)(4,1)} %bitcast.136), calls=%async_computation.1 | async-start | bytes 4456448
  317.1 10.5 %copy-start.16 = (bf16[49,32,512]{2,1,0:T(8,128)(2,1)S(1)}, bf16[49,32,512]{2,1,0:T(8,128)(2,1)}, u32[]{:S(2)}) copy-start(bf16[49,32,512]{2,1,0:T(8,128)(2,1)} %get-tuple-element.81) | copy-start | bytes 4816900
  408.3 8.8 %copy-start.12 = (bf16[7,7,32,512]{3,2,1,0:T(8,128)(2,1)S(1)}, bf16[7,7,32,512]{3,2,1,0:T(8,128)(2,1)}, u32[]{:S(2)}) copy-start(bf16[7,7,32,512]{3,2,1,0:T(8,128)(2,1)} %get-tuple-element.95) | copy-start | bytes 4816900
  408.3 8.8 %copy-start.15 = (bf16[7,7,32,512]{3,2,1,0:T(8,128)(2,1)S(1)}, bf16[7,7,32,512]{3,2,1,0:T(8,128)(2,1)}, u32[]{:S(2)}) copy-start(bf16[7,7,32,512]{3,2,1,0:T(8,128)(2,1)} %get-tuple-element.96) | copy-start | bytes 4816900
  408.3 19.2 %slice-start.2 = ((s8[6422528]{0:T(1024)(128)(4,1)}), s8[4194304]{0:T(1024)(128)(4,1)S(1)}, s32[]{:S(2)}) async-start(s8[6422528]{0:T(1024)(128)(4,1)} %bitcast.140), calls=%async_computation.2 | async-start | bytes 8388608
  417.1 10.4 %slice-start.3 = ((s8[6422528]{0:T(1024)(128)(4,1)}), s8[2228224]{0:T(1024)(128)(4,1)S(1)}, s32[]{:S(2)}) async-start(s8[6422528]{0:T(1024)(128)(4,1)} %bitcast.140), calls=%async_computation.3 | async-start | bytes 4456448
  417.1 10.4 %copy-start.14 = (bf16[49,32,512]{2,1,0:T(8,128)(2,1)S(1)}, bf16[49,32,512]{2,1,0:T(8,128)(2,1)}, u32[]{:S(2)}) copy-start(bf16[49,32,512]{2,1,0:T(8,128)(2,1)} %get-tuple-element.97) | copy-start | bytes 4816900
  434.5 2.3 copy-start.2
  436.8 1.6 copy-start.8
  438.6 2.4 copy-start.1
  440.9 1.6 copy-start.7
  589.8 6.0 copy-start.3
  589.9 6.0 copy-start.4
  589.9 6.1 copy-start.6
  589.9 6.8 %copy-start.5 = (f32[96,128]{1,0:T(8,128)S(1)}, f32[96,128]{1,0:T(8,128)}, u32[]{:S(2)}) copy-start(f32[96,128]{1,0:T(8,128)} %get-tuple-element.115) | copy-start | bytes 147460
  623.3 11.8 %copy-start.9 = (f32[16,128]{1,0:T(8,128)S(1)}, f32[16,128]{1,0:T(8,128)}, u32[]{:S(2)}) copy-start(f32[16,128]{1,0:T(8,128)} %small_sum.1) | copy-start | bytes 24580

commit v4 on v3

--- a/solution.py
+++ b/solution.py
@@ -33,231 +33,6 @@
 
 def matmul(left, right):
     return jnp.dot(left, right, preferred_element_type=F32)
-
-
-def small_sum_kernel(n_seg, n_clip, inner, x_ref, o_ref, mid, near, far, send_sem, recv_sem):
-    seg = lax.axis_index("seg")
-    clip = lax.axis_index("clip")
-    outer = n_clip // inner
-    group = clip // inner
-    place = lax.rem(clip, inner)
-    n_near = n_seg * inner - 1
-    n_far = outer - 1
-
-    def near_peer(i):
-        return (
-            lax.rem(seg + i // inner, n_seg),
-            group * inner + lax.rem(place + lax.rem(i, inner), inner),
-        )
-
-    def far_peer(i):
-        return (seg, lax.rem(group + i, outer) * inner + place)
-
-    def copy_near(i):
-        return pltpu.make_async_remote_copy(
-            src_ref=x_ref,
-            dst_ref=near.at[i - 1],
-            send_sem=send_sem.at[i - 1],
-            recv_sem=recv_sem.at[i - 1],
-            device_id=near_peer(i),
-            device_id_type=MESH_ID,
-        )
-
-    def copy_far(i):
-        return pltpu.make_async_remote_copy(
-            src_ref=mid,
-            dst_ref=far.at[i - 1],
-            send_sem=send_sem.at[n_near + i - 1],
-            recv_sem=recv_sem.at[n_near + i - 1],
-            device_id=far_peer(i),
-            device_id_type=MESH_ID,
-        )
-
-    def repeat(first, last, action):
-        if last - first <= 8:
-            for i in range(first, last):
-                action(i)
-        else:
-
-            def body(i, carry):
-                action(i)
-                return carry
-
-            lax.fori_loop(first, last, body, 0)
-
-    barrier = pltpu.get_barrier_semaphore()
-
-    def greet(peer):
-        pl.semaphore_signal(barrier, inc=1, device_id=peer, device_id_type=MESH_ID)
-
-    repeat(1, n_near + 1, lambda i: greet(near_peer(i)))
-    repeat(1, n_far + 1, lambda i: greet(far_peer(i)))
-    pl.semaphore_wait(barrier, n_near + n_far)
-    repeat(1, n_near + 1, lambda i: copy_near(i).start())
-    repeat(1, n_near + 1, lambda i: copy_near(i).wait())
-    mid[...] = x_ref[...] + jnp.sum(near[...], axis=0)
-    repeat(1, n_far + 1, lambda i: copy_far(i).start())
-    repeat(1, n_far + 1, lambda i: copy_far(i).wait())
-    o_ref[...] = mid[...] + jnp.sum(far[...], axis=0)
-
-
-def small_sum(values):
-    n_seg = lax.axis_size("seg")
-    n_clip = lax.axis_size("clip")
-    inner = 4 if n_clip % 4 == 0 else 1
-    n_near = n_seg * inner - 1
-    n_far = n_clip // inner - 1
-    rows = values.shape[0]
-    return pl.pallas_call(
-        functools.partial(small_sum_kernel, n_seg, n_clip, inner),
-        out_shape=jax.ShapeDtypeStruct(values.shape, F32),
-        in_specs=[pl.BlockSpec(memory_space=pltpu.VMEM)],
-        out_specs=pl.BlockSpec(memory_space=pltpu.VMEM),
-        scratch_shapes=[
-            pltpu.VMEM(values.shape, F32),
-            pltpu.VMEM((n_near,) + values.shape, F32),
-            pltpu.VMEM((n_far,) + values.shape, F32),
-            pltpu.SemaphoreType.DMA((n_near + n_far,)),
-            pltpu.SemaphoreType.DMA((n_near + n_far,)),
-        ],
-        compiler_params=pltpu.CompilerParams(collective_id=rows // 8, has_side_effects=True),
-        name="small_sum",
-    )(values)
-
-
-def scatter_kernel(n_clip, n_jobs, *refs):
-    grads = refs[:n_jobs]
-    outs = refs[n_jobs : 2 * n_jobs]
-    ones = refs[2 * n_jobs : 3 * n_jobs]
-    twos = refs[3 * n_jobs : 4 * n_jobs]
-    threes = refs[4 * n_jobs : 5 * n_jobs]
-    fours = refs[5 * n_jobs : 6 * n_jobs]
-    send_sem, recv_sem = refs[6 * n_jobs :]
-    seg = lax.axis_index("seg")
-    clip = lax.axis_index("clip")
-    depth = n_clip // 4
-    z = clip // 4
-    y = lax.rem(clip // 2, 2)
-    x = lax.rem(clip, 2)
-    first = (1 - seg) * y + seg * x
-    second = (1 - seg) * x + seg * y
-    step = 1 + seg
-    jump = 2 - seg
-    across_first = (seg, clip + jump * (1 - 2 * first))
-    across_second = (seg, clip + step * (1 - 2 * second))
-    other = (1 - seg, clip)
-    per_job = 1 + 2 + 1 + (depth - 1)
-
-    def along(i):
-        return (seg, lax.rem(z + i, depth) * 4 + y * 2 + x)
-
-    barrier = pltpu.get_barrier_semaphore()
-    for peer in [other, across_first, across_second] + [along(i) for i in range(1, depth)]:
-        pl.semaphore_signal(barrier, inc=1, device_id=peer, device_id_type=MESH_ID)
-    pl.semaphore_wait(barrier, depth + 2)
-
-    def remote(job, number, source, target, peer):
-        index = job * per_job + number
-        return pltpu.make_async_remote_copy(
-            src_ref=source,
-            dst_ref=target,
-            send_sem=send_sem.at[index],
-            recv_sem=recv_sem.at[index],
-            device_id=peer,
-            device_id_type=MESH_ID,
-        )
-
-    def core_copy(job):
-        return remote(job, 0, grads[job].at[1 - seg], ones[job], other)
-
-    def first_copy(job, k):
-        source = ones[job].at[:, jump * (1 - first) + step * k]
-        return remote(job, 1 + k, source, twos[job].at[:, k], across_first)
-
-    def second_copy(job):
-        return remote(job, 3, twos[job].at[:, 1 - second], threes[job], across_second)
-
-    def line_copy(job, i):
-        source = threes[job].at[lax.rem(z + i, depth)]
-        return remote(job, 3 + i, source, fours[job].at[i - 1], along(i))
-
-    for job in range(n_jobs):
-        core_copy(job).start()
-    for job in range(n_jobs):
-        core_copy(job).wait()
-        one = ones[job]
-
-        def add_one(i, carry, job=job, one=one):
-            zz = i // 4
-            w = lax.rem(i, 4)
-            total = one[zz, w].astype(F32) + grads[job][seg, zz, w].astype(F32)
-            one[zz, w] = total.astype(BF16)
-            return carry
-
-        lax.fori_loop(0, 4 * depth, add_one, 0)
-        for k in range(2):
-            first_copy(job, k).start()
-    for job in range(n_jobs):
-        for k in range(2):
-            first_copy(job, k).wait()
-        one, two = ones[job], twos[job]
-
-        def add_two(i, carry, one=one, two=two):
-            zz = i // 2
-            k = lax.rem(i, 2)
-            total = two[zz, k].astype(F32) + one[zz, jump * first + step * k].astype(F32)
-            two[zz, k] = total.astype(BF16)
-            return carry
-
-        lax.fori_loop(0, 2 * depth, add_two, 0)
-        second_copy(job).start()
-    for job in range(n_jobs):
-        second_copy(job).wait()
-        two, three = twos[job], threes[job]
-
-        def add_three(zz, carry, two=two, three=three):
-            three[zz] = (three[zz].astype(F32) + two[zz, second].astype(F32)).astype(BF16)
-            return carry
-
-        lax.fori_loop(0, depth, add_three, 0)
-        for i in range(1, depth):
-            line_copy(job, i).start()
-    for job in range(n_jobs):
-        for i in range(1, depth):
-            line_copy(job, i).wait()
-        total = threes[job][z].astype(F32)
-        for i in range(1, depth):
-            total = total + fours[job][i - 1].astype(F32)
-        outs[job][...] = total
-
-
-def reduce_scatter(grads):
-    n_seg = lax.axis_size("seg")
-    n_clip = lax.axis_size("clip")
-    fits = n_seg == 2 and n_clip == 16 and all(g.shape[1] % 16 == 0 for g in grads)
-    if not fits:
-        return [lax.psum_scatter(g, AXES, scatter_dimension=0, tiled=True)[0].astype(F32) for g in grads]
-    depth = n_clip // 4
-    n_jobs = len(grads)
-    sizes = [g.shape[1:] for g in grads]
-    shaped = [g.reshape((n_seg, depth, 4) + s) for g, s in zip(grads, sizes)]
-    vmem = pl.BlockSpec(memory_space=pltpu.VMEM)
-    copies = n_jobs * (depth + 3)
-    return pl.pallas_call(
-        functools.partial(scatter_kernel, n_clip, n_jobs),
-        out_shape=[jax.ShapeDtypeStruct(s, F32) for s in sizes],
-        in_specs=[vmem] * n_jobs,
-        out_specs=[vmem] * n_jobs,
-        scratch_shapes=[pltpu.VMEM((depth, 4) + s, BF16) for s in sizes]
-        + [pltpu.VMEM((depth, 2) + s, BF16) for s in sizes]
-        + [pltpu.VMEM((depth,) + s, BF16) for s in sizes]
-        + [pltpu.VMEM((depth - 1,) + s, BF16) for s in sizes]
-        + [pltpu.SemaphoreType.DMA((copies,)), pltpu.SemaphoreType.DMA((copies,))],
-        compiler_params=pltpu.CompilerParams(
-            collective_id=20, has_side_effects=True, vmem_limit_bytes=60 * 1024 * 1024
-        ),
-        name="reduce_scatter",
-    )(*shaped)
 
 
 def layout():
@@ -324,39 +99,6 @@
     return [pieces[i] for i in range(16)]
 
 
-def scatter_gradients(grads):
-    devices = lax.axis_size("seg") * lax.axis_size("clip")
-    wide = widths(devices)
-    rows, rows_cls = small_rows(devices)
-
-    def shards(i):
-        flat = grads[i].reshape(-1)
-        return jnp.pad(flat, (0, devices * wide[i] - flat.shape[0])).reshape(devices, wide[i])
-
-    def pack(ids, n_rows):
-        packed = jnp.concatenate([shards(i) for i in ids], axis=1).astype(BF16)
-        return jnp.pad(packed, ((0, 0), (0, n_rows * LANES - packed.shape[1]))).reshape(devices, n_rows, LANES)
-
-    smalls = (3, 4, 5, 6, 10, 11, 12, 13)
-    jobs = []
-    for base in (7, 0):
-        for i in (2, 1, 0):
-            columns = grads[base + i].shape[-1]
-            jobs.append(grads[base + i].astype(BF16).reshape(devices, -1, columns))
-    jobs.append(pack(smalls, rows))
-    jobs.append(pack((14, 15), rows_cls))
-    sums = reduce_scatter(jobs)
-    mine = {}
-    for k, i in enumerate((9, 8, 7, 2, 1, 0)):
-        mine[i] = sums[k].reshape(-1)
-    for ids, flat in ((smalls, sums[6].reshape(-1)), ((14, 15), sums[7].reshape(-1))):
-        offset = 0
-        for i in ids:
-            mine[i] = flat[offset : offset + wide[i]]
-            offset += wide[i]
-    return jnp.concatenate([mine[i] for i in range(16)])
-
-
 def part_of(master, index):
     devices = lax.axis_size("seg") * lax.axis_size("clip")
     wide = widths(devices)
@@ -364,22 +106,9 @@
     return master[start : start + wide[index]]
 
 
-def norm_table(master, live_part):
-    devices = lax.axis_size("seg") * lax.axis_size("clip")
-    me = lax.axis_index(AXES)
-    width = 2 * MID + D
-
-    def spread(indices, amount):
-        parts = jnp.stack([part_of(master, i) for i in indices]).astype(BF16).astype(F32)
-        table = jnp.zeros((len(indices), devices, parts.shape[1]), F32)
-        table = lax.dynamic_update_slice(table, parts[:, None, :], (0, me, 0))
-        return table.reshape(len(indices), -1)[:, :amount]
-
-    norms = spread((5, 6, 12, 13), width).reshape(-1, LANES)
-    bias = spread((15,), CLASSES)
-    bias = jnp.pad(bias.reshape(-1), (0, 2 * LANES - CLASSES)).reshape(2, LANES)
-    live = jnp.full((NORM_ROWS - norms.shape[0] - 2, LANES), live_part, F32)
-    return jnp.concatenate([norms, bias, live])
+def norm_rows(vectors):
+    rows = jnp.stack([jnp.pad(v, ((0, 0), (0, LANES - v.shape[1]))) for v in vectors], axis=1)
+    return jnp.pad(rows, ((0, 0), (0, 16 - rows.shape[1]), (0, 0)))
 
 
 def lanes_first(values):
@@ -387,6 +116,20 @@
     rows, columns = values.shape[-2:]
     split = values.reshape(lead + (rows, columns // LANES, LANES))
     return jnp.swapaxes(split, -3, -2).reshape(lead + (-1, LANES))
+
+
+def split_rows(target, kind, block, pieces, rows):
+    size = rows.shape[1] // pieces
+    for k, name in enumerate(piece_names(kind, block, pieces)):
+        target[name] = rows[:, k * size : (k + 1) * size].reshape(-1, MID)
+
+
+def piece_names(kind, block, pieces):
+    return [kind + "abc"[k] + str(block) for k in range(pieces)]
+
+
+def weight_names(block):
+    return piece_names("in", block, 2) + piece_names("mid", block, 3) + ["out%d" % block, "small"]
 
 
 def weight_shards(master):
@@ -398,11 +141,12 @@
     small = []
     for block in range(2):
         base = 7 * block
-        shards["in%d" % block] = part_of(low, base).reshape(-1, MID)
-        shards["mid%d" % block] = part_of(low, base + 1).reshape(-1, MID)
+        split_rows(shards, "in", block, 2, part_of(low, base).reshape(1, -1, MID))
+        split_rows(shards, "mid", block, 3, part_of(low, base + 1).reshape(1, -1, MID))
         shards["out%d" % block] = part_of(low, base + 2).reshape(-1, D)
         small.append(part_of(low, base + 3).reshape(-1, GATE))
         small.append(lanes_first(part_of(low, base + 4).reshape(-1, MID)))
+    small.append(norm_rows([part_of(low, i)[None] for i in (5, 6, 12, 13, 15)])[0])
     shards["small"] = jnp.concatenate(small)
     cls = part_of(low, 14).reshape(-1, CLASSES)
     shards["cls"] = jnp.pad(cls, ((0, 0), (0, 2 * LANES - CLASSES)))
@@ -415,14 +159,28 @@
     small = []
     for block in range(2):
         w_in, w_mid, w_out, w_red, w_exp = pieces[7 * block : 7 * block + 5]
-        whole["in%d" % block] = w_in
-        whole["mid%d" % block] = w_mid.reshape(9 * MID, MID)
+        split_rows(whole, "in", block, 2, w_in.reshape(SMALL_SHARDS, -1, MID))
+        split_rows(whole, "mid", block, 3, w_mid.reshape(SMALL_SHARDS, -1, MID))
         whole["out%d" % block] = w_out
         small.append(w_red.reshape(SMALL_SHARDS, -1, GATE))
         small.append(lanes_first(w_exp.reshape(SMALL_SHARDS, -1, MID)))
+    vectors = [pieces[i].reshape(SMALL_SHARDS, -1) for i in (5, 6, 12, 13)]
+    bias = jnp.pad(pieces[15], (0, 6 * SMALL_SHARDS - CLASSES)).reshape(SMALL_SHARDS, 6)
+    small.append(norm_rows(vectors + [bias]))
     whole["small"] = jnp.concatenate(small, axis=1).reshape(-1, LANES)
     whole["cls"] = jnp.pad(pieces[14], ((0, 0), (0, 2 * LANES - CLASSES)))
     return whole
+
+
+def scatter_gradients(grads):
+    devices = lax.axis_size("seg") * lax.axis_size("clip")
+    wide = widths(devices)
+    columns = []
+    for values, width in zip(grads, wide):
+        flat = values.reshape(-1)
+        columns.append(jnp.pad(flat, (0, devices * width - flat.shape[0])).reshape(devices, width))
+    packed = jnp.concatenate(columns, axis=1)
+    return lax.psum_scatter(packed, AXES, scatter_dimension=0, tiled=True)[0]
 
 
 def conv(values, kernel, numbers):
@@ -493,7 +251,7 @@
         repeat(1, n_far + 1, lambda i: greet(self.far_peer(i)))
         pl.semaphore_wait(barrier, n_near + n_far)
 
-    def all_sum(self, source, middle, near, far):
+    def all_sum(self, source, middle, near, far, between=lambda: None):
         n_near = self.n_seg * 4 - 1
         n_far = self.outer - 1
         base = self.take(n_near + n_far)
@@ -508,6 +266,7 @@
         repeat(1, n_near + 1, lambda i: close(i).wait())
         middle[...] = source[...] + jnp.sum(near[...], axis=0)
         repeat(1, n_far + 1, lambda i: distant(i).start())
+        between()
         repeat(1, n_far + 1, lambda i: distant(i).wait())
         return middle[...] + jnp.sum(far[...], axis=0)
 
@@ -581,8 +340,20 @@
             self.advance()
 
 
-def row_vector(table, start, count):
-    return jnp.concatenate([table[start + k : start + k + 1, :] for k in range(count)], axis=1)
+def row_vector(table, row, start, count):
+    return jnp.concatenate([table[start + k, row : row + 1, :] for k in range(count)], axis=1)
+
+
+def build_table(small, table):
+    lane = lax.broadcasted_iota(jnp.int32, (8, LANES), 1)
+    for q in range(SMALL_SHARDS // 4):
+        rows = [small[4 * q + j, 64:80, :].astype(F32)[:8] for j in range(4)]
+        one = pltpu.roll(rows[1], 96, 1)
+        two = pltpu.roll(rows[2], 64, 1)
+        three = pltpu.roll(rows[3], 32, 1)
+        table[3 * q] = jnp.where(lane < 96, rows[0], one)
+        table[3 * q + 1] = jnp.where(lane < 64, one, two)
+        table[3 * q + 2] = jnp.where(lane < 32, two, three)
 
 
 def put_rows(target, start, vector, count):
@@ -595,23 +366,56 @@
     return jnp.sum(values.reshape(-1, 8, values.shape[-1]), axis=0)
 
 
+def excite_pick(shards, k):
+    deep = GATE // shards
+    line = lax.broadcasted_iota(jnp.int32, (GATE, shards * 16), 0)
+    column = lax.broadcasted_iota(jnp.int32, (GATE, shards * 16), 1)
+    wanted = (line // deep) * 16 + k * deep + lax.rem(line, deep)
+    return (column == wanted).astype(F32).astype(BF16)
+
+
 def excite_weights(small, block):
     shards = small.shape[0]
     rows = small[:, 32 * block + 16 : 32 * block + 32].reshape(shards * 16, LANES)
-    deep = GATE // shards
-    line = lax.broadcasted_iota(jnp.int32, (GATE, shards * 16), 0)
-    column = lax.broadcasted_iota(jnp.int32, (GATE, shards * 16), 1)
-    parts = []
-    for k in range(MID // LANES):
-        wanted = (line // deep) * 16 + k * deep + lax.rem(line, deep)
-        pick = (column == wanted).astype(F32).astype(BF16)
-        parts.append(matmul(pick, rows))
+    parts = [matmul(excite_pick(shards, k), rows) for k in range(MID // LANES)]
     return jnp.concatenate(parts, axis=1).astype(BF16)
 
 
 SMALL_SHARDS = 32
-NORM_ROWS = 104
-BLOCK_NORMS = 48
+TABLE = ((2 * MID + D) // LANES + 1, 8, LANES)
+
+
+JOBS = (
+    ("ina0", "inb0", "small", "mida0", "midb0", "midc0", "out0", "ina1", "inb1", "mida1", "midb1", "midc1"),
+    ("out1", "cls"),
+)
+PUSHES = (
+    {
+        "start": "ina0 small",
+        "dpad": "ina0 small inb0",
+        "fpad": "ina0 small inb0",
+        "warm": "ina0 small inb0 mida0",
+        "load": "inb0 mida0 midb0",
+        "ready": "mida0 midb0 midc0",
+        "first": "mida0 midb0 midc0 out0",
+        "far1": "midb0 midc0 out0",
+        "sum1": "midc0 out0 ina1",
+        "second": "out0 ina1 inb1",
+        "excite": "ina1 inb1 mida1",
+        "third": "ina1 inb1 mida1 midb1",
+        "far2": "inb1 mida1 midb1 midc1",
+        "sum2": "mida1 midb1 midc1",
+        "fourth": "midb1 midc1",
+        "sum3": "midc1",
+    },
+    {
+        "start": "out1",
+        "first": "out1 cls",
+        "sum1": "out1 cls",
+        "second": "out1 cls",
+        "excite": "cls",
+    },
+)
 
 
 def forward_kernel(n_seg, n_clip, block, jobs, plan, *refs):
@@ -623,21 +427,21 @@
         return taken if count != 1 else taken[0]
 
     last = block == 1
-    x_hbm, mask, following, norm_in = pop(4)
+    x_hbm, mask, following, table_in = pop(4)
     shards = dict(zip(jobs, [pop() for _ in jobs]))
     given = dict(zip(plan, [pop() for _ in plan]))
     wholes = dict(zip(jobs, [pop() for _ in jobs]))
     h1_out, low_out, gate_out, mix_out, f_out, h2_out, a2_out, h3_out = pop(8)
-    out_hbm, norm_out, st1, st2, st3 = pop(5)
+    out_hbm, table_out, st1, st2, st3 = pop(5)
     xv, w_in, w_mid, w_out, small = pop(5)
     h1v, a1v, lowv, rv, edge, dpad, mixv, gatev, fpad, h2v, a2v, h3v = pop(12)
     wide_sum, wide_square, w_exp = pop(3)
-    sums = [pop(4) for _ in range(4)]
+    sums = [pop(4) for _ in range(3)]
     pooled = pop() if last else None
     send_sem, recv_sem = pop(2)
     links = Links(n_seg, n_clip, send_sem, recv_sem)
     frames = xv.shape[1]
-    live = norm_out if not last else norm_in
+    table = table_in if last else table_out
     outgoing = []
 
     def send_out(source, target):
@@ -660,44 +464,50 @@
         copy.start()
         return copy
 
-    def push(*names):
-        for name in names:
+    def push(point):
+        for name in PUSHES[block].get(point, "").split():
             if name in gathers and gathers[name].at <= 3:
                 gathers[name].advance()
 
-    own_in = "in%d" % block
-    own_mid = "mid%d" % block
     own_out = "out%d" % block
-    if not last:
-        push(own_in, "small")
-        sums[0][0][...] = norm_in[...]
-        norm_out[...] = links.all_sum(*sums[0])
-        push(own_in, "small", own_mid)
-        dpad[...] = jnp.zeros_like(dpad)
-        fpad[...] = jnp.zeros_like(fpad)
-        push(own_in, "small")
-        push(own_in, "small", own_mid, own_out)
+
+    def load_pieces(kind, count, target):
+        rows = target.shape[0] // SMALL_SHARDS
+        size = rows // count
+        wide = target.reshape(SMALL_SHARDS, rows, MID)
+        return [
+            load(name, wide.at[:, k * size : (k + 1) * size])
+            for k, name in enumerate(piece_names(kind, block, count))
+        ]
+
+    push("start")
+    dpad[...] = jnp.zeros_like(dpad)
+    push("dpad")
+    fpad[...] = jnp.zeros_like(fpad)
+    push("fpad")
+    push("warm")
+    push("load")
+    waits = load_pieces("in", 2, w_in) + [load("small", small)]
+    push("ready")
+    for copy in waits:
+        copy.wait()
+    load_x.wait()
+    if last:
+        table_out[...] = table_in[...]
     else:
-        push(own_mid)
-        dpad[...] = jnp.zeros_like(dpad)
-        fpad[...] = jnp.zeros_like(fpad)
-    wait_in = load(own_in, w_in)
-    wait_small = load("small", small)
-    wait_in.wait()
-    load_x.wait()
-    norms = live
-    base = BLOCK_NORMS * block
-    live_rows = norms[98:99, 0:1]
+        table_out[...] = jnp.zeros_like(table_out)
+        build_table(small, table_out)
     half = MID // LANES
 
     def norm(index, tot, columns, start, out):
+        live_rows = table[TABLE[0] - 1, 0:1, 0:1]
         mean = jnp.concatenate([tot[k : k + 1] for k in range(4)], axis=1) / live_rows
         square = jnp.concatenate([tot[4 + k : 5 + k] for k in range(4)], axis=1) / live_rows
         inv = lax.rsqrt(square - mean * mean + NORM_EPS)
         out[0:1, :] = mean
         out[1:2, :] = inv
-        gain = row_vector(norms, base + start, columns // LANES)
-        shift = row_vector(norms, base + 24 + start, columns // LANES)
+        gain = row_vector(table, 2 * block, start, columns // LANES)
+        shift = row_vector(table, 2 * block + 1, start, columns // LANES)
         scale = gain * inv
         return scale, shift - mean * scale
 
@@ -716,15 +526,16 @@
 
     one, two = lax.fori_loop(0, GRID, first, (zeros, zeros))
     send_out(h1v, h1_out)
-    push(own_mid, own_out)
-    if not last:
-        push("in1")
-    stat = sums[1][0]
+    push("first")
+    stat = sums[0][0]
     put_rows(stat, 0, jnp.sum(one, axis=0, keepdims=True), 4)
     put_rows(stat, 4, jnp.sum(two, axis=0, keepdims=True), 4)
-    scale_one, shift_one = norm(0, links.all_sum(*sums[1]), MID, 0, st1)
-    push(own_mid)
-    wait_small.wait()
+    stat[8:16, :] = jnp.broadcast_to(HW * jnp.sum(mask[:, :LANES], axis=0, keepdims=True), (8, LANES))
+    total = links.all_sum(*sums[0], lambda: push("far1"))
+    if not last:
+        table_out[TABLE[0] - 1] = total[8:16]
+    scale_one, shift_one = norm(0, total, MID, 0, st1)
+    push("sum1")
     w_exp[...] = excite_weights(small, block)
     red = small[:, 32 * block : 32 * block + 16].reshape(MID, GATE)
 
@@ -742,9 +553,7 @@
     send_out(lowv, low_out)
     swap = links.remote(links.take(1), rv, edge, links.other)
     swap.start()
-    if last:
-        push(own_mid)
-    push(own_out)
+    push("second")
     swap.wait()
     row = lax.rem(lax.broadcasted_iota(jnp.int32, (frames, GATE), 0), 8)
 
@@ -757,6 +566,7 @@
         return carry
 
     lax.fori_loop(0, GRID, change, 0)
+    push("change")
 
     def excite(i, carry):
         for j in range(GRID):
@@ -776,15 +586,16 @@
     send_out(mixv, mix_out)
     send_out(gatev, gate_out)
     send_out(fpad.at[pl.ds(1, GRID), pl.ds(1, GRID)], f_out)
-    wait_mid = load(own_mid, w_mid)
-    push(own_out, "in1", "cls")
-    wait_mid.wait()
+    wait_mid = load_pieces("mid", 3, w_mid)
+    push("excite")
+    for copy in wait_mid:
+        copy.wait()
 
     def third(i, carry):
         part = None
         for k in range(9):
             window = fpad[i + k // 3, pl.ds(k % 3, GRID)].reshape(GRID * frames, MID)
-            term = matmul(window, w_mid[k])
+            term = matmul(window, w_mid[k * MID : (k + 1) * MID])
             part = term if part is None else part + term
         h2v[pl.ds(GRID * i, GRID)] = part.reshape(GRID, frames, MID)
         one, two = masked_sums(part)
@@ -792,13 +603,14 @@
 
     one, two = lax.fori_loop(0, GRID, third, (zeros, zeros))
     send_out(h2v, h2_out)
-    stat = sums[2][0]
+    stat = sums[1][0]
     put_rows(stat, 0, jnp.sum(one, axis=0, keepdims=True), 4)
     put_rows(stat, 4, jnp.sum(two, axis=0, keepdims=True), 4)
-    push(own_out)
-    scale_two, shift_two = norm(1, links.all_sum(*sums[2]), MID, half, st2)
+    push("third")
+    total = links.all_sum(*sums[1], lambda: push("far2"))
+    scale_two, shift_two = norm(1, total, MID, half, st2)
     wait_out = load(own_out, w_out)
-    push("in1", "cls")
+    push("sum2")
     wait_out.wait()
     wide_sum[...] = jnp.zeros_like(wide_sum)
     wide_square[...] = jnp.zeros_like(wide_square)
@@ -821,15 +633,14 @@
     lax.fori_loop(0, GRID, fourth, 0)
     send_out(a2v, a2_out)
     send_out(h3v, h3_out)
-    push("in1", "cls")
-    stat = sums[3][0]
+    push("fourth")
+    stat = sums[2][0]
     put_rows(stat, 0, jnp.sum(wide_sum[...], axis=0, keepdims=True), 4)
     put_rows(stat, 4, jnp.sum(wide_square[...], axis=0, keepdims=True), 4)
-    scale_three, shift_three = norm(2, links.all_sum(*sums[3]), D, 2 * half, st3)
-    push("cls")
+    scale_three, shift_three = norm(2, links.all_sum(*sums[2]), D, 2 * half, st3)
+    push("sum3")
     if last:
         pooled[...] = jnp.zeros_like(pooled)
-        norm_out[...] = jnp.zeros_like(norm_out)
 
     def fifth(p, carry):
         for k in range(4):
@@ -851,7 +662,7 @@
         copy.wait()
 
 
-def forward_block(block, x, mask, following, norms, shards, given):
+def forward_block(block, x, mask, following, table, shards, given):
     n_seg = lax.axis_size("seg")
     n_clip = lax.axis_size("clip")
     cells, frames, width = x.shape
@@ -877,14 +688,14 @@
         jax.ShapeDtypeStruct(grid_shape(MID), BF16),
         jax.ShapeDtypeStruct(grid_shape(D), BF16),
         jax.ShapeDtypeStruct((frames, D), F32) if last else jax.ShapeDtypeStruct(x.shape, BF16),
-        jax.ShapeDtypeStruct(norms.shape, F32),
+        jax.ShapeDtypeStruct(TABLE, F32),
         jax.ShapeDtypeStruct((8, MID), F32),
         jax.ShapeDtypeStruct((8, MID), F32),
         jax.ShapeDtypeStruct((8, D), F32),
     ]
     out_specs = [any_spec] * (len(jobs) + 9) + [vmem] * 4
 
-    shapes = [(D, MID), (9, MID, MID), (MID, D), (SMALL_SHARDS, 4 * 16, LANES)]
+    shapes = [(D, MID), (9 * MID, MID), (MID, D), (SMALL_SHARDS, 80, LANES)]
     scratch = [pltpu.VMEM(x.shape, BF16)]
     scratch += [pltpu.VMEM(s, BF16) for s in shapes]
     scratch += [
@@ -904,7 +715,7 @@
         pltpu.VMEM((8, D), F32),
         pltpu.VMEM((GATE, MID), BF16),
     ]
-    for shape in (norms.shape, (8, LANES), (8, LANES), (8, MID)):
+    for shape in ((16, LANES), (8, LANES), (8, MID)):
         scratch += sum_scratch(n_seg, n_clip, shape)
     if last:
         scratch.append(pltpu.VMEM((frames, D), F32))
@@ -920,7 +731,7 @@
             collective_id=30 + block, has_side_effects=True, vmem_limit_bytes=60 * 1024 * 1024
         ),
         name="forward_block",
-    )(x, mask, following, norms, *[shards[n] for n in jobs], *[given[n] for n in plan])
+    )(x, mask, following, table, *[shards[n] for n in jobs], *[given[n] for n in plan])
     wholes = dict(zip(jobs, results[: len(jobs)]))
     return wholes, results[len(jobs) :]
 
@@ -935,8 +746,8 @@
 
     last = block == 1
     h3_hbm, x_hbm, d_in, h2_hbm, h1_hbm, gate_hbm = pop(6)
-    in_hbm, mid_hbm, out_hbm, small_hbm = pop(4)
-    norms, st1, st2, st3, mask, present, following = pop(7)
+    in_a, in_b, mid_a, mid_b, mid_c, out_hbm, small_hbm = pop(7)
+    table, st1, st2, st3, mask, present, following = pop(7)
     dh3_out, dh2_out, de_out, dr_out, dh1_out, dx_out, norm_grads = pop(7)
     dv, h3v, xv, h2v, h1v, gatev, dyv, pad2, dsv, edge, pad_s, pad_e = pop(12)
     drv, dh1v, w_in, w_mid, w_out, small, w_exp = pop(7)
@@ -961,11 +772,19 @@
     if not last:
         loads_one.append(load(d_in, dv))
     loads_two = [load(out_hbm, w_out), load(h2_hbm, h2v)]
-    loads_three = [load(mid_hbm, w_mid), load(h1_hbm, h1v), load(gate_hbm, gatev), load(small_hbm, small)]
-    loads_four = [load(in_hbm, w_in)]
+    loads_three = [load(h1_hbm, h1v), load(gate_hbm, gatev), load(small_hbm, small)]
+    loads_four = []
+    for parts, target, waits in (
+        ((mid_a, mid_b, mid_c), w_mid, loads_three),
+        ((in_a, in_b), w_in, loads_four),
+    ):
+        rows = target.shape[0] // SMALL_SHARDS
+        size = rows // len(parts)
+        wide = target.reshape(SMALL_SHARDS, rows, MID)
+        for k, source in enumerate(parts):
+            waits.append(load(source, wide.at[:, k * size : (k + 1) * size]))
     links.meet()
-    base = BLOCK_NORMS * block
-    live_rows = norms[98:99, 0:1]
+    live_rows = table[TABLE[0] - 1, 0:1, 0:1]
     half = MID // LANES
     pad2[...] = jnp.zeros_like(pad2)
     pad_s[...] = jnp.zeros_like(pad_s)
@@ -974,8 +793,8 @@
     sum_shift[...] = jnp.zeros_like(sum_shift)
 
     def vectors(start, columns, stats):
-        gain = row_vector(norms, base + start, columns // LANES)
-        shift = row_vector(norms, base + 24 + start, columns // LANES)
+        gain = row_vector(table, 2 * block, start, columns // LANES)
+        shift = row_vector(table, 2 * block + 1, start, columns // LANES)
         return gain, shift, stats[0:1, :], stats[1:2, :]
 
     def totals(index, start, columns, gain_rows, shift_rows):
@@ -1064,7 +883,7 @@
         part = None
         for k in range(9):
             window = pad2[i + 2 - k // 3, pl.ds(2 - k % 3, GRID)].reshape(GRID * frames, MID)
-            term = dot_t(window, w_mid[k])
+            term = dot_t(window, w_mid[k * MID : (k + 1) * MID])
             part = term if part is None else part + term
         part = part.reshape(GRID, frames, MID)
         for j in range(GRID):
@@ -1137,16 +956,24 @@
             span = slice(k * MID, (k + 1) * MID)
             part = dot_t(rows, w_in[span, :])
             dv[pl.ds(GRID * i, GRID), :, span] += part.reshape(GRID, frames, MID)
+        dx_copy(i).start()
         return carry
+
+    dx_base = links.take(GRID)
+
+    def dx_copy(i):
+        rows = pl.ds(GRID * i, GRID)
+        return pltpu.make_async_copy(dv.at[rows], dx_out.at[rows], links.recv_sem.at[dx_base + i])
 
     lax.fori_loop(0, GRID, sixth, 0)
     send_out(dh1v, dh1_out)
-    send_out(dv, dx_out)
+    for i in range(GRID):
+        dx_copy(i).wait()
     for copy in outgoing:
         copy.wait()
 
 
-def backward_block(block, h3, x, d_in, h2, h1, gate, weights, norms, stats, masks):
+def backward_block(block, h3, x, d_in, h2, h1, gate, weights, table, stats, masks):
     n_seg = lax.axis_size("seg")
     n_clip = lax.axis_size("clip")
     cells, frames, width = x.shape
@@ -1164,7 +991,7 @@
         jax.ShapeDtypeStruct(grid_shape(GATE), BF16),
         jax.ShapeDtypeStruct(grid_shape(MID), BF16),
         jax.ShapeDtypeStruct(grid_shape(D), F32),
-        jax.ShapeDtypeStruct((BLOCK_NORMS, LANES), F32),
+        jax.ShapeDtypeStruct((48, LANES), F32),
     ]
     scratch = [
         pltpu.VMEM(grid_shape(D), F32),
@@ -1182,34 +1009,344 @@
         pltpu.VMEM(grid_shape(GATE), BF16),
         pltpu.VMEM(grid_shape(MID), BF16),
         pltpu.VMEM((D, MID), BF16),
-        pltpu.VMEM((9, MID, MID), BF16),
+        pltpu.VMEM((9 * MID, MID), BF16),
         pltpu.VMEM((MID, D), BF16),
-        pltpu.VMEM((SMALL_SHARDS, 64, LANES), BF16),
+        pltpu.VMEM((SMALL_SHARDS, 80, LANES), BF16),
         pltpu.VMEM((GATE, MID), BF16),
         pltpu.VMEM((8, D), F32),
         pltpu.VMEM((8, D), F32),
     ]
     for shape in ((8, MID), (8, LANES), (8, LANES)):
         scratch += sum_scratch(n_seg, n_clip, shape)
-    count = 3 * (n_seg * 4 + n_clip // 4) + 32
+    count = 3 * (n_seg * 4 + n_clip // 4) + 40
     scratch += [pltpu.SemaphoreType.DMA((count,)), pltpu.SemaphoreType.DMA((count,))]
     d_spec = vmem if last else any_spec
     return pl.pallas_call(
         functools.partial(backward_kernel, n_seg, n_clip, block),
         out_shape=outs,
-        in_specs=[any_spec, any_spec, d_spec] + [any_spec] * 7 + [vmem] * 7,
+        in_specs=[any_spec, any_spec, d_spec] + [any_spec] * 10 + [vmem] * 7,
         out_specs=[any_spec] * 6 + [vmem],
         scratch_shapes=scratch,
         compiler_params=pltpu.CompilerParams(
             collective_id=40 + block, has_side_effects=True, vmem_limit_bytes=62 * 1024 * 1024
         ),
         name="backward_block",
-    )(h3, x, d_in, h2, h1, gate, *weights, norms, *stats, *masks)
-
-
-def weight_gradients(x, kept, steps):
-    gated, a_low, mixed, a_two = kept
-    d_three, d_two, d_excite, d_reduced, d_one = steps
+    )(h3, x, d_in, h2, h1, gate, *weights, table, *stats, *masks)
+
+
+class Scatter:
+    def __init__(self, links, grad, rows, buffers, finish):
+        self.links = links
+        self.grad = grad
+        self.rows = rows
+        self.one, self.two, self.three, self.four = buffers
+        self.finish = finish
+        self.depth = links.outer
+        self.base = links.take(self.depth + 3)
+        self.at = -1
+
+    def copies(self):
+        links, base, depth = self.links, self.base, self.depth
+        if self.at == 0:
+            source = self.grad.at[1 - links.seg, :, :, self.rows]
+            return [links.remote(base, source, self.one, links.other)]
+        if self.at == 1:
+            found = []
+            for k in range(2):
+                source = self.one.at[:, links.jump * (1 - links.first) + links.step * k]
+                found.append(links.remote(base + 1 + k, source, self.two.at[:, k], links.across_first))
+            return found
+        if self.at == 2:
+            source = self.two.at[:, 1 - links.second]
+            return [links.remote(base + 3, source, self.three, links.across_second)]
+        found = []
+        for i in range(1, depth):
+            source = self.three.at[lax.rem(links.group + i, depth)]
+            found.append(links.remote(base + 3 + i, source, self.four.at[i - 1], links.far_peer(i)))
+        return found
+
+    def add(self):
+        links, depth = self.links, self.depth
+        one, two, three, four = self.one, self.two, self.three, self.four
+        if self.at == 0:
+
+            def add_one(i, carry):
+                z = i // 4
+                w = lax.rem(i, 4)
+                total = one[z, w].astype(F32) + self.grad[links.seg, z, w, self.rows].astype(F32)
+                one[z, w] = total.astype(BF16)
+                return carry
+
+            lax.fori_loop(0, 4 * depth, add_one, 0)
+        elif self.at == 1:
+
+            def add_two(i, carry):
+                z = i // 2
+                k = lax.rem(i, 2)
+                kept = one[z, links.jump * links.first + links.step * k]
+                two[z, k] = (two[z, k].astype(F32) + kept.astype(F32)).astype(BF16)
+                return carry
+
+            lax.fori_loop(0, 2 * depth, add_two, 0)
+        elif self.at == 2:
+
+            def add_three(z, carry):
+                three[z] = (three[z].astype(F32) + two[z, links.second].astype(F32)).astype(BF16)
+                return carry
+
+            lax.fori_loop(0, depth, add_three, 0)
+        else:
+            total = three[links.group].astype(F32)
+            for i in range(1, depth):
+                total = total + four[i - 1].astype(F32)
+            self.finish(total)
+
+    def advance(self):
+        if self.at > 3:
+            return
+        if self.at >= 0:
+            for copy in self.copies():
+                copy.wait()
+            self.add()
+        self.at += 1
+        if self.at <= 3:
+            for copy in self.copies():
+                copy.start()
+
+
+SCATTERED = {
+    "cls": (64, 2 * LANES),
+    "out1": (16, D),
+    "mida1": (48, MID),
+    "midb1": (48, MID),
+    "midc1": (48, MID),
+    "in1": (64, MID),
+    "out0": (16, D),
+    "mida0": (48, MID),
+    "midb0": (48, MID),
+    "midc0": (48, MID),
+    "in0": (64, MID),
+    "small": (80, LANES),
+}
+
+
+def gradient_kernel(n_seg, n_clip, *refs):
+    refs = list(refs)
+
+    def pop(count=1):
+        taken = refs[:count]
+        del refs[:count]
+        return taken if count != 1 else taken[0]
+
+    sources = [pop(10) for _ in range(2)]
+    cls_hbm, norm_rows_in, bias = pop(3)
+    out_refs = {}
+    for block in (0, 1):
+        out_refs["in%d" % block], out_refs["mid%d" % block], out_refs["out%d" % block] = pop(3)
+    out_refs["small"], out_refs["cls"], tail = pop(3)
+    big3, bigx, mid_a2, mid_d2, mid_d1, mid_low, mid_de, thin_dr, thin_s, fpad = pop(10)
+    g_in, g_mid, g_out, g_small, g_cls, squares = pop(6)
+    sums = pop(4)
+    buffers = {name: pop(4) for name in SCATTERED}
+    send_sem, recv_sem = pop(2)
+    links = Links(n_seg, n_clip, send_sem, recv_sem)
+    cells, frames = bigx.shape[0], bigx.shape[1]
+    rows_all = cells * frames
+    devices = SMALL_SHARDS
+
+    def load(source, target):
+        copy = links.local(source.reshape(target.shape), target)
+        copy.start()
+        return copy
+
+    interior = fpad.at[pl.ds(1, GRID), pl.ds(1, GRID)]
+    names = ("x", "d1", "f", "d2", "a2", "d3", "low", "dr", "s", "de")
+    targets = dict(zip(names, (bigx, mid_d1, interior, mid_d2, mid_a2, big3, mid_low, thin_dr, thin_s, mid_de)))
+    hbm = [dict(zip(names, source)) for source in sources]
+
+    def fetch(block, *keys):
+        return [load(hbm[block][key], targets[key]) for key in keys]
+
+    waits = {
+        "out": fetch(1, "a2", "d3"),
+        "small": fetch(1, "low", "dr", "s", "de"),
+    }
+    load_cls = load(cls_hbm, g_cls)
+    fpad[...] = jnp.zeros_like(fpad)
+    waits["mid"] = fetch(1, "f", "d2")
+    waits["in"] = fetch(1, "x", "d1")
+    links.meet()
+    squares[...] = jnp.zeros_like(squares)
+
+    def folded(ref, rows):
+        return ref.reshape(n_seg, links.outer, 4, rows, ref.shape[-1])
+
+    grads = {"cls": g_cls, "small": g_small}
+    jobs = {}
+
+    def make(name):
+        kind = name[:-1] if name not in ("cls", "small") else name
+        block = name[-1]
+        rows, columns = SCATTERED[name]
+        start = 0
+        if kind.startswith("mid"):
+            ref, shard_rows = g_mid, 3 * rows
+            start = rows * "abc".index(kind[3])
+            out = out_refs["mid" + block]
+        else:
+            ref = {"in": g_in, "out": g_out, "small": g_small, "cls": g_cls}[kind]
+            shard_rows = rows
+            out = out_refs[kind + block if kind in ("in", "out") else kind]
+
+        def finish(total):
+            out[start : start + rows, :] = total
+            squares[:, :columns] += fold(total * total)
+
+        jobs[name] = Scatter(links, folded(ref, shard_rows), pl.ds(start, rows), buffers[name], finish)
+
+    for name in SCATTERED:
+        make(name)
+
+    def push(*wanted):
+        for name in wanted:
+            jobs[name].advance()
+
+    def dot_tn(left, right):
+        return lax.dot_general(left, right, (((0,), (0,)), ((), ())), preferred_element_type=F32)
+
+    def ready(kind):
+        for copy in waits[kind]:
+            copy.wait()
+
+    def task_out():
+        ready("out")
+
+        def body(k, carry):
+            span = pl.ds(pl.multiple_of(k * MID, MID), MID)
+            part = dot_tn(mid_a2[...].reshape(rows_all, MID), big3[:, :, span].reshape(rows_all, MID))
+            g_out[:, span] = part.astype(BF16)
+            return carry
+
+        lax.fori_loop(0, D // MID, body, 0)
+
+    def task_in():
+        ready("in")
+
+        def body(k, carry):
+            span = pl.ds(pl.multiple_of(k * MID, MID), MID)
+            part = dot_tn(bigx[:, :, span].reshape(rows_all, MID), mid_d1[...].reshape(rows_all, MID))
+            g_in[span, :] = part.astype(BF16)
+            return carry
+
+        lax.fori_loop(0, D // MID, body, 0)
+
+    def task_mid(first, last):
+        if first == 0:
+            ready("mid")
+
+        def body(k, carry):
+            window = fpad[pl.ds(k // 3, GRID), pl.ds(lax.rem(k, 3), GRID)].reshape(rows_all, MID)
+            part = dot_tn(window, mid_d2[...].reshape(rows_all, MID))
+            g_mid[pl.ds(pl.multiple_of(k * MID, MID), MID), :] = part.astype(BF16)
+            return carry
+
+        lax.fori_loop(first, last, body, 0)
+
+    def task_small(block):
+        ready("small")
+        part = dot_tn(mid_low[...].reshape(rows_all, MID), thin_dr[...].reshape(rows_all, GATE))
+        g_small[:, 32 * block : 32 * block + 16, :] = part.astype(BF16).reshape(devices, 16, LANES)
+        part = dot_tn(thin_s[...].reshape(rows_all, GATE), mid_de[...].reshape(rows_all, MID)).astype(BF16)
+        rows = jnp.zeros((devices * 16, LANES), F32)
+        for k in range(MID // LANES):
+            rows = rows + dot_tn(excite_pick(devices, k), part[:, k * LANES : (k + 1) * LANES])
+        g_small[:, 32 * block + 16 : 32 * block + 32, :] = rows.astype(BF16).reshape(devices, 16, LANES)
+
+    g_small[:, 64:80, :] = norm_rows_in[...]
+    load_cls.wait()
+    push("cls")
+    task_out()
+    push("cls", "out1")
+    waits["out"] = fetch(0, "a2", "d3")
+    task_mid(0, 4)
+    push("cls", "out1")
+    task_mid(4, 9)
+    push("cls", "out1", "mida1", "midb1")
+    waits["mid"] = fetch(0, "f", "d2")
+    task_small(1)
+    waits["small"] = fetch(0, "low", "dr", "s", "de")
+    push("out1", "mida1", "midc1")
+    task_in()
+    push("cls", "out1", "midb1", "mida1", "in1")
+    waits["in"] = fetch(0, "x", "d1")
+    task_out()
+    push("midc1", "midb1", "mida1", "in1", "out0")
+    task_mid(0, 4)
+    push("mida1", "midc1", "midb1", "in1", "out0")
+    task_mid(4, 9)
+    push("midb1", "midc1", "in1", "out0", "mida0", "midb0")
+    task_small(0)
+    push("midc1", "in1", "out0", "mida0", "midc0")
+    task_in()
+    push("out0", "midb0", "mida0", "in0")
+    push("midc0", "midb0", "mida0", "in0", "small")
+    push("mida0", "midc0", "midb0", "in0", "small")
+    push("midb0", "midc0", "in0", "small")
+    push("midc0", "in0", "small")
+    for name in SCATTERED:
+        while jobs[name].at <= 3:
+            jobs[name].advance()
+    total = jnp.sum(jnp.sum(squares[...], axis=0, keepdims=True), axis=1, keepdims=True)
+    sums[0][0:8, :] = bias[...]
+    sums[0][8:16, :] = jnp.broadcast_to(total, (8, LANES))
+    tail[...] = links.all_sum(*sums)
+
+
+def gradient_sums(sources, g_cls, norm_rows_in, bias):
+    n_seg = lax.axis_size("seg")
+    n_clip = lax.axis_size("clip")
+    depth = n_clip // 4
+    cells, frames, width = sources[0][0].shape
+    any_spec = pl.BlockSpec(memory_space=pl.ANY)
+    vmem = pl.BlockSpec(memory_space=pltpu.VMEM)
+
+    def grid_shape(columns):
+        return pltpu.VMEM((cells, frames, columns), BF16)
+
+    outs = []
+    for block in (0, 1):
+        outs += [(64, MID), (144, MID), (16, D)]
+    outs += [(80, LANES), (64, 2 * LANES), (16, LANES)]
+    scratch = [grid_shape(D), grid_shape(D)] + [grid_shape(MID)] * 5 + [grid_shape(GATE)] * 2
+    scratch += [
+        pltpu.VMEM((GRID + 2, GRID + 2, frames, MID), BF16),
+        pltpu.VMEM((D, MID), BF16),
+        pltpu.VMEM((9 * MID, MID), BF16),
+        pltpu.VMEM((MID, D), BF16),
+        pltpu.VMEM((SMALL_SHARDS, 80, LANES), BF16),
+        pltpu.VMEM((D, 2 * LANES), BF16),
+        pltpu.VMEM((8, D), F32),
+    ]
+    scratch += sum_scratch(n_seg, n_clip, (16, LANES))
+    for shape in SCATTERED.values():
+        for lead in ((depth, 4), (depth, 2), (depth,), (depth - 1,)):
+            scratch.append(pltpu.VMEM(lead + shape, BF16))
+    count = n_seg * 4 + depth + len(SCATTERED) * (depth + 3) + 40
+    scratch += [pltpu.SemaphoreType.DMA((count,)), pltpu.SemaphoreType.DMA((count,))]
+    return pl.pallas_call(
+        functools.partial(gradient_kernel, n_seg, n_clip),
+        out_shape=[jax.ShapeDtypeStruct(s, F32) for s in outs],
+        in_specs=[any_spec] * 21 + [vmem, vmem],
+        out_specs=[vmem] * len(outs),
+        scratch_shapes=scratch,
+        compiler_params=pltpu.CompilerParams(
+            collective_id=50, has_side_effects=True, vmem_limit_bytes=62 * 1024 * 1024
+        ),
+        name="gradient_sums",
+    )(*sources[0], *sources[1], g_cls, norm_rows_in, bias)
+
+
+def weight_gradients(x, d_one, gated, d_two, a_two, d_three, a_low, d_reduced, mixed, d_excite):
     return [
         matmul(x.reshape(-1, D).T, d_one.reshape(-1, MID)),
         conv(gated, d_two, ("HWCN", "HWIO", "HWNC")).reshape(9 * MID, MID),
@@ -1228,7 +1365,7 @@
     following = (slot_ids[None, :] + 1 < clip_counts[:, None]).astype(F32)
     frame_mask = jnp.broadcast_to(present.reshape(frames, 1), (frames, MID))
     frame_following = jnp.broadcast_to(following.reshape(frames, 1), (frames, GATE))
-    table = norm_table(master, HW * jnp.sum(present))
+    table = jnp.zeros(TABLE, F32)
     x_low = inputs.reshape(frames, HW, D).transpose(1, 0, 2)
     shards = weight_shards(master)
     if shards is None:
@@ -1236,14 +1373,13 @@
         jobs = ((), ())
     else:
         weights = {}
-        jobs = (("in0", "small", "mid0", "out0", "in1"), ("mid1", "out1", "cls"))
+        jobs = JOBS
     kept = []
     flowing = x_low
     flows = []
     for block in range(2):
         flows.append(flowing)
-        names = ("in%d" % block, "small", "mid%d" % block, "out%d" % block)
-        given = {name: weights[name] for name in names if name not in jobs[block]}
+        given = {name: weights[name] for name in weight_names(block) if name not in jobs[block]}
         gathered, results = forward_block(
             block,
             flowing,
@@ -1259,7 +1395,8 @@
         kept.append(results[:8] + results[10:])
         flowing = results[8]
     w_cls = weights["cls"][:, :CLASSES]
-    b_cls = table[96:98].reshape(-1)[:CLASSES]
+    bias_row = 64 + 4
+    b_cls = weights["small"].reshape(SMALL_SHARDS, 80, LANES)[:, bias_row, :6].reshape(-1)[:CLASSES].astype(F32)
     partial_value = jnp.sum(flowing.reshape(clip_local, slot_local, D), axis=1)
     pooled_sum = lax.psum(partial_value.astype(BF16), "seg").astype(F32)
     counts_float = clip_counts.astype(F32)
@@ -1276,7 +1413,8 @@
     scaled = d_pooled / (HW * counts_float)[:, None]
     d_flow = (present[:, :, None] * scaled[:, None]).reshape(frames, D)
     masks = (frame_mask, frame_mask[:, :GATE], frame_following)
-    grads = [None, None]
+    sources = [None, None]
+    norm_grads = [None, None]
     for block in (1, 0):
         h_one, a_low, gate, mixed, gated, h_two, a_two, h_three, st_one, st_two, st_three = kept[block]
         *steps, d_flow, norm_sums = backward_block(
@@ -1287,22 +1425,39 @@
             h_two,
             h_one,
             gate,
-            [weights[name + str(block)] for name in ("in", "mid", "out")] + [weights["small"]],
+            [weights[name] for name in weight_names(block)],
             table,
             (st_one, st_two, st_three),
             masks,
         )
-        grads[block] = weight_gradients(flows[block], (gated, a_low, mixed, a_two), steps)
-        devices = seg_count * lax.axis_size("clip")
-        grads[block] += [norm_sums[:24].reshape(-1) / devices, norm_sums[24:].reshape(-1) / devices]
-    grad_mine = scatter_gradients(grads[0] + grads[1] + [g_cls, g_bias])
-    tail = jnp.concatenate(
-        [
-            jnp.pad(g_bias, (0, 8 * LANES - CLASSES)).reshape(8, LANES),
-            jnp.full((8, LANES), jnp.sum(grad_mine * grad_mine), F32),
-        ]
-    )
-    tail = small_sum(tail)
+        sources[block] = (flows[block], steps[4], gated, steps[1], a_two, steps[0], a_low, steps[3], mixed, steps[2])
+        norm_grads[block] = [norm_sums[:24].reshape(-1), norm_sums[24:].reshape(-1)]
+    devices = seg_count * lax.axis_size("clip")
+    bias_rows = jnp.pad(g_bias, (0, 8 * LANES - CLASSES)).reshape(8, LANES)
+    if shards is None:
+        grads = []
+        for block in (0, 1):
+            grads += weight_gradients(*sources[block]) + [v / devices for v in norm_grads[block]]
+        grad_mine = scatter_gradients(grads + [g_cls, g_bias])
+        square = jnp.full((8, LANES), jnp.sum(grad_mine * grad_mine), F32)
+        tail = lax.psum(jnp.concatenate([bias_rows, square]), AXES)
+    else:
+        vectors = [v.reshape(SMALL_SHARDS, -1) / devices for b in (0, 1) for v in norm_grads[b]]
+        padded = jnp.pad(g_bias, (0, 6 * SMALL_SHARDS - CLASSES)).reshape(SMALL_SHARDS, 6)
+        extra = norm_rows(vectors + [padded]).astype(BF16)
+        cls_low = jnp.pad(g_cls.astype(BF16), ((0, 0), (0, 2 * LANES - CLASSES)))
+        *sums, tail = gradient_sums(sources, cls_low, extra, bias_rows)
+        mine = []
+        small = sums[6]
+        for block in (0, 1):
+            mine += [v.reshape(-1) for v in sums[3 * block : 3 * block + 3]]
+            mine.append(small[32 * block : 32 * block + 16].reshape(-1))
+            turned = small[32 * block + 16 : 32 * block + 32].reshape(MID // LANES, -1, LANES)
+            mine.append(jnp.swapaxes(turned, 0, 1).reshape(-1))
+            mine.append(small[64 + 2 * block, :96])
+            mine.append(small[65 + 2 * block, :96])
+        mine += [sums[7][:, :CLASSES].reshape(-1), small[68, :6]]
+        grad_mine = jnp.concatenate(mine)
     norm = jnp.sqrt(tail[8, 0])
     bias_grad = tail[:8].reshape(-1)[:CLASSES]
     factor = jnp.minimum(1.0, CLIP_LIMIT / (norm + 1e-06))

time: 646 us -> 557 us (0.86)
  matrix products: 57.9 us -> 2.56 us
  Pallas kernels: 508 us -> 485 us
    dot_general x11 -> x3, matrix products: 37.1 us -> 2.56 us  [matmul(): return jnp.dot(left, right, preferred_element_type=F32)]
    conv_general_dilated x2 -> x0, matrix products: 20.8 us -> none  [conv(): lax.conv_general_dilated(values, kernel, (1, 1), ((1, 1), (1, 1)), dimens...]
    pallas_call x2 -> x1, Pallas kernels: 151 us -> 142 us  [gradient_sums(): pl.pallas_call(functools.partial(gradient_kernel, n_seg, n_clip), out_sha...]
    pallas_call x2, Pallas kernels: 211 us -> 203 us  [forward_block(): pl.pallas_call(functools.partial(forward_kernel, n_seg, n_clip, block, jo...]
    unnamed x57 -> x36, local copies, waits for them, and re-layouts: 24.7 us -> 22.7 us
where the time goes in v4:
time: 557 us; the launch traced here: 552 us
  Pallas kernels  485 us (87%)
  local copies, waits for them, and re-layouts  49.6 us (9%)
  other arithmetic  7.81 us (1%)
    pallas_call x2, Pallas kernels, forward_block(): pl.pallas_call(functools.partial(forward_kernel, n_seg, n_clip, block, jo...  203 us
    pallas_call x1, Pallas kernels, gradient_sums(): pl.pallas_call(functools.partial(gradient_kernel, n_seg, n_clip), out_sha...  142 us
    pallas_call x2, Pallas kernels, backward_block(): pl.pallas_call(functools.partial(backward_kernel, n_seg, n_clip, block),...  140 us
    unnamed x36, local copies, waits for them, and re-layouts  22.7 us

profile of v4, /device:TPU:0, one launch (start us, length us, event | category | flops | bytes accessed | tf_op | source)
XLA Modules:
  0.0 551.7 jit_solution(8629769652933032849)
XLA Ops:
  0.6 1.3 convert_element_type.86
  2.0 0.1 slice_bitcast_fusion.16
  2.1 0.1 fusion.19
  2.2 0.1 constant_dynamic-update-slice_fusion.2
  2.3 0.1 fusion.17
  2.5 0.1 reshape.253
  2.6 0.7 slice_bitcast_fusion.6
  3.3 0.1 fusion.18
  3.4 0.1 reshape.248
  3.5 0.1 reshape.256
  3.6 0.7 slice_bitcast_fusion
  4.3 0.1 lt.49
  4.4 0.1 lt.57
  4.5 0.1 lt.54
  4.6 0.1 lt.50
  4.7 0.1 lt.51
  4.7 0.7 broadcast_in_dim.16.refs_1_.refs_17_
  5.5 0.7 reshape.252.refs_10_
  6.1 0.7 broadcast_in_dim.17.refs_2_.refs_19_
  6.8 6.7 %copy.53 = bf16[4,8,49,2048]{3,1,0,2:T(8,128)(2,1)} copy(bf16[4,8,49,2048]{3,1,2,0:T(8,128)(2,1)} %param.6) | data formatting | bytes 12845056 | tf_op args[0]
  13.5 0.6 broadcast_in_dim.18.refs_3_
  14.1 130.9 %forward_block.2 = (bf16[1024,512]{1,0:T(8,128)(2,1)}, bf16[1024,512]{1,0:T(8,128)(2,1)}, bf16[2560,128]{1,0:T(8,128)(2,1)}, bf16[1536,512]{1,0:T(8,128)(2,1)}, ...) custom-call(bf16[49,32,2048]{2,1,0:T(8,128)(2,1)} %bitcast.126, ...), custom_call_target="tpu_custom_call" | custom-call | tf_op jit(solution)/shard_map/forward_block/pallas_call | solution.py:724
  145.0 0.7 reshape.260.refs_4_
  145.7 0.2 reshape.261
  145.9 0.6 pad.71.refs_5_
  146.5 72.0 %forward_block.3 = (bf16[512,2048]{1,0:T(8,128)(2,1)}, bf16[2048,256]{1,0:T(8,128)(2,1)}, f32[49,32,512]{2,1,0:T(8,128)}, bf16[49,32,512]{2,1,0:T(8,128)(2,1)}, ...) custom-call(bf16[49,32,2048]{2,1,0:T(8,128)(2,1)} %get-tuple-element, ...), custom_call_target="tpu_custom_call" | custom-call | tf_op jit(solution)/shard_map/forward_block/pallas_call | solution.py:724
  218.5 1.1 bitcast_reduce_fusion
  219.7 3.4 psum.7
  223.0 0.8 slice.213
  223.9 0.1 reshape.282
  224.0 1.6 fusion.21
  225.6 0.2 fusion.6
  225.8 0.4 convolution_divide_fusion
  226.2 0.8 bitcast_multiply_fusion.refs_2_
  227.0 0.7 slice.169.refs_18_
  227.7 68.6 %backward_block.2 = (bf16[49,32,2048]{2,1,0:T(8,128)(2,1)}, bf16[7,7,32,512]{3,2,1,0:T(8,128)(2,1)}, bf16[49,32,512]{2,1,0:T(8,128)(2,1)}, bf16[49,32,128]{2,1,0...) custom-call(bf16[49,32,2048]{2,1,0:T(8,128)(2,1)} %get-tuple-element.78.refs_0_, ...), custom_call_target="tpu_custom_call" | custom-call | tf_op jit(solution)/shard_map/backward_block/pallas_call | solution.py:1024
  296.3 71.7 %backward_block.3 = (bf16[49,32,2048]{2,1,0:T(8,128)(2,1)}, bf16[7,7,32,512]{3,2,1,0:T(8,128)(2,1)}, bf16[49,32,512]{2,1,0:T(8,128)(2,1)}, bf16[49,32,128]{2,1,0...) custom-call(bf16[49,32,2048]{2,1,0:T(8,128)(2,1)} %get-tuple-element.69.refs_0_, ...), custom_call_target="tpu_custom_call" | custom-call | tf_op jit(solution)/shard_map/backward_block/pallas_call | solution.py:1024
  368.0 11.8 %copy.42 = f32[4,8,49,2048]{3,1,2,0:T(8,128)} copy(f32[4,8,49,2048]{3,1,0,2:T(8,128)} %bitcast.129) | data formatting | bytes 25690112
  379.8 0.1 fusion.11
  379.9 0.1 reshape.264
  380.1 0.1 div.89
  380.2 0.1 div.91
  380.4 0.1 div.93
  380.5 0.1 div.95
  380.6 0.1 stack.53
  380.7 0.7 pad.79.refs_21_
  381.4 0.6 pad_bitcast_fusion.5.refs_22_
  382.0 0.6 fusion
  382.6 1.1 pad.72.refs_20_
  383.7 142.0 %gradient_sums.1 = (f32[64,512]{1,0:T(8,128)}, f32[144,512]{1,0:T(8,128)}, f32[16,2048]{1,0:T(8,128)}, f32[64,512]{1,0:T(8,128)}, f32[144,512]{1,0:T(8,128)}, /*...) custom-call(bf16[49,32,2048]{2,1,0:T(8,128)(2,1)} %bitcast.128, ...), custom_call_target="tpu_custom_call" | custom-call | tf_op jit(solution)/shard_map/gradient_sums/pallas_call | solution.py:1336
  525.8 1.1 copy.46
  526.9 1.0 copy.49
  527.9 0.9 copy.45
  528.9 0.9 copy.47
  529.9 0.2 reshape.278
  530.2 0.6 fusion.20
  530.8 0.6 copy.40
  531.4 0.6 copy.41
  532.0 0.6 slice_bitcast_fusion.21
  532.6 0.5 slice_bitcast_fusion.20
  533.1 10.6 %concatenate.7 = f32[298246]{0:T(1024)S(1)} concatenate(f32[32768]{0:T(1024)S(1)} %bitcast.133, f32[73728]{0:T(1024)S(1)} %bitcast.131, f32[32768]{0:T(1024)S(1)} %bitcast.134, f32[2048]{0:T(1024)} %get-tuple-element.185, f32[2048]{0:T(1024)} %bitcast.144, f32[96]{0:T(128)} %get-tuple-element.181, f32[96]{0:T(128)} %get-tuple-element.180, f32[32768]{0:T(1024)S(1)} %bitcast.135, ...), dimensions={0} | concatenate | bytes 2385968 | tf_op jit(solution)/shard_map/concatenate | solution.py:1460
  543.7 1.2 slice.184
  545.6 4.2 fusion.15
  549.9 0.6 slice.186
  (61 shorter events, 0.5 us)
Async XLA Ops:
  2.0 2.6 copy-start.9
  2.3 11.1 %copy-start.5 = (bf16[80,128]{1,0:T(8,128)(2,1)}, bf16[80,128]{1,0:T(8,128)(2,1)S(1)}, u32[]{:S(2)}) copy-start(bf16[80,128]{1,0:T(8,128)(2,1)S(1)} %constant_dynamic-update-slice_fusion.refs_6_) | copy-start | bytes 61444
  218.5 7.3 %copy-start.10 = (s32[4]{0:T(128)S(1)}, s32[4]{0:T(128)}, u32[]{:S(2)}) copy-start(s32[4]{0:T(128)} %param.8) | copy-start | bytes 52
  218.5 7.3 %copy-start.11 = (bf16[2048,256]{1,0:T(8,128)(2,1)S(1)}, bf16[2048,256]{1,0:T(8,128)(2,1)}, u32[]{:S(2)}) copy-start(bf16[2048,256]{1,0:T(8,128)(2,1)} %get-tuple-element.80) | copy-start | bytes 3145732
  368.0 12.1 %copy-start.7 = (f32[48,128]{1,0:T(8,128)S(1)}, f32[48,128]{1,0:T(8,128)}, u32[]{:S(2)}) copy-start(f32[48,128]{1,0:T(8,128)} %get-tuple-element.119) | copy-start | bytes 73732
  368.0 12.3 %copy-start.6 = (f32[48,128]{1,0:T(8,128)S(1)}, f32[48,128]{1,0:T(8,128)}, u32[]{:S(2)}) copy-start(f32[48,128]{1,0:T(8,128)} %get-tuple-element.120) | copy-start | bytes 73732
  525.8 4.1 copy-start.2
  525.8 4.1 copy-start.1
  525.8 4.1 copy-start.3
  525.8 4.4 copy-start.4
  529.8 15.8 %copy-start = (f32[298246]{0:T(1024)S(1)}, f32[298246]{0:T(1024)}, u32[]{:S(2)}) copy-start(f32[298246]{0:T(1024)} %param.9) | copy-start | bytes 3578956
  545.6 4.2 copy-start.8

commit v5 on v4

--- a/solution.py
+++ b/solution.py
@@ -251,7 +251,7 @@
         repeat(1, n_far + 1, lambda i: greet(self.far_peer(i)))
         pl.semaphore_wait(barrier, n_near + n_far)
 
-    def all_sum(self, source, middle, near, far, between=lambda: None):
+    def sum_near(self, source, middle, near, far):
         n_near = self.n_seg * 4 - 1
         n_far = self.outer - 1
         base = self.take(n_near + n_far)
@@ -266,9 +266,15 @@
         repeat(1, n_near + 1, lambda i: close(i).wait())
         middle[...] = source[...] + jnp.sum(near[...], axis=0)
         repeat(1, n_far + 1, lambda i: distant(i).start())
-        between()
-        repeat(1, n_far + 1, lambda i: distant(i).wait())
-        return middle[...] + jnp.sum(far[...], axis=0)
+
+        def rest():
+            repeat(1, n_far + 1, lambda i: distant(i).wait())
+            return middle[...] + jnp.sum(far[...], axis=0)
+
+        return rest
+
+    def all_sum(self, source, middle, near, far):
+        return self.sum_near(source, middle, near, far)()
 
 
 def repeat(first, last, action):
@@ -385,37 +391,23 @@
 TABLE = ((2 * MID + D) // LANES + 1, 8, LANES)
 
 
-JOBS = (
-    ("ina0", "inb0", "small", "mida0", "midb0", "midc0", "out0", "ina1", "inb1", "mida1", "midb1", "midc1"),
-    ("out1", "cls"),
+STAGES = (
+    (
+        "ina0", "small", "inb0", "mida0", "@dpad", "@fpad", "ina0", "midb0", "small", "ina0", "midc0", "inb0",
+        "small", "ina0", "out0", "mida0", "inb0", "small", "ina0", "midb0", "mida0", "ina1", "small", "inb0",
+        "inb1", "midc0", "midb0", "mida1", "inb0", "@first", "midb1", "mida0", "midc0", "out0", "@near1", "mida0",
+        "midc1", "midb0", "ina1", "inb1", "@far1", "midb0", "midc0", "out0", "ina1", "mida1", "@second", "inb1",
+        "@swap", "@excite", "midc0", "midb1", "@third", "out0", "ina1", "mida1", "midc1", "@near2", "out0", "ina1",
+        "inb1", "midb1", "@far2", "mida1", "midc1", "@fourth", "inb1", "mida1", "midb1", "@near3", "midc1",
+        "@far3", "midb1", "@fifth", "midc1",
+    ),
+    (
+        "out1", "@dpad", "@fpad", "@first", "cls", "@near1", "out1", "@far1", "cls", "@second", "@swap", "out1",
+        "@excite", "cls", "@third", "out1", "@near2", "cls", "@far2", "out1", "@fourth", "cls", "@near3", "@far3",
+        "@fifth",
+    ),
 )
-PUSHES = (
-    {
-        "start": "ina0 small",
-        "dpad": "ina0 small inb0",
-        "fpad": "ina0 small inb0",
-        "warm": "ina0 small inb0 mida0",
-        "load": "inb0 mida0 midb0",
-        "ready": "mida0 midb0 midc0",
-        "first": "mida0 midb0 midc0 out0",
-        "far1": "midb0 midc0 out0",
-        "sum1": "midc0 out0 ina1",
-        "second": "out0 ina1 inb1",
-        "excite": "ina1 inb1 mida1",
-        "third": "ina1 inb1 mida1 midb1",
-        "far2": "inb1 mida1 midb1 midc1",
-        "sum2": "mida1 midb1 midc1",
-        "fourth": "midb1 midc1",
-        "sum3": "midc1",
-    },
-    {
-        "start": "out1",
-        "first": "out1 cls",
-        "sum1": "out1 cls",
-        "second": "out1 cls",
-        "excite": "cls",
-    },
-)
+JOBS = tuple(tuple(dict.fromkeys(item for item in order if item[0] != "@")) for order in STAGES)
 
 
 def forward_kernel(n_seg, n_clip, block, jobs, plan, *refs):
@@ -454,49 +446,37 @@
     load_x.start()
     gathers = {name: Gather(links, shards[name], wholes[name]) for name in jobs}
 
-    def load(name, target):
-        if name in gathers:
-            gathers[name].finish()
-            source = wholes[name]
-        else:
-            source = given[name]
-        copy = links.local(source.reshape(target.shape), target)
-        copy.start()
-        return copy
-
-    def push(point):
-        for name in PUSHES[block].get(point, "").split():
-            if name in gathers and gathers[name].at <= 3:
-                gathers[name].advance()
-
-    own_out = "out%d" % block
-
-    def load_pieces(kind, count, target):
+    targets = {"out%d" % block: w_out, "small": small}
+    for kind, target, count in (("in", w_in, 2), ("mid", w_mid, 3)):
         rows = target.shape[0] // SMALL_SHARDS
         size = rows // count
         wide = target.reshape(SMALL_SHARDS, rows, MID)
-        return [
-            load(name, wide.at[:, k * size : (k + 1) * size])
-            for k, name in enumerate(piece_names(kind, block, count))
-        ]
-
-    push("start")
-    dpad[...] = jnp.zeros_like(dpad)
-    push("dpad")
-    fpad[...] = jnp.zeros_like(fpad)
-    push("fpad")
-    push("warm")
-    push("load")
-    waits = load_pieces("in", 2, w_in) + [load("small", small)]
-    push("ready")
-    for copy in waits:
-        copy.wait()
-    load_x.wait()
-    if last:
-        table_out[...] = table_in[...]
-    else:
-        table_out[...] = jnp.zeros_like(table_out)
-        build_table(small, table_out)
+        for k, name in enumerate(piece_names(kind, block, count)):
+            targets[name] = wide.at[:, k * size : (k + 1) * size]
+    loads = {}
+
+    def load(name):
+        source = wholes[name] if name in gathers else given[name]
+        loads[name] = links.local(source.reshape(targets[name].shape), targets[name])
+        loads[name].start()
+
+    def push(name):
+        if gathers[name].at <= 3:
+            gathers[name].advance()
+            if gathers[name].at > 3 and name in targets:
+                load(name)
+
+    def need(*names):
+        for name in names:
+            while name not in loads:
+                push(name)
+        for name in names:
+            loads[name].wait()
+
+    for name in weight_names(block):
+        if name not in gathers:
+            load(name)
+    table = table_in if last else table_out
     half = MID // LANES
 
     def norm(index, tot, columns, start, out):
@@ -517,6 +497,7 @@
         return fold(masked), fold(masked * shaped)
 
     zeros = jnp.zeros((8, MID), F32)
+    kept = {}
 
     def first(i, carry):
         part = matmul(xv[pl.ds(GRID * i, GRID)].reshape(GRID * frames, D), w_in[...])
@@ -524,37 +505,59 @@
         one, two = masked_sums(part)
         return (carry[0] + one, carry[1] + two)
 
-    one, two = lax.fori_loop(0, GRID, first, (zeros, zeros))
-    send_out(h1v, h1_out)
-    push("first")
-    stat = sums[0][0]
-    put_rows(stat, 0, jnp.sum(one, axis=0, keepdims=True), 4)
-    put_rows(stat, 4, jnp.sum(two, axis=0, keepdims=True), 4)
-    stat[8:16, :] = jnp.broadcast_to(HW * jnp.sum(mask[:, :LANES], axis=0, keepdims=True), (8, LANES))
-    total = links.all_sum(*sums[0], lambda: push("far1"))
-    if not last:
-        table_out[TABLE[0] - 1] = total[8:16]
-    scale_one, shift_one = norm(0, total, MID, 0, st1)
-    push("sum1")
-    w_exp[...] = excite_weights(small, block)
-    red = small[:, 32 * block : 32 * block + 16].reshape(MID, GATE)
+    def put_sums(index, one, two):
+        stat = sums[index][0]
+        put_rows(stat, 0, jnp.sum(one, axis=0, keepdims=True), 4)
+        put_rows(stat, 4, jnp.sum(two, axis=0, keepdims=True), 4)
+        return stat
+
+    def stage_dpad():
+        dpad[...] = jnp.zeros_like(dpad)
+
+    def stage_fpad():
+        fpad[...] = jnp.zeros_like(fpad)
+        if last:
+            table_out[...] = table_in[...]
+        else:
+            table_out[...] = jnp.zeros_like(table_out)
+
+    def stage_first():
+        need(*piece_names("in", block, 2))
+        load_x.wait()
+        stat = put_sums(0, *lax.fori_loop(0, GRID, first, (zeros, zeros)))
+        present = HW * jnp.sum(mask[:, :LANES], axis=0, keepdims=True)
+        stat[8:16, :] = jnp.broadcast_to(present, (8, LANES))
+        send_out(h1v, h1_out)
+
+    def stage_near1():
+        kept["rest"] = links.sum_near(*sums[0])
+
+    def stage_far1():
+        need("small")
+        total = kept["rest"]()
+        if not last:
+            build_table(small, table_out)
+            table_out[TABLE[0] - 1] = total[8:16]
+        kept["one"] = norm(0, total, MID, 0, st1)
 
     def second(i, carry):
         for j in range(GRID):
-            y = h1v[GRID * i + j] * scale_one + shift_one
+            y = h1v[GRID * i + j] * kept["one"][0] + kept["one"][1]
             a = y * jax.nn.sigmoid(y)
             a1v[GRID * i + j] = a
             lowv[GRID * i + j] = a.astype(BF16)
-        part = matmul(lowv[pl.ds(GRID * i, GRID)].reshape(GRID * frames, MID), red)
+        part = matmul(lowv[pl.ds(GRID * i, GRID)].reshape(GRID * frames, MID), kept["red"])
         rv[pl.ds(GRID * i, GRID)] = part.astype(BF16).reshape(GRID, frames, GATE)
         return carry
 
-    lax.fori_loop(0, GRID, second, 0)
-    send_out(lowv, low_out)
-    swap = links.remote(links.take(1), rv, edge, links.other)
-    swap.start()
-    push("second")
-    swap.wait()
+    def stage_second():
+        w_exp[...] = excite_weights(small, block)
+        kept["red"] = small[:, 32 * block : 32 * block + 16].reshape(MID, GATE)
+        lax.fori_loop(0, GRID, second, 0)
+        send_out(lowv, low_out)
+        kept["swap"] = links.remote(links.take(1), rv, edge, links.other)
+        kept["swap"].start()
+
     row = lax.rem(lax.broadcasted_iota(jnp.int32, (frames, GATE), 0), 8)
 
     def change(i, carry):
@@ -565,8 +568,9 @@
             dpad[i + 1, j + 1] = following[...] * (later - now)
         return carry
 
-    lax.fori_loop(0, GRID, change, 0)
-    push("change")
+    def stage_swap():
+        kept["swap"].wait()
+        lax.fori_loop(0, GRID, change, 0)
 
     def excite(i, carry):
         for j in range(GRID):
@@ -582,14 +586,11 @@
             fpad[i + 1, j + 1] = (a1v[GRID * i + j] * (1.0 + gate)).astype(BF16)
         return carry
 
-    lax.fori_loop(0, GRID, excite, 0)
-    send_out(mixv, mix_out)
-    send_out(gatev, gate_out)
-    send_out(fpad.at[pl.ds(1, GRID), pl.ds(1, GRID)], f_out)
-    wait_mid = load_pieces("mid", 3, w_mid)
-    push("excite")
-    for copy in wait_mid:
-        copy.wait()
+    def stage_excite():
+        lax.fori_loop(0, GRID, excite, 0)
+        send_out(mixv, mix_out)
+        send_out(gatev, gate_out)
+        send_out(fpad.at[pl.ds(1, GRID), pl.ds(1, GRID)], f_out)
 
     def third(i, carry):
         part = None
@@ -601,23 +602,22 @@
         one, two = masked_sums(part)
         return (carry[0] + one, carry[1] + two)
 
-    one, two = lax.fori_loop(0, GRID, third, (zeros, zeros))
-    send_out(h2v, h2_out)
-    stat = sums[1][0]
-    put_rows(stat, 0, jnp.sum(one, axis=0, keepdims=True), 4)
-    put_rows(stat, 4, jnp.sum(two, axis=0, keepdims=True), 4)
-    push("third")
-    total = links.all_sum(*sums[1], lambda: push("far2"))
-    scale_two, shift_two = norm(1, total, MID, half, st2)
-    wait_out = load(own_out, w_out)
-    push("sum2")
-    wait_out.wait()
-    wide_sum[...] = jnp.zeros_like(wide_sum)
-    wide_square[...] = jnp.zeros_like(wide_square)
+    def stage_third():
+        need(*piece_names("mid", block, 3))
+        put_sums(1, *lax.fori_loop(0, GRID, third, (zeros, zeros)))
+        send_out(h2v, h2_out)
+
+    def stage_near2():
+        kept["rest"] = links.sum_near(*sums[1])
+
+    def stage_far2():
+        kept["two"] = norm(1, kept["rest"](), MID, half, st2)
+        wide_sum[...] = jnp.zeros_like(wide_sum)
+        wide_square[...] = jnp.zeros_like(wide_square)
 
     def fourth(i, carry):
         for j in range(GRID):
-            y = h2v[GRID * i + j] * scale_two + shift_two
+            y = h2v[GRID * i + j] * kept["two"][0] + kept["two"][1]
             a2v[GRID * i + j] = (y * jax.nn.sigmoid(y)).astype(BF16)
         rows = a2v[pl.ds(GRID * i, GRID)].reshape(GRID * frames, MID)
         for k in range(4):
@@ -630,22 +630,26 @@
             wide_square[:, k * MID : (k + 1) * MID] += two
         return carry
 
-    lax.fori_loop(0, GRID, fourth, 0)
-    send_out(a2v, a2_out)
-    send_out(h3v, h3_out)
-    push("fourth")
-    stat = sums[2][0]
-    put_rows(stat, 0, jnp.sum(wide_sum[...], axis=0, keepdims=True), 4)
-    put_rows(stat, 4, jnp.sum(wide_square[...], axis=0, keepdims=True), 4)
-    scale_three, shift_three = norm(2, links.all_sum(*sums[2]), D, 2 * half, st3)
-    push("sum3")
-    if last:
-        pooled[...] = jnp.zeros_like(pooled)
+    def stage_fourth():
+        need("out%d" % block)
+        lax.fori_loop(0, GRID, fourth, 0)
+        put_sums(2, wide_sum[...], wide_square[...])
+        send_out(a2v, a2_out)
+        send_out(h3v, h3_out)
+
+    def stage_near3():
+        kept["rest"] = links.sum_near(*sums[2])
+
+    def stage_far3():
+        kept["three"] = norm(2, kept["rest"](), D, 2 * half, st3)
+        if last:
+            pooled[...] = jnp.zeros_like(pooled)
 
     def fifth(p, carry):
         for k in range(4):
             span = slice(k * MID, (k + 1) * MID)
-            pre = h3v[p, :, span].astype(F32) * scale_three[:, span] + shift_three[:, span]
+            scale, shift = kept["three"]
+            pre = h3v[p, :, span].astype(F32) * scale[:, span] + shift[:, span]
             pre = pre + xv[p, :, span].astype(F32)
             value = pre * jax.nn.sigmoid(pre)
             if last:
@@ -654,8 +658,33 @@
                 xv[p, :, span] = value.astype(BF16)
         return carry
 
-    lax.fori_loop(0, HW, fifth, 0)
-    send_out(pooled if last else xv, out_hbm)
+    def stage_fifth():
+        lax.fori_loop(0, HW, fifth, 0)
+        send_out(pooled if last else xv, out_hbm)
+
+    stages = {
+        "dpad": stage_dpad,
+        "fpad": stage_fpad,
+        "first": stage_first,
+        "near1": stage_near1,
+        "far1": stage_far1,
+        "second": stage_second,
+        "swap": stage_swap,
+        "excite": stage_excite,
+        "third": stage_third,
+        "near2": stage_near2,
+        "far2": stage_far2,
+        "fourth": stage_fourth,
+        "near3": stage_near3,
+        "far3": stage_far3,
+        "fifth": stage_fifth,
+    }
+    for item in STAGES[block]:
+        if item[0] == "@":
+            with jax.named_scope(item[1:]):
+                stages[item[1:]]()
+        elif item in gathers:
+            push(item)
     for name in jobs:
         gathers[name].finish()
     for copy in outgoing:
@@ -1130,6 +1159,20 @@
 }
 
 
+ORDER = (
+    "cls", "@out1a", "@out1b", "out1", "cls", "@in1a", "in1", "@in1b", "out1", "cls", "@mid1a", "in1", "@mid1b",
+    "mida1", "midb1", "midc1", "@mid1c", "cls", "out1", "mida1", "@small1", "@in0a", "in0", "in1", "@in0b", "cls",
+    "out1", "midb1", "midc1", "@mid0a", "mida1", "@mid0b", "mida0", "midb0", "midc0", "out1", "in1", "@mid0c",
+    "midb1", "@small0", "small", "in0", "@out0a", "midc1", "mida1", "in1", "@out0b", "out0", "midb1", "mida0",
+    "mida1", "out0", "in0", "midc1", "midb1", "mida0", "midc1", "midb0", "out0", "in0", "mida0", "midc0", "midb0",
+    "in0", "out0", "small", "mida0", "midc0", "midb0", "small", "out0", "midc0", "small", "midb0", "midc0",
+    "small",
+)
+
+
+ORDER_FIRST = "out1a"
+
+
 def gradient_kernel(n_seg, n_clip, *refs):
     refs = list(refs)
 
@@ -1167,14 +1210,15 @@
     def fetch(block, *keys):
         return [load(hbm[block][key], targets[key]) for key in keys]
 
-    waits = {
-        "out": fetch(1, "a2", "d3"),
-        "small": fetch(1, "low", "dr", "s", "de"),
+    operands = {
+        "out": ("a2", "d3"),
+        "in": ("x", "d1"),
+        "mid": ("f", "d2"),
+        "small": ("low", "dr", "s", "de"),
     }
     load_cls = load(cls_hbm, g_cls)
+    waits = {"out": fetch(1, *operands["out"])}
     fpad[...] = jnp.zeros_like(fpad)
-    waits["mid"] = fetch(1, "f", "d2")
-    waits["in"] = fetch(1, "x", "d1")
     links.meet()
     squares[...] = jnp.zeros_like(squares)
 
@@ -1214,37 +1258,30 @@
     def dot_tn(left, right):
         return lax.dot_general(left, right, (((0,), (0,)), ((), ())), preferred_element_type=F32)
 
-    def ready(kind):
-        for copy in waits[kind]:
-            copy.wait()
-
-    def task_out():
-        ready("out")
-
+    turn = 1 - links.seg
+
+    def task_out(first, last):
         def body(k, carry):
             span = pl.ds(pl.multiple_of(k * MID, MID), MID)
             part = dot_tn(mid_a2[...].reshape(rows_all, MID), big3[:, :, span].reshape(rows_all, MID))
             g_out[:, span] = part.astype(BF16)
             return carry
 
-        lax.fori_loop(0, D // MID, body, 0)
-
-    def task_in():
-        ready("in")
-
-        def body(k, carry):
+        lax.fori_loop(first, last, body, 0)
+
+    def task_in(first, last):
+        def body(i, carry):
+            k = i + turn * (3 - 2 * i)
             span = pl.ds(pl.multiple_of(k * MID, MID), MID)
             part = dot_tn(bigx[:, :, span].reshape(rows_all, MID), mid_d1[...].reshape(rows_all, MID))
             g_in[span, :] = part.astype(BF16)
             return carry
 
-        lax.fori_loop(0, D // MID, body, 0)
+        lax.fori_loop(first, last, body, 0)
 
     def task_mid(first, last):
-        if first == 0:
-            ready("mid")
-
-        def body(k, carry):
+        def body(i, carry):
+            k = i + turn * (8 - 2 * i)
             window = fpad[pl.ds(k // 3, GRID), pl.ds(lax.rem(k, 3), GRID)].reshape(rows_all, MID)
             part = dot_tn(window, mid_d2[...].reshape(rows_all, MID))
             g_mid[pl.ds(pl.multiple_of(k * MID, MID), MID), :] = part.astype(BF16)
@@ -1253,7 +1290,6 @@
         lax.fori_loop(first, last, body, 0)
 
     def task_small(block):
-        ready("small")
         part = dot_tn(mid_low[...].reshape(rows_all, MID), thin_dr[...].reshape(rows_all, GATE))
         g_small[:, 32 * block : 32 * block + 16, :] = part.astype(BF16).reshape(devices, 16, LANES)
         part = dot_tn(thin_s[...].reshape(rows_all, GATE), mid_de[...].reshape(rows_all, MID)).astype(BF16)
@@ -1262,37 +1298,40 @@
             rows = rows + dot_tn(excite_pick(devices, k), part[:, k * LANES : (k + 1) * LANES])
         g_small[:, 32 * block + 16 : 32 * block + 32, :] = rows.astype(BF16).reshape(devices, 16, LANES)
 
+    def run(piece):
+        letter = piece[-1] if piece[-1] in "abc" else ""
+        kind, block = piece[: len(piece) - 1 - len(letter)], int(piece[len(piece) - 1 - len(letter)])
+        part = "abc".index(letter) if letter else 0
+        if part == 0:
+            for copy in waits[kind]:
+                copy.wait()
+            if block == 0 and kind != "small":
+                for name in SCATTERED:
+                    if name.startswith(kind) and name[-1] == "1":
+                        while jobs[name].at < 1:
+                            jobs[name].advance()
+        if kind == "mid":
+            task_mid(3 * part, 3 * part + 3)
+        elif kind == "in":
+            task_in(2 * part, 2 * part + 2)
+        elif kind == "out":
+            task_out(2 * part, 2 * part + 2)
+        else:
+            task_small(block)
+        if block == 1 and part == {"mid": 2, "in": 1, "out": 1, "small": 0}[kind]:
+            waits[kind] = fetch(0, *operands[kind])
+        if block == 1 and piece == ORDER_FIRST:
+            for other in ("in", "mid", "small"):
+                waits[other] = fetch(1, *operands[other])
+
     g_small[:, 64:80, :] = norm_rows_in[...]
     load_cls.wait()
-    push("cls")
-    task_out()
-    push("cls", "out1")
-    waits["out"] = fetch(0, "a2", "d3")
-    task_mid(0, 4)
-    push("cls", "out1")
-    task_mid(4, 9)
-    push("cls", "out1", "mida1", "midb1")
-    waits["mid"] = fetch(0, "f", "d2")
-    task_small(1)
-    waits["small"] = fetch(0, "low", "dr", "s", "de")
-    push("out1", "mida1", "midc1")
-    task_in()
-    push("cls", "out1", "midb1", "mida1", "in1")
-    waits["in"] = fetch(0, "x", "d1")
-    task_out()
-    push("midc1", "midb1", "mida1", "in1", "out0")
-    task_mid(0, 4)
-    push("mida1", "midc1", "midb1", "in1", "out0")
-    task_mid(4, 9)
-    push("midb1", "midc1", "in1", "out0", "mida0", "midb0")
-    task_small(0)
-    push("midc1", "in1", "out0", "mida0", "midc0")
-    task_in()
-    push("out0", "midb0", "mida0", "in0")
-    push("midc0", "midb0", "mida0", "in0", "small")
-    push("mida0", "midc0", "midb0", "in0", "small")
-    push("midb0", "midc0", "in0", "small")
-    push("midc0", "in0", "small")
+    for item in ORDER:
+        if item[0] == "@":
+            with jax.named_scope("product"):
+                run(item[1:])
+        else:
+            push(item)
     for name in SCATTERED:
         while jobs[name].at <= 3:
             jobs[name].advance()

time: 557 us -> 499 us (0.90)
  Pallas kernels: 485 us -> 423 us
    pallas_call x2, Pallas kernels: 203 us -> 171 us  [forward_block(): pl.pallas_call(functools.partial(forward_kernel, n_seg, n_clip, block, jo...]
    pallas_call x1, Pallas kernels: 142 us -> 111 us  [gradient_sums(): pl.pallas_call(functools.partial(gradient_kernel, n_seg, n_clip), out_sha...]
where the time goes in v5:
time: 499 us; the launch traced here: 490 us
  Pallas kernels  423 us (85%)
  local copies, waits for them, and re-layouts  49.6 us (10%)
  other arithmetic  7.81 us (2%)
    pallas_call x2, Pallas kernels, forward_block(): pl.pallas_call(functools.partial(forward_kernel, n_seg, n_clip, block, jo...  171 us
    pallas_call x2, Pallas kernels, backward_block(): pl.pallas_call(functools.partial(backward_kernel, n_seg, n_clip, block),...  140 us
    pallas_call x1, Pallas kernels, gradient_sums(): pl.pallas_call(functools.partial(gradient_kernel, n_seg, n_clip), out_sha...  111 us
    unnamed x36, local copies, waits for them, and re-layouts  22.7 us
    concatenate x1, local copies, waits for them, and re-layouts, on_device(): grad_mine = jnp.concatenate(mine)  10.6 us

profile of v5, /device:TPU:0, one launch (start us, length us, event | category | flops | bytes accessed | tf_op | source)
XLA Modules:
  0.0 489.6 jit_solution(3961160759059098466)
XLA Ops:
  0.6 1.3 convert_element_type.86
  2.0 0.1 slice_bitcast_fusion.16
  2.1 0.1 fusion.19
  2.2 0.1 constant_dynamic-update-slice_fusion.2
  2.3 0.1 fusion.17
  2.5 0.1 reshape.253
  2.6 0.7 slice_bitcast_fusion.6
  3.3 0.1 fusion.18
  3.4 0.1 reshape.248
  3.5 0.1 reshape.256
  3.6 0.7 slice_bitcast_fusion
  4.3 0.1 lt.49
  4.4 0.1 lt.57
  4.5 0.1 lt.54
  4.6 0.1 lt.50
  4.7 0.1 lt.51
  4.7 0.7 broadcast_in_dim.16.refs_1_.refs_17_
  5.5 0.7 reshape.252.refs_10_
  6.1 0.7 broadcast_in_dim.17.refs_2_.refs_19_
  6.8 6.7 %copy.53 = bf16[4,8,49,2048]{3,1,0,2:T(8,128)(2,1)} copy(bf16[4,8,49,2048]{3,1,2,0:T(8,128)(2,1)} %param.6) | data formatting | bytes 12845056 | tf_op args[0]
  13.5 0.6 broadcast_in_dim.18.refs_3_
  14.1 110.8 %forward_block.2 = (bf16[1024,512]{1,0:T(8,128)(2,1)}, bf16[2560,128]{1,0:T(8,128)(2,1)}, bf16[1024,512]{1,0:T(8,128)(2,1)}, bf16[1536,512]{1,0:T(8,128)(2,1)}, ...) custom-call(bf16[49,32,2048]{2,1,0:T(8,128)(2,1)} %bitcast.126, ...), custom_call_target="tpu_custom_call" | custom-call | tf_op jit(solution)/shard_map/forward_block/pallas_call | solution.py:753
  124.9 0.7 reshape.260.refs_4_
  125.6 0.2 reshape.261
  125.7 0.6 pad.71.refs_5_
  126.4 60.5 %forward_block.3 = (bf16[512,2048]{1,0:T(8,128)(2,1)}, bf16[2048,256]{1,0:T(8,128)(2,1)}, f32[49,32,512]{2,1,0:T(8,128)}, bf16[49,32,512]{2,1,0:T(8,128)(2,1)}, ...) custom-call(bf16[49,32,2048]{2,1,0:T(8,128)(2,1)} %get-tuple-element, ...), custom_call_target="tpu_custom_call" | custom-call | tf_op jit(solution)/shard_map/forward_block/pallas_call | solution.py:753
  186.9 1.1 bitcast_reduce_fusion
  188.0 3.4 psum.7
  191.4 0.8 slice.213
  192.2 0.1 reshape.282
  192.4 1.6 fusion.21
  194.0 0.2 fusion.6
  194.2 0.4 convolution_divide_fusion
  194.6 0.8 bitcast_multiply_fusion.refs_2_
  195.4 0.7 slice.169.refs_18_
  196.1 68.4 %backward_block.2 = (bf16[49,32,2048]{2,1,0:T(8,128)(2,1)}, bf16[7,7,32,512]{3,2,1,0:T(8,128)(2,1)}, bf16[49,32,512]{2,1,0:T(8,128)(2,1)}, bf16[49,32,128]{2,1,0...) custom-call(bf16[49,32,2048]{2,1,0:T(8,128)(2,1)} %get-tuple-element.78.refs_0_, ...), custom_call_target="tpu_custom_call" | custom-call | tf_op jit(solution)/shard_map/backward_block/pallas_call | solution.py:1053
  264.5 71.8 %backward_block.3 = (bf16[49,32,2048]{2,1,0:T(8,128)(2,1)}, bf16[7,7,32,512]{3,2,1,0:T(8,128)(2,1)}, bf16[49,32,512]{2,1,0:T(8,128)(2,1)}, bf16[49,32,128]{2,1,0...) custom-call(bf16[49,32,2048]{2,1,0:T(8,128)(2,1)} %get-tuple-element.69.refs_0_, ...), custom_call_target="tpu_custom_call" | custom-call | tf_op jit(solution)/shard_map/backward_block/pallas_call | solution.py:1053
  336.3 11.8 %copy.42 = f32[4,8,49,2048]{3,1,2,0:T(8,128)} copy(f32[4,8,49,2048]{3,1,0,2:T(8,128)} %bitcast.129) | data formatting | bytes 25690112
  348.1 0.1 fusion.11
  348.2 0.1 reshape.264
  348.4 0.1 div.89
  348.5 0.1 div.91
  348.6 0.1 div.93
  348.8 0.1 div.95
  348.9 0.1 stack.53
  349.0 0.7 pad.79.refs_21_
  349.7 0.6 pad_bitcast_fusion.5.refs_22_
  350.3 0.6 fusion
  350.8 1.1 pad.72.refs_20_
  352.0 111.3 %gradient_sums.1 = (f32[64,512]{1,0:T(8,128)}, f32[144,512]{1,0:T(8,128)}, f32[16,2048]{1,0:T(8,128)}, f32[64,512]{1,0:T(8,128)}, f32[144,512]{1,0:T(8,128)}, /*...) custom-call(bf16[49,32,2048]{2,1,0:T(8,128)(2,1)} %bitcast.128, ...), custom_call_target="tpu_custom_call" | custom-call | tf_op jit(solution)/shard_map/gradient_sums/pallas_call | solution.py:1375
  463.4 1.1 copy.46
  464.5 1.0 copy.49
  465.5 0.9 copy.45
  466.5 0.9 copy.47
  467.5 0.2 reshape.278
  467.7 0.6 fusion.20
  468.3 0.6 copy.40
  468.9 0.6 copy.41
  469.5 0.6 slice_bitcast_fusion.21
  470.1 0.5 slice_bitcast_fusion.20
  470.6 10.6 %concatenate.7 = f32[298246]{0:T(1024)S(1)} concatenate(f32[32768]{0:T(1024)S(1)} %bitcast.133, f32[73728]{0:T(1024)S(1)} %bitcast.131, f32[32768]{0:T(1024)S(1)} %bitcast.134, f32[2048]{0:T(1024)} %get-tuple-element.185, f32[2048]{0:T(1024)} %bitcast.144, f32[96]{0:T(128)} %get-tuple-element.181, f32[96]{0:T(128)} %get-tuple-element.180, f32[32768]{0:T(1024)S(1)} %bitcast.135, ...), dimensions={0} | concatenate | bytes 2385968 | tf_op jit(solution)/shard_map/concatenate | solution.py:1499
  481.2 1.2 slice.184
  483.2 4.2 fusion.15
  487.4 0.6 slice.186
  (61 shorter events, 0.5 us)
Async XLA Ops:
  2.0 2.6 copy-start.9
  2.3 11.1 %copy-start.5 = (bf16[80,128]{1,0:T(8,128)(2,1)}, bf16[80,128]{1,0:T(8,128)(2,1)S(1)}, u32[]{:S(2)}) copy-start(bf16[80,128]{1,0:T(8,128)(2,1)S(1)} %constant_dynamic-update-slice_fusion.refs_5_) | copy-start | bytes 61444
  186.9 7.3 %copy-start.10 = (s32[4]{0:T(128)S(1)}, s32[4]{0:T(128)}, u32[]{:S(2)}) copy-start(s32[4]{0:T(128)} %param.8) | copy-start | bytes 52
  186.9 7.3 %copy-start.11 = (bf16[2048,256]{1,0:T(8,128)(2,1)S(1)}, bf16[2048,256]{1,0:T(8,128)(2,1)}, u32[]{:S(2)}) copy-start(bf16[2048,256]{1,0:T(8,128)(2,1)} %get-tuple-element.80) | copy-start | bytes 3145732
  336.3 12.1 %copy-start.7 = (f32[48,128]{1,0:T(8,128)S(1)}, f32[48,128]{1,0:T(8,128)}, u32[]{:S(2)}) copy-start(f32[48,128]{1,0:T(8,128)} %get-tuple-element.119) | copy-start | bytes 73732
  336.3 12.3 %copy-start.6 = (f32[48,128]{1,0:T(8,128)S(1)}, f32[48,128]{1,0:T(8,128)}, u32[]{:S(2)}) copy-start(f32[48,128]{1,0:T(8,128)} %get-tuple-element.120) | copy-start | bytes 73732
  463.3 4.1 copy-start.2
  463.3 4.1 copy-start.1
  463.4 4.1 copy-start.3
  463.4 4.4 copy-start.4
  467.4 15.8 %copy-start = (f32[298246]{0:T(1024)S(1)}, f32[298246]{0:T(1024)}, u32[]{:S(2)}) copy-start(f32[298246]{0:T(1024)} %param.9) | copy-start | bytes 3578956
  483.2 4.2 copy-start.8

commit v6 on v5

--- a/solution.py
+++ b/solution.py
@@ -797,9 +797,21 @@
         copy.start()
         return copy
 
-    loads_one = [load(h3_hbm, h3v), load(x_hbm, xv)]
+    streams = [(h3_hbm, h3v), (x_hbm, xv)]
     if not last:
-        loads_one.append(load(d_in, dv))
+        streams.append((d_in, dv))
+    wide_base = links.take(len(streams) * GRID)
+
+    def wide_copies(i):
+        rows = pl.ds(GRID * i, GRID)
+        return [
+            pltpu.make_async_copy(source.at[rows], target.at[rows], links.recv_sem.at[wide_base + GRID * k + i])
+            for k, (source, target) in enumerate(streams)
+        ]
+
+    for i in range(GRID):
+        for copy in wide_copies(i):
+            copy.start()
     loads_two = [load(out_hbm, w_out), load(h2_hbm, h2v)]
     loads_three = [load(h1_hbm, h1v), load(gate_hbm, gatev), load(small_hbm, small)]
     loads_four = []
@@ -844,9 +856,12 @@
     def dot_t(left, right):
         return lax.dot_general(left, right, (((1,), (1,)), ((), ())), preferred_element_type=F32)
 
-    for copy in loads_one:
-        copy.wait()
     gain3, shift3, mean3, inv3 = vectors(2 * half, D, st3)
+
+    def first_rows(i, carry):
+        for copy in wide_copies(i):
+            copy.wait()
+        return lax.fori_loop(GRID * i, GRID * i + GRID, first, carry)
 
     def first(p, carry):
         for k in range(4):
@@ -860,7 +875,7 @@
             sum_shift[:, span] += fold(grad)
         return carry
 
-    lax.fori_loop(0, HW, first, 0)
+    lax.fori_loop(0, GRID, first_rows, 0)
     part_gain, part_shift = totals(0, 2 * half, D, sum_gain[...], sum_shift[...])
     factor3 = gain3 * inv3
     for copy in loads_two:
@@ -1047,7 +1062,7 @@
     ]
     for shape in ((8, MID), (8, LANES), (8, LANES)):
         scratch += sum_scratch(n_seg, n_clip, shape)
-    count = 3 * (n_seg * 4 + n_clip // 4) + 40
+    count = 3 * (n_seg * 4 + n_clip // 4) + 64
     scratch += [pltpu.SemaphoreType.DMA((count,)), pltpu.SemaphoreType.DMA((count,))]
     d_spec = vmem if last else any_spec
     return pl.pallas_call(
@@ -1159,6 +1174,11 @@
 }
 
 
+FLAT_MID = 256
+FLAT_OUT = 832
+FLAT_SMALL = 1088
+FLAT_ROWS = 1122
+FLAT_CLS = 2243
 ORDER = (
     "cls", "@out1a", "@out1b", "out1", "cls", "@in1a", "in1", "@in1b", "out1", "cls", "@mid1a", "in1", "@mid1b",
     "mida1", "midb1", "midc1", "@mid1c", "cls", "out1", "mida1", "@small1", "@in0a", "in0", "in1", "@in0b", "cls",
@@ -1183,12 +1203,9 @@
 
     sources = [pop(10) for _ in range(2)]
     cls_hbm, norm_rows_in, bias = pop(3)
-    out_refs = {}
-    for block in (0, 1):
-        out_refs["in%d" % block], out_refs["mid%d" % block], out_refs["out%d" % block] = pop(3)
-    out_refs["small"], out_refs["cls"], tail = pop(3)
+    flat, tail = pop(2)
     big3, bigx, mid_a2, mid_d2, mid_d1, mid_low, mid_de, thin_dr, thin_s, fpad = pop(10)
-    g_in, g_mid, g_out, g_small, g_cls, squares = pop(6)
+    g_in, g_mid, g_out, g_small, g_cls, squares, turned = pop(7)
     sums = pop(4)
     buffers = {name: pop(4) for name in SCATTERED}
     send_sem, recv_sem = pop(2)
@@ -1228,23 +1245,60 @@
     grads = {"cls": g_cls, "small": g_small}
     jobs = {}
 
+    def put(block, first, values, stride=1):
+        count = values.shape[0]
+        if block == 0:
+            flat[pl.ds(first, count, stride), :] = values
+        else:
+            turned[pl.ds(first + 8, count, stride), :] = pltpu.roll(values, 64, 1)
+
+    def put_small(total):
+        lane = lax.broadcasted_iota(jnp.int32, (1, LANES), 1)
+        for block in range(2):
+            rows = total[32 * block : 32 * block + 32]
+            put(block, FLAT_SMALL, rows[:16])
+            for k in range(4):
+                put(block, FLAT_SMALL + 16 + k, rows[16 + 4 * k : 20 + 4 * k], 4)
+            gain = total[64 + 2 * block : 65 + 2 * block]
+            shift = pltpu.roll(total[65 + 2 * block : 66 + 2 * block], 96, 1)
+            put(block, FLAT_SMALL + 32, jnp.where(lane < 96, gain, shift))
+            put(block, FLAT_SMALL + 33, shift)
+        flat[FLAT_CLS + 87 : FLAT_CLS + 88, :] = total[68:69]
+
+    def put_classifier(total):
+        lane = lax.broadcasted_iota(jnp.int32, (1, LANES), 1)
+        flat[FLAT_CLS:, :] = jnp.zeros_like(flat[FLAT_CLS:, :])
+        for i in range(total.shape[0]):
+            line, by = divmod(CLASSES * i, LANES)
+            line += FLAT_CLS
+            low, high = total[i : i + 1, :LANES], total[i : i + 1, LANES:]
+            if by:
+                low, high = pltpu.roll(low, by, 1), pltpu.roll(high, by, 1)
+            here = lane >= by
+            flat[line : line + 1, :] += jnp.where(here, low, 0.0)
+            flat[line + 1 : line + 2, :] += jnp.where(here, high, low)
+            if by + CLASSES - LANES > LANES:
+                flat[line + 2 : line + 3, :] += jnp.where(here, 0.0, high)
+
     def make(name):
         kind = name[:-1] if name not in ("cls", "small") else name
         block = name[-1]
         rows, columns = SCATTERED[name]
-        start = 0
-        if kind.startswith("mid"):
-            ref, shard_rows = g_mid, 3 * rows
-            start = rows * "abc".index(kind[3])
-            out = out_refs["mid" + block]
-        else:
-            ref = {"in": g_in, "out": g_out, "small": g_small, "cls": g_cls}[kind]
-            shard_rows = rows
-            out = out_refs[kind + block if kind in ("in", "out") else kind]
+        start = rows * "abc".index(kind[3]) if kind.startswith("mid") else 0
+        ref = {"in": g_in, "out": g_out, "small": g_small, "cls": g_cls}.get(kind, g_mid)
+        shard_rows = 3 * rows if kind.startswith("mid") else rows
 
         def finish(total):
-            out[start : start + rows, :] = total
             squares[:, :columns] += fold(total * total)
+            if kind == "cls":
+                put_classifier(total)
+            elif kind == "small":
+                put_small(total)
+            else:
+                lines = columns // LANES
+                first = {"in": 0, "out": FLAT_OUT}.get(kind, FLAT_MID) + start * lines
+                for k in range(lines):
+                    put(int(block), first + k, total[:, k * LANES : (k + 1) * LANES], lines)
 
         jobs[name] = Scatter(links, folded(ref, shard_rows), pl.ds(start, rows), buffers[name], finish)
 
@@ -1335,6 +1389,11 @@
     for name in SCATTERED:
         while jobs[name].at <= 3:
             jobs[name].advance()
+    lane = lax.broadcasted_iota(jnp.int32, (FLAT_ROWS, LANES), 1)
+    now, before = turned[8 : 8 + FLAT_ROWS, :], turned[7 : 7 + FLAT_ROWS, :]
+    old = flat[FLAT_SMALL + 33 : FLAT_SMALL + 34, :]
+    flat[FLAT_ROWS - 1 : 2 * FLAT_ROWS - 1, :] = jnp.where(lane < 64, before, now)
+    flat[FLAT_ROWS - 1 : FLAT_ROWS, :] = jnp.where(lane[:1] < 64, old, now[:1])
     total = jnp.sum(jnp.sum(squares[...], axis=0, keepdims=True), axis=1, keepdims=True)
     sums[0][0:8, :] = bias[...]
     sums[0][8:16, :] = jnp.broadcast_to(total, (8, LANES))
@@ -1352,10 +1411,7 @@
     def grid_shape(columns):
         return pltpu.VMEM((cells, frames, columns), BF16)
 
-    outs = []
-    for block in (0, 1):
-        outs += [(64, MID), (144, MID), (16, D)]
-    outs += [(80, LANES), (64, 2 * LANES), (16, LANES)]
+    outs = [(FLAT_CLS + 93, LANES), (16, LANES)]
     scratch = [grid_shape(D), grid_shape(D)] + [grid_shape(MID)] * 5 + [grid_shape(GATE)] * 2
     scratch += [
         pltpu.VMEM((GRID + 2, GRID + 2, frames, MID), BF16),
@@ -1365,6 +1421,7 @@
         pltpu.VMEM((SMALL_SHARDS, 80, LANES), BF16),
         pltpu.VMEM((D, 2 * LANES), BF16),
         pltpu.VMEM((8, D), F32),
+        pltpu.VMEM((FLAT_ROWS + 14, LANES), F32),
     ]
     scratch += sum_scratch(n_seg, n_clip, (16, LANES))
     for shape in SCATTERED.values():
@@ -1485,18 +1542,8 @@
         padded = jnp.pad(g_bias, (0, 6 * SMALL_SHARDS - CLASSES)).reshape(SMALL_SHARDS, 6)
         extra = norm_rows(vectors + [padded]).astype(BF16)
         cls_low = jnp.pad(g_cls.astype(BF16), ((0, 0), (0, 2 * LANES - CLASSES)))
-        *sums, tail = gradient_sums(sources, cls_low, extra, bias_rows)
-        mine = []
-        small = sums[6]
-        for block in (0, 1):
-            mine += [v.reshape(-1) for v in sums[3 * block : 3 * block + 3]]
-            mine.append(small[32 * block : 32 * block + 16].reshape(-1))
-            turned = small[32 * block + 16 : 32 * block + 32].reshape(MID // LANES, -1, LANES)
-            mine.append(jnp.swapaxes(turned, 0, 1).reshape(-1))
-            mine.append(small[64 + 2 * block, :96])
-            mine.append(small[65 + 2 * block, :96])
-        mine += [sums[7][:, :CLASSES].reshape(-1), small[68, :6]]
-        grad_mine = jnp.concatenate(mine)
+        flat, tail = gradient_sums(sources, cls_low, extra, bias_rows)
+        grad_mine = flat.reshape(-1)[: master.shape[0]]
     norm = jnp.sqrt(tail[8, 0])
     bias_grad = tail[:8].reshape(-1)[:CLASSES]
     factor = jnp.minimum(1.0, CLIP_LIMIT / (norm + 1e-06))

time: 499 us -> 474 us (0.950)
  local copies, waits for them, and re-layouts: 49.6 us -> 31.9 us
  Pallas kernels: 423 us -> 416 us
    concatenate x1 -> x0, local copies, waits for them, and re-layouts: 10.6 us -> none  [on_device(): grad_mine = jnp.concatenate(mine)]
    pallas_call x2, Pallas kernels: 140 us -> 132 us  [backward_block(): pl.pallas_call(functools.partial(backward_kernel, n_seg, n_clip, block),...]
    unnamed x36 -> x22, local copies, waits for them, and re-layouts: 22.7 us -> 18.6 us
where the time goes in v6:
time: 474 us; the launch traced here: 465 us
  Pallas kernels  416 us (88%)
  local copies, waits for them, and re-layouts  31.9 us (7%)
  other arithmetic  8.17 us (2%)
    pallas_call x2, Pallas kernels, forward_block(): pl.pallas_call(functools.partial(forward_kernel, n_seg, n_clip, block, jo...  171 us
    pallas_call x2, Pallas kernels, backward_block(): pl.pallas_call(functools.partial(backward_kernel, n_seg, n_clip, block),...  132 us
    pallas_call x1, Pallas kernels, gradient_sums(): pl.pallas_call(functools.partial(gradient_kernel, n_seg, n_clip), out_sha...  112 us
    unnamed x22, local copies, waits for them, and re-layouts  18.6 us

profile of v6, /device:TPU:0, one launch (start us, length us, event | category | flops | bytes accessed | tf_op | source)
XLA Modules:
  0.0 464.8 jit_solution(2459020250759715632)
XLA Ops:
  0.6 1.3 convert_element_type.86
  2.0 0.0 copy-start.5
  2.0 0.1 slice_bitcast_fusion.14
  2.1 0.1 fusion.19
  2.2 0.1 constant_dynamic-update-slice_fusion.2
  2.3 0.1 fusion.17
  2.5 0.1 reshape.205
  2.5 0.1 reshape.217
  2.6 0.7 slice_bitcast_fusion.6
  3.3 0.1 fusion.18
  3.4 0.1 reshape.212
  3.5 0.1 reshape.220
  3.6 0.7 slice_bitcast_fusion
  4.3 0.1 lt.49
  4.4 0.1 lt.57
  4.5 0.1 lt.54
  4.6 0.0 copy-done.5
  4.6 0.1 lt.50
  4.6 0.1 lt.51
  4.7 0.7 broadcast_in_dim.16.refs_1_.refs_17_
  5.4 0.7 reshape.216.refs_10_
  6.1 0.7 broadcast_in_dim.17.refs_2_.refs_19_
  6.8 6.7 %copy.43 = bf16[4,8,49,2048]{3,1,0,2:T(8,128)(2,1)} copy(bf16[4,8,49,2048]{3,1,2,0:T(8,128)(2,1)} %param.6) | data formatting | bytes 12845056 | tf_op args[0]
  13.5 0.0 copy-done.1
  13.5 0.6 broadcast_in_dim.18.refs_3_
  14.2 110.9 %forward_block.2 = (bf16[1024,512]{1,0:T(8,128)(2,1)}, bf16[2560,128]{1,0:T(8,128)(2,1)}, bf16[1024,512]{1,0:T(8,128)(2,1)}, bf16[1536,512]{1,0:T(8,128)(2,1)}, ...) custom-call(bf16[49,32,2048]{2,1,0:T(8,128)(2,1)} %bitcast.92, ...), custom_call_target="tpu_custom_call" | custom-call | tf_op jit(solution)/shard_map/forward_block/pallas_call | solution.py:753
  125.0 0.7 reshape.224.refs_4_
  125.7 0.2 reshape.225
  125.9 0.6 pad.71.refs_5_
  126.5 60.6 %forward_block.3 = (bf16[512,2048]{1,0:T(8,128)(2,1)}, bf16[2048,256]{1,0:T(8,128)(2,1)}, f32[49,32,512]{2,1,0:T(8,128)}, bf16[49,32,512]{2,1,0:T(8,128)(2,1)}, ...) custom-call(bf16[49,32,2048]{2,1,0:T(8,128)(2,1)} %get-tuple-element, ...), custom_call_target="tpu_custom_call" | custom-call | tf_op jit(solution)/shard_map/forward_block/pallas_call | solution.py:753
  187.1 0.0 copy-start.6
  187.1 0.0 copy-start.7
  187.2 1.1 bitcast_reduce_fusion
  188.3 3.4 psum.7
  191.6 0.8 slice.177
  192.5 0.1 reshape.234
  192.6 1.6 fusion.20
  194.2 0.2 fusion.6
  194.4 0.0 copy-done.6
  194.4 0.0 copy-done.7
  194.4 0.4 convolution_divide_fusion
  194.8 0.8 bitcast_multiply_fusion.refs_2_
  195.6 0.7 slice.142.refs_18_
  196.3 66.1 %backward_block.2 = (bf16[49,32,2048]{2,1,0:T(8,128)(2,1)}, bf16[7,7,32,512]{3,2,1,0:T(8,128)(2,1)}, bf16[49,32,512]{2,1,0:T(8,128)(2,1)}, bf16[49,32,128]{2,1,0...) custom-call(bf16[49,32,2048]{2,1,0:T(8,128)(2,1)} %get-tuple-element.71.refs_0_, ...), custom_call_target="tpu_custom_call" | custom-call | tf_op jit(solution)/shard_map/backward_block/pallas_call | solution.py:1068
  262.4 66.4 %backward_block.3 = (bf16[49,32,2048]{2,1,0:T(8,128)(2,1)}, bf16[7,7,32,512]{3,2,1,0:T(8,128)(2,1)}, bf16[49,32,512]{2,1,0:T(8,128)(2,1)}, bf16[49,32,128]{2,1,0...) custom-call(bf16[49,32,2048]{2,1,0:T(8,128)(2,1)} %get-tuple-element.62.refs_0_, ...), custom_call_target="tpu_custom_call" | custom-call | tf_op jit(solution)/shard_map/backward_block/pallas_call | solution.py:1068
  328.8 0.0 copy-start.3
  328.8 0.0 copy-start.2
  328.8 11.8 %copy.38 = f32[4,8,49,2048]{3,1,2,0:T(8,128)} copy(f32[4,8,49,2048]{3,1,0,2:T(8,128)} %bitcast.95) | data formatting | bytes 25690112
  340.6 0.1 fusion.11
  340.7 0.1 reshape.228
  340.9 0.0 copy-done.3
  340.9 0.1 div.89
  341.0 0.1 div.91
  341.1 0.1 div.93
  341.3 0.1 div.95
  341.4 0.1 stack.53
  341.5 0.7 pad.79.refs_21_
  342.2 0.6 pad_bitcast_fusion.5.refs_22_
  342.8 0.6 fusion
  343.4 1.1 pad.72.refs_20_
  344.5 111.7 %gradient_sums.1 = (f32[2336,128]{1,0:T(8,128)}, f32[16,128]{1,0:T(8,128)}) custom-call(bf16[49,32,2048]{2,1,0:T(8,128)(2,1)} %bitcast.94, bf16[49,32,512]{2,1,0:T(8,128)(2,1)} %get-tuple-element.94.refs_1_, bf16[7,7,32,512]{3,2,1,0:T(8,128)(2,1)} %get-tuple-element.95.refs_2_, bf16[7,7,32,512]{3,2,1,0:T(8,128)(2,1)} %get-tuple-element.96.refs_3_, ...), custom_call_target="tpu_custom_call" | custom-call | tf_op jit(solution)/shard_map/gradient_sums/pallas_call | solution.py:1432
  456.2 1.2 slice.148
  458.1 4.6 fusion.15
  462.7 0.6 slice.150
  (40 shorter events, 0.3 us)
Async XLA Ops:
  2.0 2.6 copy-start.5
  2.3 11.2 %copy-start.1 = (bf16[80,128]{1,0:T(8,128)(2,1)}, bf16[80,128]{1,0:T(8,128)(2,1)S(1)}, u32[]{:S(2)}) copy-start(bf16[80,128]{1,0:T(8,128)(2,1)S(1)} %constant_dynamic-update-slice_fusion.refs_5_) | copy-start | bytes 61444
  187.1 7.3 %copy-start.6 = (s32[4]{0:T(128)S(1)}, s32[4]{0:T(128)}, u32[]{:S(2)}) copy-start(s32[4]{0:T(128)} %param.8) | copy-start | bytes 52
  187.1 7.3 %copy-start.7 = (bf16[2048,256]{1,0:T(8,128)(2,1)S(1)}, bf16[2048,256]{1,0:T(8,128)(2,1)}, u32[]{:S(2)}) copy-start(bf16[2048,256]{1,0:T(8,128)(2,1)} %get-tuple-element.73) | copy-start | bytes 3145732
  328.8 12.1 %copy-start.3 = (f32[48,128]{1,0:T(8,128)S(1)}, f32[48,128]{1,0:T(8,128)}, u32[]{:S(2)}) copy-start(f32[48,128]{1,0:T(8,128)} %get-tuple-element.112) | copy-start | bytes 73732
  328.8 12.3 %copy-start.2 = (f32[48,128]{1,0:T(8,128)S(1)}, f32[48,128]{1,0:T(8,128)}, u32[]{:S(2)}) copy-start(f32[48,128]{1,0:T(8,128)} %get-tuple-element.113) | copy-start | bytes 73732
  344.5 113.6 %copy-start = (f32[298246]{0:T(1024)S(1)}, f32[298246]{0:T(1024)}, u32[]{:S(2)}) copy-start(f32[298246]{0:T(1024)} %param.9) | copy-start | bytes 3578956
  458.1 4.6 copy-start.4

commit v7 on v6

--- a/solution.py
+++ b/solution.py
@@ -388,6 +388,7 @@
 
 
 SMALL_SHARDS = 32
+SLOTS_HERE = 8
 TABLE = ((2 * MID + D) // LANES + 1, 8, LANES)
 
 
@@ -420,16 +421,18 @@
 
     last = block == 1
     x_hbm, mask, following, table_in = pop(4)
+    share, chosen = pop(2) if last else (None, None)
     shards = dict(zip(jobs, [pop() for _ in jobs]))
     given = dict(zip(plan, [pop() for _ in plan]))
     wholes = dict(zip(jobs, [pop() for _ in jobs]))
     h1_out, low_out, gate_out, mix_out, f_out, h2_out, a2_out, h3_out = pop(8)
     out_hbm, table_out, st1, st2, st3 = pop(5)
+    g_cls, g_bias = pop(2) if last else (None, None)
     xv, w_in, w_mid, w_out, small = pop(5)
     h1v, a1v, lowv, rv, edge, dpad, mixv, gatev, fpad, h2v, a2v, h3v = pop(12)
     wide_sum, wide_square, w_exp = pop(3)
     sums = [pop(4) for _ in range(3)]
-    pooled = pop() if last else None
+    pooled, clip_sums, clip_other, w_cls = pop(4) if last else [None] * 4
     send_sem, recv_sem = pop(2)
     links = Links(n_seg, n_clip, send_sem, recv_sem)
     frames = xv.shape[1]
@@ -442,11 +445,19 @@
         outgoing.append(copy)
 
     links.meet()
-    load_x = links.local(x_hbm, xv)
-    load_x.start()
+    x_base = links.take(GRID)
+
+    def load_x(i):
+        rows = pl.ds(GRID * i, GRID)
+        return pltpu.make_async_copy(x_hbm.at[rows], xv.at[rows], links.recv_sem.at[x_base + i])
+
+    for i in range(GRID):
+        load_x(i).start()
     gathers = {name: Gather(links, shards[name], wholes[name]) for name in jobs}
 
     targets = {"out%d" % block: w_out, "small": small}
+    if last:
+        targets["cls"] = w_cls
     for kind, target, count in (("in", w_in, 2), ("mid", w_mid, 3)):
         rows = target.shape[0] // SMALL_SHARDS
         size = rows // count
@@ -473,7 +484,7 @@
         for name in names:
             loads[name].wait()
 
-    for name in weight_names(block):
+    for name in targets:
         if name not in gathers:
             load(name)
     table = table_in if last else table_out
@@ -500,6 +511,7 @@
     kept = {}
 
     def first(i, carry):
+        load_x(i).wait()
         part = matmul(xv[pl.ds(GRID * i, GRID)].reshape(GRID * frames, D), w_in[...])
         h1v[pl.ds(GRID * i, GRID)] = part.reshape(GRID, frames, MID)
         one, two = masked_sums(part)
@@ -523,7 +535,6 @@
 
     def stage_first():
         need(*piece_names("in", block, 2))
-        load_x.wait()
         stat = put_sums(0, *lax.fori_loop(0, GRID, first, (zeros, zeros)))
         present = HW * jnp.sum(mask[:, :LANES], axis=0, keepdims=True)
         stat[8:16, :] = jnp.broadcast_to(present, (8, LANES))
@@ -660,7 +671,45 @@
 
     def stage_fifth():
         lax.fori_loop(0, HW, fifth, 0)
+        if last:
+            classify()
         send_out(pooled if last else xv, out_hbm)
+
+    def classify():
+        clips = frames // SLOTS_HERE
+        clip_sums[...] = jnp.zeros_like(clip_sums)
+        for c in range(clips):
+            rows = pooled[SLOTS_HERE * c : SLOTS_HERE * (c + 1), :]
+            clip_sums[c : c + 1, :] = jnp.sum(rows, axis=0, keepdims=True)
+        swap = links.remote(links.take(1), clip_sums, clip_other, links.other)
+        swap.start()
+        lane = lax.broadcasted_iota(jnp.int32, (1, 2 * LANES), 1)
+        bias = jnp.zeros((1, 2 * LANES), F32)
+        for d in range(SMALL_SHARDS):
+            piece = small[d, 64:80, :].astype(F32)[4:5]
+            piece = jnp.concatenate([piece, jnp.zeros_like(piece)], axis=1)
+            own = jnp.logical_and(lane >= 6 * d, lane < 6 * d + 6)
+            bias = bias + jnp.where(own, pltpu.roll(piece, 6 * d, 1) if d else piece, 0.0)
+        need("cls")
+        swap.wait()
+        mean = (clip_sums[...] + clip_other[...]) * share[:, 0:1]
+        low = jnp.concatenate([mean, jnp.zeros_like(mean)], axis=0).astype(BF16)
+        scores = matmul(low, w_cls[...])[:8] + bias
+        scores = jnp.where(lane < CLASSES, scores, -1e30)
+        scores = jnp.exp(scores - jnp.max(scores, axis=1, keepdims=True))
+        chance = scores / jnp.sum(scores, axis=1, keepdims=True)
+        clips_total = clips * links.n_clip
+        d_scores = jnp.where(share[:, 0:1] > 0.0, (chance - chosen[...]) / clips_total, 0.0)
+        g_bias[...] = jnp.broadcast_to(jnp.sum(d_scores, axis=0, keepdims=True) / n_seg, g_bias.shape)
+        d_low = jnp.concatenate([d_scores, jnp.zeros_like(d_scores)], axis=0).astype(BF16)
+        grad = lax.dot_general(low, d_low, (((0,), (0,)), ((), ())), preferred_element_type=F32)
+        g_cls[...] = (grad / n_seg).astype(BF16)
+        d_mean = lax.dot_general(d_low, w_cls[...], (((1,), (1,)), ((), ())), preferred_element_type=F32)
+        d_mean = d_mean[:8] * share[:, 0:1]
+        for c in range(clips):
+            rows = slice(SLOTS_HERE * c, SLOTS_HERE * (c + 1))
+            here = mask[rows, 0:1]
+            pooled[rows, :] = jnp.broadcast_to(d_mean[c : c + 1], (SLOTS_HERE, D)) * here
 
     stages = {
         "dpad": stage_dpad,
@@ -691,7 +740,7 @@
         copy.wait()
 
 
-def forward_block(block, x, mask, following, table, shards, given):
+def forward_block(block, x, mask, following, table, extra, shards, given):
     n_seg = lax.axis_size("seg")
     n_clip = lax.axis_size("clip")
     cells, frames, width = x.shape
@@ -723,6 +772,9 @@
         jax.ShapeDtypeStruct((8, D), F32),
     ]
     out_specs = [any_spec] * (len(jobs) + 9) + [vmem] * 4
+    if last:
+        outs += [jax.ShapeDtypeStruct((D, 2 * LANES), BF16), jax.ShapeDtypeStruct((8, 2 * LANES), F32)]
+        out_specs += [vmem] * 2
 
     shapes = [(D, MID), (9 * MID, MID), (MID, D), (SMALL_SHARDS, 80, LANES)]
     scratch = [pltpu.VMEM(x.shape, BF16)]
@@ -747,20 +799,21 @@
     for shape in ((16, LANES), (8, LANES), (8, MID)):
         scratch += sum_scratch(n_seg, n_clip, shape)
     if last:
-        scratch.append(pltpu.VMEM((frames, D), F32))
-    count = 4 * (n_seg * 4 + depth) + len(jobs) * (depth + 4) + 32
+        scratch += [pltpu.VMEM((frames, D), F32), pltpu.VMEM((8, D), F32), pltpu.VMEM((8, D), F32)]
+        scratch.append(pltpu.VMEM((D, 2 * LANES), BF16))
+    count = 4 * (n_seg * 4 + depth) + len(jobs) * (depth + 4) + 48
     scratch += [pltpu.SemaphoreType.DMA((count,)), pltpu.SemaphoreType.DMA((count,))]
     results = pl.pallas_call(
         functools.partial(forward_kernel, n_seg, n_clip, block, jobs, plan),
         out_shape=outs,
-        in_specs=[any_spec, vmem, vmem, vmem] + [any_spec] * (len(jobs) + len(plan)),
+        in_specs=[any_spec, vmem, vmem, vmem] + [vmem] * len(extra) + [any_spec] * (len(jobs) + len(plan)),
         out_specs=out_specs,
         scratch_shapes=scratch,
         compiler_params=pltpu.CompilerParams(
             collective_id=30 + block, has_side_effects=True, vmem_limit_bytes=60 * 1024 * 1024
         ),
         name="forward_block",
-    )(x, mask, following, table, *[shards[n] for n in jobs], *[given[n] for n in plan])
+    )(x, mask, following, table, *extra, *[shards[n] for n in jobs], *[given[n] for n in plan])
     wholes = dict(zip(jobs, results[: len(jobs)]))
     return wholes, results[len(jobs) :]
 
@@ -1079,8 +1132,9 @@
 
 
 class Scatter:
-    def __init__(self, links, grad, rows, buffers, finish):
+    def __init__(self, links, grad, rows, buffers, alternate, finish):
         self.links = links
+        self.alternate = alternate
         self.grad = grad
         self.rows = rows
         self.one, self.two, self.three, self.four = buffers
@@ -1094,16 +1148,24 @@
         if self.at == 0:
             source = self.grad.at[1 - links.seg, :, :, self.rows]
             return [links.remote(base, source, self.one, links.other)]
+        found = []
         if self.at == 1:
-            found = []
             for k in range(2):
                 source = self.one.at[:, links.jump * (1 - links.first) + links.step * k]
                 found.append(links.remote(base + 1 + k, source, self.two.at[:, k], links.across_first))
             return found
+        if self.alternate:
+            if self.at == 2:
+                for i in range(1, depth):
+                    source = self.two.at[lax.rem(links.group + i, depth)]
+                    found.append(links.remote(base + 2 + i, source, self.three.at[i - 1], links.far_peer(i)))
+            else:
+                source = self.four.at[1 - links.second]
+                found.append(links.remote(base + depth + 2, source, self.four.at[2], links.across_second))
+            return found
         if self.at == 2:
             source = self.two.at[:, 1 - links.second]
             return [links.remote(base + 3, source, self.three, links.across_second)]
-        found = []
         for i in range(1, depth):
             source = self.three.at[lax.rem(links.group + i, depth)]
             found.append(links.remote(base + 3 + i, source, self.four.at[i - 1], links.far_peer(i)))
@@ -1132,6 +1194,12 @@
                 return carry
 
             lax.fori_loop(0, 2 * depth, add_two, 0)
+        elif self.at == 2 and self.alternate:
+            for k in range(2):
+                total = two[links.group, k].astype(F32)
+                for i in range(1, depth):
+                    total = total + three[i - 1, k].astype(F32)
+                four[k] = total.astype(BF16)
         elif self.at == 2:
 
             def add_three(z, carry):
@@ -1139,6 +1207,8 @@
                 return carry
 
             lax.fori_loop(0, depth, add_three, 0)
+        elif self.alternate:
+            self.finish(four[links.second].astype(F32) + four[2].astype(F32))
         else:
             total = three[links.group].astype(F32)
             for i in range(1, depth):
@@ -1180,17 +1250,17 @@
 FLAT_ROWS = 1122
 FLAT_CLS = 2243
 ORDER = (
-    "cls", "@out1a", "@out1b", "out1", "cls", "@in1a", "in1", "@in1b", "out1", "cls", "@mid1a", "in1", "@mid1b",
-    "mida1", "midb1", "midc1", "@mid1c", "cls", "out1", "mida1", "@small1", "@in0a", "in0", "in1", "@in0b", "cls",
-    "out1", "midb1", "midc1", "@mid0a", "mida1", "@mid0b", "mida0", "midb0", "midc0", "out1", "in1", "@mid0c",
-    "midb1", "@small0", "small", "in0", "@out0a", "midc1", "mida1", "in1", "@out0b", "out0", "midb1", "mida0",
-    "mida1", "out0", "in0", "midc1", "midb1", "mida0", "midc1", "midb0", "out0", "in0", "mida0", "midc0", "midb0",
-    "in0", "out0", "small", "mida0", "midc0", "midb0", "small", "out0", "midc0", "small", "midb0", "midc0",
-    "small",
+    "cls", "@mid1a", "cls", "@mid1b", "mida1", "midb1", "midc1", "@mid1c", "cls", "mida1", "@in1a", "in1", "@in1b",
+    "cls", "midb1", "@out1a", "mida1", "midc1", "@out1b", "out1", "cls", "@small1", "in1", "midb1", "out1",
+    "@out0a", "midc1", "@out0b", "out0", "mida1", "@mid0a", "in1", "@mid0b", "mida0", "midb0", "midc0", "out0",
+    "midb1", "out1", "@mid0c", "mida1", "midc1", "@small0", "small", "@in0a", "in0", "out0", "midb1", "@in0b",
+    "in1", "out1", "mida0", "in0", "out0", "in1", "midc1", "mida0", "out1", "midb0", "in0", "out0", "mida0",
+    "midc0", "midb0", "mida0", "in0", "small", "midc0", "midb0", "in0", "small", "midc0", "small", "midb0",
+    "midc0", "small",
 )
-
-
-ORDER_FIRST = "out1a"
+ALTERNATE = ("mida1", "midb1", "in1")
+
+ORDER_FIRST = "mid1a"
 
 
 def gradient_kernel(n_seg, n_clip, *refs):
@@ -1234,8 +1304,8 @@
         "small": ("low", "dr", "s", "de"),
     }
     load_cls = load(cls_hbm, g_cls)
-    waits = {"out": fetch(1, *operands["out"])}
     fpad[...] = jnp.zeros_like(fpad)
+    waits = {"mid": fetch(1, *operands["mid"])}
     links.meet()
     squares[...] = jnp.zeros_like(squares)
 
@@ -1300,7 +1370,7 @@
                 for k in range(lines):
                     put(int(block), first + k, total[:, k * LANES : (k + 1) * LANES], lines)
 
-        jobs[name] = Scatter(links, folded(ref, shard_rows), pl.ds(start, rows), buffers[name], finish)
+        jobs[name] = Scatter(links, folded(ref, shard_rows), pl.ds(start, rows), buffers[name], name in ALTERNATE, finish)
 
     for name in SCATTERED:
         make(name)
@@ -1365,7 +1435,7 @@
                         while jobs[name].at < 1:
                             jobs[name].advance()
         if kind == "mid":
-            task_mid(3 * part, 3 * part + 3)
+            task_mid((0, 3, 5)[part], (3, 5, 9)[part])
         elif kind == "in":
             task_in(2 * part, 2 * part + 2)
         elif kind == "out":
@@ -1375,7 +1445,7 @@
         if block == 1 and part == {"mid": 2, "in": 1, "out": 1, "small": 0}[kind]:
             waits[kind] = fetch(0, *operands[kind])
         if block == 1 and piece == ORDER_FIRST:
-            for other in ("in", "mid", "small"):
+            for other in ("in", "out", "small"):
                 waits[other] = fetch(1, *operands[other])
 
     g_small[:, 64:80, :] = norm_rows_in[...]
@@ -1424,8 +1494,9 @@
         pltpu.VMEM((FLAT_ROWS + 14, LANES), F32),
     ]
     scratch += sum_scratch(n_seg, n_clip, (16, LANES))
-    for shape in SCATTERED.values():
-        for lead in ((depth, 4), (depth, 2), (depth,), (depth - 1,)):
+    for name, shape in SCATTERED.items():
+        ends = ((depth - 1, 2), (3,)) if name in ALTERNATE else ((depth,), (depth - 1,))
+        for lead in ((depth, 4), (depth, 2)) + ends:
             scratch.append(pltpu.VMEM(lead + shape, BF16))
     count = n_seg * 4 + depth + len(SCATTERED) * (depth + 3) + 40
     scratch += [pltpu.SemaphoreType.DMA((count,)), pltpu.SemaphoreType.DMA((count,))]
@@ -1470,44 +1541,36 @@
     else:
         weights = {}
         jobs = JOBS
+    rows = ((0, 8 - clip_local), (0, 0))
+    share = jnp.pad(1.0 / (HW * clip_counts.astype(F32))[:, None], rows)
+    share = jnp.broadcast_to(share, (8, LANES))
+    onehot = (labels[:, None] == jnp.arange(2 * LANES, dtype=jnp.int32)[None, :]).astype(F32)
+    target = jnp.pad(onehot, rows)
     kept = []
     flowing = x_low
     flows = []
     for block in range(2):
         flows.append(flowing)
-        given = {name: weights[name] for name in weight_names(block) if name not in jobs[block]}
+        names = weight_names(block) + (["cls"] if block == 1 else [])
+        given = {name: weights[name] for name in names if name not in jobs[block]}
         gathered, results = forward_block(
             block,
             flowing,
             frame_mask,
             frame_following,
             table,
+            (share, target) if block == 1 else (),
             {name: shards[name] for name in jobs[block]},
             given,
         )
         weights.update(gathered)
         if block == 0:
             table = results[9]
-        kept.append(results[:8] + results[10:])
+        kept.append(results[:8] + results[10:13])
         flowing = results[8]
-    w_cls = weights["cls"][:, :CLASSES]
-    bias_row = 64 + 4
-    b_cls = weights["small"].reshape(SMALL_SHARDS, 80, LANES)[:, bias_row, :6].reshape(-1)[:CLASSES].astype(F32)
-    partial_value = jnp.sum(flowing.reshape(clip_local, slot_local, D), axis=1)
-    pooled_sum = lax.psum(partial_value.astype(BF16), "seg").astype(F32)
-    counts_float = clip_counts.astype(F32)
-    pooled = pooled_sum / (HW * counts_float)[:, None]
-    pooled_low = pooled.astype(BF16)
-    logits = matmul(pooled_low, w_cls) + b_cls
-    clips_total = clip_local * lax.axis_size("clip")
-    onehot = (labels[:, None] == jnp.arange(CLASSES, dtype=jnp.int32)[None, :]).astype(F32)
-    d_logits = (jax.nn.softmax(logits, axis=1) - onehot) / clips_total
-    d_lin = d_logits.astype(BF16)
-    g_cls = matmul(pooled_low.T, d_lin) / seg_count
-    g_bias = jnp.sum(d_logits, axis=0) / seg_count
-    d_pooled = matmul(d_lin, w_cls.T)
-    scaled = d_pooled / (HW * counts_float)[:, None]
-    d_flow = (present[:, :, None] * scaled[:, None]).reshape(frames, D)
+    d_flow = flowing
+    g_cls, g_bias = results[13:]
+    g_bias = g_bias[0, :CLASSES]
     masks = (frame_mask, frame_mask[:, :GATE], frame_following)
     sources = [None, None]
     norm_grads = [None, None]
@@ -1534,15 +1597,14 @@
         grads = []
         for block in (0, 1):
             grads += weight_gradients(*sources[block]) + [v / devices for v in norm_grads[block]]
-        grad_mine = scatter_gradients(grads + [g_cls, g_bias])
+        grad_mine = scatter_gradients(grads + [g_cls[:, :CLASSES].astype(F32), g_bias])
         square = jnp.full((8, LANES), jnp.sum(grad_mine * grad_mine), F32)
         tail = lax.psum(jnp.concatenate([bias_rows, square]), AXES)
     else:
         vectors = [v.reshape(SMALL_SHARDS, -1) / devices for b in (0, 1) for v in norm_grads[b]]
         padded = jnp.pad(g_bias, (0, 6 * SMALL_SHARDS - CLASSES)).reshape(SMALL_SHARDS, 6)
         extra = norm_rows(vectors + [padded]).astype(BF16)
-        cls_low = jnp.pad(g_cls.astype(BF16), ((0, 0), (0, 2 * LANES - CLASSES)))
-        flat, tail = gradient_sums(sources, cls_low, extra, bias_rows)
+        flat, tail = gradient_sums(sources, g_cls, extra, bias_rows)
         grad_mine = flat.reshape(-1)[: master.shape[0]]
     norm = jnp.sqrt(tail[8, 0])
     bias_grad = tail[:8].reshape(-1)[:CLASSES]

time: 474 us -> 460 us (0.970); the launches traced: 465 us -> 457 us
    unnamed x22 -> x20, local copies, waits for them, and re-layouts: 18.6 us -> 18.6 us
where the time goes in v7:
time: 460 us; the launch traced here: 457 us
  Pallas kernels  416 us (90%)
  local copies, waits for them, and re-layouts  30.9 us (7%)
  other arithmetic  6.7 us (1%)
    pallas_call x2, Pallas kernels, forward_block(): pl.pallas_call(functools.partial(forward_kernel, n_seg, n_clip, block, jo...  174 us
    pallas_call x2, Pallas kernels, backward_block(): pl.pallas_call(functools.partial(backward_kernel, n_seg, n_clip, block),...  133 us
    pallas_call x1, Pallas kernels, gradient_sums(): pl.pallas_call(functools.partial(gradient_kernel, n_seg, n_clip), out_sha...  109 us
    unnamed x20, local copies, waits for them, and re-layouts  18.6 us

profile of v7, /device:TPU:0, one launch (start us, length us, event | category | flops | bytes accessed | tf_op | source)
XLA Modules:
  0.0 456.6 jit_solution(169891936130380467)
XLA Ops:
  0.6 1.3 convert_element_type.63
  2.0 0.1 slice_bitcast_fusion.14
  2.1 0.1 fusion.5
  2.2 0.1 constant_dynamic-update-slice_fusion.2
  2.3 0.0 copy-start.1
  2.3 0.1 fusion.3
  2.5 0.1 reshape.167
  2.5 0.0 copy-start.5
  2.5 0.1 reshape.179
  2.6 0.7 slice_bitcast_fusion.6
  3.3 0.1 fusion.4
  3.4 0.1 reshape.174
  3.5 0.1 reshape.182
  3.6 0.7 slice_bitcast_fusion
  4.3 0.0 copy-done.1
  4.3 0.7 reshape.178.refs_10_
  5.0 0.0 copy-done.5
  5.0 0.1 compare_convert_fusion
  5.0 0.1 reshape.194
  5.1 0.7 broadcast_in_dim.20.refs_1_.refs_17_
  5.8 0.1 reshape.195
  5.9 0.7 broadcast_in_dim.21.refs_2_.refs_19_
  6.6 6.7 %copy.25 = bf16[4,8,49,2048]{3,1,0,2:T(8,128)(2,1)} copy(bf16[4,8,49,2048]{3,1,2,0:T(8,128)(2,1)} %param.6) | data formatting | bytes 12845056 | tf_op args[0]
  13.3 0.6 broadcast_in_dim.44.refs_3_
  14.0 0.0 copy-start.6
  14.0 111.2 %forward_block.2 = (bf16[1024,512]{1,0:T(8,128)(2,1)}, bf16[2560,128]{1,0:T(8,128)(2,1)}, bf16[1024,512]{1,0:T(8,128)(2,1)}, bf16[1536,512]{1,0:T(8,128)(2,1)}, ...) custom-call(bf16[49,32,2048]{2,1,0:T(8,128)(2,1)} %bitcast.88, ...), custom_call_target="tpu_custom_call" | custom-call | tf_op jit(solution)/shard_map/forward_block/pallas_call | solution.py:806
  125.1 0.7 reshape.186.refs_6_
  125.8 0.2 reshape.187
  126.0 0.6 pad.80.refs_7_
  126.6 0.0 copy-done.6
  126.6 0.1 iota_compare_fusion
  126.7 0.6 pad_convert_fusion.refs_5_
  127.3 0.7 broadcast_in_dim.51.refs_4_
  128.0 63.3 %forward_block.3 = (bf16[512,2048]{1,0:T(8,128)(2,1)}, bf16[2048,256]{1,0:T(8,128)(2,1)}, f32[49,32,512]{2,1,0:T(8,128)}, bf16[49,32,512]{2,1,0:T(8,128)(2,1)}, ...) custom-call(bf16[49,32,2048]{2,1,0:T(8,128)(2,1)} %get-tuple-element, ...), custom_call_target="tpu_custom_call" | custom-call | tf_op jit(solution)/shard_map/forward_block/pallas_call | solution.py:806
  191.3 0.7 slice.134.refs_18_
  191.9 66.5 %backward_block.2 = (bf16[49,32,2048]{2,1,0:T(8,128)(2,1)}, bf16[7,7,32,512]{3,2,1,0:T(8,128)(2,1)}, bf16[49,32,512]{2,1,0:T(8,128)(2,1)}, bf16[49,32,128]{2,1,0...) custom-call(bf16[49,32,2048]{2,1,0:T(8,128)(2,1)} %get-tuple-element.72.refs_0_, ...), custom_call_target="tpu_custom_call" | custom-call | tf_op jit(solution)/shard_map/backward_block/pallas_call | solution.py:1121
  258.4 66.3 %backward_block.3 = (bf16[49,32,2048]{2,1,0:T(8,128)(2,1)}, bf16[7,7,32,512]{3,2,1,0:T(8,128)(2,1)}, bf16[49,32,512]{2,1,0:T(8,128)(2,1)}, bf16[49,32,128]{2,1,0...) custom-call(bf16[49,32,2048]{2,1,0:T(8,128)(2,1)} %get-tuple-element.63.refs_0_, ...), custom_call_target="tpu_custom_call" | custom-call | tf_op jit(solution)/shard_map/backward_block/pallas_call | solution.py:1121
  324.7 0.0 copy-start.3
  324.8 0.0 copy-start.2
  324.8 11.8 %copy.23 = f32[4,8,49,2048]{3,1,2,0:T(8,128)} copy(f32[4,8,49,2048]{3,1,0,2:T(8,128)} %bitcast.91) | data formatting | bytes 25690112
  336.5 0.0 copy-done.3
  336.5 0.1 div.48
  336.7 0.1 div.50
  336.8 0.0 copy-done.2
  336.8 0.1 div.52
  336.9 0.1 div.54
  337.0 0.7 slice.139
  337.8 0.1 reshape.188
  337.9 0.1 stack.53
  338.0 0.7 pad.87.refs_21_
  338.7 0.6 pad_bitcast_fusion.5.refs_22_
  339.3 0.0 copy-start
  339.3 108.9 %gradient_sums.1 = (f32[2336,128]{1,0:T(8,128)}, f32[16,128]{1,0:T(8,128)}) custom-call(bf16[49,32,2048]{2,1,0:T(8,128)(2,1)} %bitcast.90, bf16[49,32,512]{2,1,0:T(8,128)(2,1)} %get-tuple-element.94.refs_1_, bf16[7,7,32,512]{3,2,1,0:T(8,128)(2,1)} %get-tuple-element.95.refs_2_, bf16[7,7,32,512]{3,2,1,0:T(8,128)(2,1)} %get-tuple-element.96.refs_3_, ...), custom_call_target="tpu_custom_call" | custom-call | tf_op jit(solution)/shard_map/gradient_sums/pallas_call | solution.py:1503
  448.2 1.2 slice.141
  450.1 0.0 copy-done
  450.2 0.0 copy-start.4
  450.2 4.6 %fusion.1 = (bf16[298246]{0:T(1024)(128)(2,1)}, f32[298246]{0:T(1024)}, f32[298246]{0:T(1024)}, f32[298246]{0:T(1024)}) fusion(f32[298246]{0:T(1024)S(1)} %copy-done, f32[]{:T(128)} %bitcast.42, f32[299008]{0:T(1024)} %bitcast.92, f32[298246]{0:T(1024)} %param.10, f32[298246]{0:T(1024)} %param.11), kind=kLoop, calls=%fused_computation.52 | loop fusion | flops 5070182 | bytes 8947384 | tf_op jit(solution)/shard_map/convert_element_type | solution.py:1625
  454.8 0.0 copy-done.4
  454.8 0.6 slice.143
  (30 shorter events, 0.3 us)
Async XLA Ops:
  2.3 2.0 copy-start.1
  2.5 2.5 copy-start.5
  14.0 112.7 %copy-start.6 = (s32[4]{0:T(128)S(1)}, s32[4]{0:T(128)}, u32[]{:S(2)}) copy-start(s32[4]{0:T(128)} %param.8) | copy-start | bytes 52
  324.7 11.8 %copy-start.3 = (f32[48,128]{1,0:T(8,128)S(1)}, f32[48,128]{1,0:T(8,128)}, u32[]{:S(2)}) copy-start(f32[48,128]{1,0:T(8,128)} %get-tuple-element.113) | copy-start | bytes 73732
  324.8 12.0 %copy-start.2 = (f32[48,128]{1,0:T(8,128)S(1)}, f32[48,128]{1,0:T(8,128)}, u32[]{:S(2)}) copy-start(f32[48,128]{1,0:T(8,128)} %get-tuple-element.114) | copy-start | bytes 73732
  339.3 110.8 %copy-start = (f32[298246]{0:T(1024)S(1)}, f32[298246]{0:T(1024)}, u32[]{:S(2)}) copy-start(f32[298246]{0:T(1024)} %param.9) | copy-start | bytes 3578956
  450.2 4.6 %copy-start.4 = (f32[16,128]{1,0:T(8,128)S(1)}, f32[16,128]{1,0:T(8,128)}, u32[]{:S(2)}) copy-start(f32[16,128]{1,0:T(8,128)} %get-tuple-element.117) | copy-start | bytes 24580
